TPU v7x, 128 devices: a whole 4x4x4 slice. The times are simulated.
128 devices in a mesh: outer: 8 (over x, core), inner: 16 (over z, y).
Axes of the slice: x: 4, y: 4, z: 4, core: 2. Of those that a mesh axis runs over, the one named last changes fastest.
Arguments:
- grad_out: bfloat16 [16384, 4096], P(('outer', 'inner')), may hold values from -6 to 6
- route_weights: bfloat16 [16384, 8], P(('outer', 'inner')), may hold values from 0.049804688 to 1
- routes: int32 [16384, 8], P(('outer', 'inner')), may hold values from 0 to 15, all different within a row; in each aligned block of 128 rows (0 to 127, 128 to 255, ...) at most 96 rows name the same one
- saved_gate_up: bfloat16 [8, 16, 16, 96, 3072], P(None, 'outer', 'inner'), may hold values from -6 to 6
- down_weight: bfloat16 [16, 1536, 4096], P('outer', None, 'inner'), may hold values from -0.09375 to 0.09375
Outputs:
- grad_gate_up: bfloat16 [8, 16, 16, 96, 3072], P(None, 'outer', 'inner')
- grad_weights: float32 [16384, 8], P(('outer', 'inner'))
Inputs may be any that keep to these rules, and one draw needn't show every extreme that they name: `routes`: each row names 8 different experts. In each aligned block of 128 rows (the rows of one device) no expert is named more than 96 times, a bound that some block reaches.
All inputs are finite; a program needn't handle non-finite values.
Results may differ from a plain program's by a relative error of at most 0.0029.
Values may be sent and summed in bfloat16 or wider, within the bound.
No kernel may reach another device: no remote copies, remote signals or barrier semaphores. Data moves between devices by JAX's collectives and lax.ppermute only.
A program may use at most 192 MiB of HBM per device.

v0:
```python
import jax
import jax.numpy as jnp
from jax import lax
from jax.sharding import PartitionSpec as P


def shards(grad_out, route_weights, routes, saved_gate_up, down_weight):
    tok_rows, top_count = routes.shape
    n_outer = lax.axis_size("outer")
    exp_local = down_weight.shape[0]
    hid_units = down_weight.shape[1]
    experts = n_outer * exp_local
    capacity = saved_gate_up.shape[3]
    width = grad_out.shape[1]
    flat_routes = routes.reshape(-1)
    onehot = (flat_routes[:, None] == jnp.arange(experts, dtype=jnp.int32)[None, :]).astype(
        jnp.int32
    )
    before = jnp.cumsum(onehot, axis=0) - onehot
    position = jnp.sum(before * onehot, axis=1)
    slot = flat_routes * capacity + position
    token_of = jnp.arange(tok_rows * top_count, dtype=jnp.int32) // top_count
    send_rows = (
        jnp.zeros((experts * capacity, width), jnp.bfloat16).at[slot].set(grad_out[token_of])
    )
    send_weights = (
        jnp.zeros((experts * capacity,), jnp.bfloat16).at[slot].set(route_weights.reshape(-1))
    )
    send_rows = send_rows.reshape(n_outer, exp_local, capacity, width)
    send_weights = send_weights.reshape(n_outer, exp_local, capacity)
    recv_rows, recv_weights = (
        lax.all_to_all(send_rows, "outer", split_axis=0, concat_axis=0, tiled=True),
        lax.all_to_all(send_weights, "outer", split_axis=0, concat_axis=0, tiled=True),
    )
    gathered = lax.all_gather(down_weight, "inner", axis=2, tiled=True)
    carried = jnp.einsum("sjcd,jhd->sjch", recv_rows, gathered, preferred_element_type=jnp.float32)
    saved = saved_gate_up[:, :, 0].astype(jnp.float32)
    gate = saved[..., :hid_units]
    upper = saved[..., hid_units:]
    sigma = jax.nn.sigmoid(gate)
    active = gate * sigma
    hidden = lax.optimization_barrier((active * upper).astype(jnp.bfloat16)).astype(jnp.float32)
    slot_grad = jnp.sum(carried * hidden, axis=-1)
    scaled = recv_weights.astype(jnp.float32)[..., None] * carried
    grad_gate = scaled * upper * sigma * (1.0 + gate * (1.0 - sigma))
    grad_upper = scaled * active
    grad_gate_up = jnp.concatenate([grad_gate, grad_upper], axis=-1).astype(jnp.bfloat16)[
        :, :, None
    ]
    returned = lax.all_to_all(slot_grad, "outer", split_axis=0, concat_axis=0, tiled=True)
    grad_weights = returned.reshape(-1)[slot].reshape(tok_rows, top_count)
    return (grad_gate_up, grad_weights)


def solution(mesh):
    in_specs = (
        P(("outer", "inner"), None),
        P(("outer", "inner"), None),
        P(("outer", "inner"), None),
        P(None, "outer", "inner", None, None),
        P("outer", None, "inner"),
    )
    out_specs = (P(None, "outer", "inner", None, None), P(("outer", "inner"), None))
    return jax.shard_map(shards, mesh=mesh, in_specs=in_specs, out_specs=out_specs, check_vma=False)
```

profile of v0, /device:TPU:1, one launch (start us, length us, event | category | flops | bytes accessed | tf_op | source)
XLA Modules:
  0.0 280.2 jit_solution(15370077545904561379)
XLA Ops:
  7.2 0.7 all-gather.2.cloned.1.call-update
  7.9 0.8 copy.70
  8.9 4.5 %reduce-window.6 = s32[16,8,128]{2,1,0:T(8,128)S(1)} reduce-window(s32[16,8,128]{2,1,0:T(8,128)S(1)} %fusion.12, s32[]{:T(128)} %constant.28.clone.1), window={size=1x1x128 pad=0_0x0_0x127_0}, to_apply=%region_0.0 | reduce-window | flops 2080768 | bytes 131076 | tf_op jit(solution)/shard_map/reduce-window
  13.5 0.1 copy.72
  13.7 0.7 broadcast_multiply_fusion
  14.6 0.8 copy.74
  15.4 0.1 reshape.169
  15.7 7.6 %scatter_custom_fusion = bf16[1536]{0:T(1024)(128)(2,1)S(1)} fusion(s32[1024]{0:T(1024)S(1)} %bitcast.51, bf16[1024]{0:T(1024)(128)(2,1)S(1)} %reshape.169, bf16[]{:T(256)} %constant.26.clone.1), kind=kCustom, calls=%fused_computation.39 | custom fusion | bytes 3074 | tf_op jit(solution)/shard_map/scatter | solution.py:27
  23.3 0.7 reshape.144
  24.0 5.8 %all-to-all-start = ((bf16[8,2,96]{2,1,0:T(2,128)(2,1)}), bf16[8,2,96]{2,1,0:T(2,128)(2,1)S(1)}, u32[]{:S(2)}, u32[]{:S(2)}) async-start(bf16[8,2,96]{2,1,0:T(2,128)(2,1)} %reshape.144), calls=%async_computation | async-start | bytes 8192 | tf_op jit(solution)/shard_map/all_to_all | solution.py:33
  29.8 7.6 %gather_fusion = bf16[1024,4096]{1,0:T(8,128)(2,1)} fusion(bf16[128,4096]{1,0:T(8,128)(2,1)S(1)} %copy-done, s32[1024]{0:T(1024)S(1)} %broadcast_clamp_fusion.1), kind=kCustom, calls=%fused_computation | custom fusion | bytes 16781312 | tf_op jit(solution)/shard_map/gather | solution.py:24
  37.4 20.0 %scatter_custom_fusion.1 = bf16[1536,4096]{1,0:T(8,128)(2,1)} fusion(s32[1024]{0:T(1024)S(1)} %bitcast.52, bf16[1024,4096]{1,0:T(8,128)(2,1)} %gather_fusion, bf16[]{:T(256)} %constant.26.clone.1), kind=kCustom, calls=%fused_computation.17 | custom fusion | bytes 12583424 | tf_op jit(solution)/shard_map/scatter | solution.py:24
  57.4 5.3 %all-to-all-start.1 = ((bf16[8,2,96,4096]{3,2,1,0:T(8,128)(2,1)}), bf16[8,2,96,4096]{3,2,1,0:T(8,128)(2,1)}, u32[]{:S(2)}, u32[]{:S(2)}) async-start(bf16[8,2,96,4096]{3,2,1,0:T(8,128)(2,1)} %bitcast.47), calls=%async_computation.1 | async-start | bytes 25165824 | tf_op jit(solution)/shard_map/all_to_all | solution.py:32
  62.7 13.0 %bitcast_convert_fusion = f32[8,2,96,3072]{3,2,0,1:T(8,128)} fusion(bf16[8,2,1,96,3072]{4,3,2,1,0:T(8,128)(2,1)} %param.8), kind=kLoop, calls=%fused_computation.8 | loop fusion | flops 4718592 | bytes 28311552 | tf_op jit(solution)/shard_map/convert_element_type | solution.py:37
  75.8 125.6 %all-to-all-done.1 = bf16[8,2,96,4096]{3,2,1,0:T(8,128)(2,1)} async-done(((bf16[8,2,96,4096]{3,2,1,0:T(8,128)(2,1)}), bf16[8,2,96,4096]{3,2,1,0:T(8,128)(2,1)}, u32[]{:S(2)}, u32[]{:S(2)}) %all-to-all-start.1) | async-done | bytes 12582944 | tf_op jit(solution)/shard_map/all_to_all | solution.py:32
  201.4 26.7 %fusion = f32[2,8,96,1536]{3,2,1,0:T(8,128)} fusion(bf16[2,1536,4096]{2,1,0:T(8,128)(2,1)} %all-gather.2.cloned.1.call-done, bf16[8,2,96,4096]{3,2,1,0:T(8,128)(2,1)} %all-to-all-done.1), kind=kOutput, calls=%fused_computation.4 | convolution fusion | flops 19327352832 | bytes 47185920 | tf_op jit(solution)/shard_map/sjcd,jhd->sjch/dot_general | solution.py:36
  228.1 16.2 %fusion.8 = (bf16[8,2,1,96,1536]{4,3,0,1,2:T(8,128)(2,1)}, bf16[8,2,1,96,1536]{4,3,0,1,2:T(8,128)(2,1)}, bf16[8,2,96,1536]{3,2,0,1:T(8,128)(2,1)S(1)}) fusion(f32[8,2,96,3072]{3,2,0,1:T(8,128)} %bitcast_convert_fusion, f32[2,8,96,1536]{3,2,1,0:T(8,128)} %fusion, f32[8,2,96]{2,0,1:T(8,128)S(1)} %copy_convert_fusion), kind=kLoop, calls=%fused_computation.20 | loop fusion | flops 37748736 | bytes 42473472 | tf_op jit(solution)/shard_map/concatenate | solution.py:47
  244.3 1.0 fusion.3
  245.3 0.6 copy.78
  245.9 4.1 %all-to-all-start.2 = ((f32[8,2,96]{2,1,0:T(2,128)}), f32[8,2,96]{2,1,0:T(2,128)S(1)}, u32[]{:S(2)}, u32[]{:S(2)}) async-start(f32[8,2,96]{2,1,0:T(2,128)} %copy.78), calls=%async_computation.2 | async-start | bytes 16384 | tf_op jit(solution)/shard_map/all_to_all | solution.py:50
  250.0 7.8 %pad_maximum_fusion = bf16[8,2,1,96,3072]{4,3,0,1,2:T(8,128)(2,1)} fusion(bf16[8,2,1,96,1536]{4,3,0,1,2:T(8,128)(2,1)} %get-tuple-element.17, bf16[8,2,1,96,1536]{4,3,0,1,2:T(8,128)(2,1)} %get-tuple-element.16), kind=kLoop, calls=%fused_computation.7 | loop fusion | flops 18874368 | bytes 18874368 | tf_op jit(solution)/shard_map/concatenate | solution.py:47
  257.8 8.6 %copy.79 = bf16[8,2,1,96,3072]{4,3,2,1,0:T(8,128)(2,1)} copy(bf16[8,2,1,96,3072]{4,3,0,1,2:T(8,128)(2,1)} %pad_maximum_fusion) | data formatting | bytes 18874368
  266.5 6.1 %gather_fusion.1 = f32[1024]{0:T(1024)S(1)} fusion(f32[1536]{0:T(1024)S(1)} %reshape.146, s32[1024]{0:T(1024)S(1)} %broadcast_clamp_fusion), kind=kCustom, calls=%fused_computation.1 | custom fusion | bytes 12288 | tf_op jit(solution)/shard_map/gather | solution.py:51
  272.7 0.7 copy.80
  (28 shorter events, 0.9 us)
Async XLA Ops:
  7.2 22.6 %copy-start = (bf16[128,4096]{1,0:T(8,128)(2,1)S(1)}, bf16[128,4096]{1,0:T(8,128)(2,1)}, u32[]{:S(2)}) copy-start(bf16[128,4096]{1,0:T(8,128)(2,1)} %param.5) | copy-start | bytes 3145732
  7.2 194.2 %all-gather.2.cloned.1.call-start = ((), (), s32[]{:S(2)}) async-start(), calls=%async_computation.3 | async-start | bytes 26738688 | tf_op jit(solution)/shard_map/all_gather | solution.py:35
  24.0 33.4 %all-to-all-start = ((bf16[8,2,96]{2,1,0:T(2,128)(2,1)}), bf16[8,2,96]{2,1,0:T(2,128)(2,1)S(1)}, u32[]{:S(2)}, u32[]{:S(2)}) async-start(bf16[8,2,96]{2,1,0:T(2,128)(2,1)} %reshape.144), calls=%async_computation | async-start | bytes 8192 | tf_op jit(solution)/shard_map/all_to_all | solution.py:33
  57.4 144.0 %all-to-all-start.1 = ((bf16[8,2,96,4096]{3,2,1,0:T(8,128)(2,1)}), bf16[8,2,96,4096]{3,2,1,0:T(8,128)(2,1)}, u32[]{:S(2)}, u32[]{:S(2)}) async-start(bf16[8,2,96,4096]{3,2,1,0:T(8,128)(2,1)} %bitcast.47), calls=%async_computation.1 | async-start | bytes 25165824 | tf_op jit(solution)/shard_map/all_to_all | solution.py:32
  228.1 16.2 %copy-start.2 = (f32[2,8,96,1536]{3,2,1,0:T(8,128)S(1)}, f32[2,8,96,1536]{3,2,1,0:T(8,128)}, u32[]{:S(2)}) copy-start(f32[2,8,96,1536]{3,2,1,0:T(8,128)} %fusion) | copy-start | bytes 28311556
  245.9 20.5 %all-to-all-start.2 = ((f32[8,2,96]{2,1,0:T(2,128)}), f32[8,2,96]{2,1,0:T(2,128)S(1)}, u32[]{:S(2)}, u32[]{:S(2)}) async-start(f32[8,2,96]{2,1,0:T(2,128)} %copy.78), calls=%async_computation.2 | async-start | bytes 16384 | tf_op jit(solution)/shard_map/all_to_all | solution.py:50
  250.0 23.4 %copy-start.1 = (bf16[128,4096]{1,0:T(8,128)(2,1)S(1)}, bf16[128,4096]{1,0:T(8,128)(2,1)}, u32[]{:S(2)}) copy-start(bf16[128,4096]{1,0:T(8,128)(2,1)} %param.5) | copy-start | bytes 3145732
Sparse Core Ops, SparseCore 0:
  10.1 166.2 all-gather.1
where the time goes:
time: 281 us; the launch traced here: 280 us
  waiting for transfers between devices  126 us (45%)
  local copies, waits for them, and re-layouts  54.4 us (19%)
  other arithmetic  43.4 us (15%)
  matrix products  26.7 us (10%)
  starting transfers between devices  15.3 us (5%)
  between operations  14.1 us (5%)
    all_to_all x1, waiting for transfers between devices, shards(): lax.all_to_all(send_rows, 'outer', split_axis=0, concat_axis=0, tiled=True)  126 us
    dot_general x1, matrix products, shards(): jnp.einsum('sjcd,jhd->sjch', recv_rows, gathered, preferred_element_type=...  26.7 us
    concatenate x2, other arithmetic, shards(): jnp.concatenate([grad_gate, grad_upper], axis=-1).astype(jnp.bfloat16)  24 us
    scatter x1, local copies, waits for them, and re-layouts, shards(): jnp.zeros((experts * capacity, width), jnp.bfloat16).at[slot]  20 us
    convert_element_type x1, other arithmetic, shards(): saved = saved_gate_up[:, :, 0].astype(jnp.float32)  13 us
    unnamed x10, local copies, waits for them, and re-layouts  10.9 us
    gather x1, local copies, waits for them, and re-layouts, shards(): grad_out[token_of]  7.61 us
    scatter x1, local copies, waits for them, and re-layouts, shards(): jnp.zeros((experts * capacity,), jnp.bfloat16).at[slot]  7.59 us
  transfers between devices with their start and end apart: 4, of which 1 were waited for; matrix products, arithmetic and copies ran while one was open for 26% of the time, Pallas kernels for 0%

commit v1 on v0

v1 whole, which is shorter than its diff:
```python
import functools

import jax
import jax.numpy as jnp
from jax import lax
from jax.experimental import pallas as pl
from jax.experimental.pallas import tpu as pltpu
from jax.sharding import PartitionSpec as P

BF = jnp.bfloat16
F32 = jnp.float32
SHARD = 256
TILE = 512
WAVE_TILES = 2
VMEM = 56 * 1024 * 1024


def ring(axis, step):
    pairs = []
    for z in range(4):
        for y in range(4):
            if axis == "y":
                pairs.append((z * 4 + y, z * 4 + (y + step) % 4))
            else:
                pairs.append((z * 4 + y, ((z + step) % 4) * 4 + y))
    return pairs


def along(x, axis, step):
    return lax.ppermute(x, "inner", ring(axis, step))


def along_x(x, step):
    pairs = [(a * 2 + c, ((a + step) % 4) * 2 + c) for a in range(4) for c in range(2)]
    return lax.ppermute(x, "outer", pairs)


def together(*groups):
    return [list(g) for g in lax.optimization_barrier(tuple(tuple(g) for g in groups))]


def params(steps):
    return pltpu.CompilerParams(
        dimension_semantics=("arbitrary",) * steps, vmem_limit_bytes=VMEM
    )


def plan_kernel(routes_ref, weights_ref, out_ref):
    routes = routes_ref[...]
    weights = weights_ref[...].astype(F32)
    tokens = routes.shape[1]
    experts = out_ref.shape[0] * 2
    expert = lax.broadcasted_iota(jnp.int32, (experts, tokens), 0)
    named = jnp.zeros((experts, tokens), F32)
    weight = jnp.zeros((experts, tokens), F32)
    for k in range(routes.shape[0]):
        same = routes[k : k + 1, :] == expert
        named = jnp.where(same, 1.0, named)
        weight = jnp.where(same, weights[k : k + 1, :], weight)
    earlier = lax.broadcasted_iota(jnp.int32, (tokens, tokens), 0)
    later = lax.broadcasted_iota(jnp.int32, (tokens, tokens), 1)
    before = jnp.where(earlier < later, 1.0, 0.0).astype(BF)
    position = jnp.dot(named.astype(BF), before, preferred_element_type=F32)
    position = jnp.where(named > 0.0, position, -1.0)
    for e in range(experts):
        out_ref[e // 2, e % 2 : e % 2 + 1, :] = position[e : e + 1, :]
        out_ref[e // 2, 2 + e % 2 : 3 + e % 2, :] = weight[e : e + 1, :]


def plan(routes, route_weights, n_outer):
    return pl.pallas_call(
        plan_kernel,
        out_shape=jax.ShapeDtypeStruct((n_outer, 4, routes.shape[1]), F32),
        name="plan",
    )(routes, route_weights)


def pick_kernel(routes_ref, grads_ref, out_ref):
    routes = routes_ref[...]
    total = jnp.zeros(routes.shape, F32)
    for o in range(grads_ref.shape[0]):
        for j in range(2):
            total = jnp.where(routes == 2 * o + j, grads_ref[o, j : j + 1, :], total)
    out_ref[...] = total


def pick(routes, grads):
    return pl.pallas_call(
        pick_kernel, out_shape=jax.ShapeDtypeStruct(routes.shape, F32), name="pick"
    )(routes, grads)


def fill_kernel(source_ref, tokens_ref, plan_ref, *rest):
    rows_ref, weight_ref = rest[-2:]
    tokens = plan_ref.shape[-1]
    cap = rows_ref.shape[2]
    slot = lax.broadcasted_iota(jnp.int32, (cap, tokens), 0).astype(F32)
    width = tokens_ref.shape[-1]
    step = 1024
    picks = []
    for j in range(2):
        owned = slot == plan_ref[0, j : j + 1, :]
        picks.append(jnp.where(owned, 1.0, 0.0))
        weight = jnp.sum(
            jnp.where(owned, plan_ref[0, 2 + j : 3 + j, :], 0.0), axis=1, keepdims=True
        )
        weight_ref[j, 0] = jnp.broadcast_to(weight, weight_ref.shape[2:])
    picks = jnp.concatenate(picks, axis=0).astype(BF)
    for c in range(0, width, step):
        rows = jnp.dot(picks, tokens_ref[0, :, c : c + step], preferred_element_type=F32)
        rows_ref[0, 0, :, c : c + step] = rows[:cap].astype(BF)
        rows_ref[1, 0, :, c : c + step] = rows[cap:].astype(BF)


def fill(sources, tokens, plans, cap, earlier=None):
    count, rows, width = tokens.shape
    n_outer = plans.shape[0]
    extra = [] if earlier is None else list(earlier)
    return pl.pallas_call(
        fill_kernel,
        grid_spec=pltpu.PrefetchScalarGridSpec(
            num_scalar_prefetch=1,
            grid=(count,),
            in_specs=[
                pl.BlockSpec((1, rows, width), lambda q, src: (q, 0, 0)),
                pl.BlockSpec((1, 4, rows), lambda q, src: (src[q], 0, 0)),
            ]
            + [pl.BlockSpec(memory_space=pl.ANY)] * len(extra),
            out_specs=[
                pl.BlockSpec((2, 1, cap, width), lambda q, src: (0, src[q], 0, 0)),
                pl.BlockSpec((2, 1, cap, 128), lambda q, src: (0, src[q], 0, 0)),
            ],
        ),
        out_shape=[
            jax.ShapeDtypeStruct((2, n_outer, cap, width), BF),
            jax.ShapeDtypeStruct((2, n_outer, cap, 128), F32),
        ],
        input_output_aliases={3: 0, 4: 1} if extra else {},
        compiler_params=params(1),
        cost_estimate=pl.CostEstimate(
            flops=2 * count * 2 * cap * rows * width,
            bytes_accessed=count * (rows + 2 * cap) * width * 2,
            transcendentals=0,
        ),
        name="fill",
    )(sources, tokens, plans, *extra)


def product(rows, weight):
    return lax.dot_general(
        rows, weight, (((1,), (1,)), ((), ())), preferred_element_type=F32
    )


def backward(total_ref, gate_ref, up_ref, weight_ref, out_ref, sums_ref):
    sources, cap = gate_ref.shape[0], gate_ref.shape[3]
    for s in range(sources):
        at = slice(s * cap, (s + 1) * cap)
        for c in range(0, TILE, 128):
            cols = slice(c, c + 128)
            carried = total_ref[at, cols]
            gate = gate_ref[s, 0, 0, :, cols].astype(F32)
            upper = up_ref[s, 0, 0, :, cols].astype(F32)
            sigma = 0.5 * jnp.tanh(0.5 * gate) + 0.5
            active = gate * sigma
            hidden = (active * upper).astype(BF).astype(F32)
            sums_ref[at, :] += carried * hidden
            scaled = weight_ref[0, at, :] * carried
            out_ref[0, s, :, cols] = (
                scaled * upper * (sigma + active * (1.0 - sigma))
            ).astype(BF)
            out_ref[1, s, :, cols] = (scaled * active).astype(BF)


def out_copies(stage_ref, out_ref, sems, slot, j, tile):
    hid = out_ref.shape[-1] // 2
    return [
        pltpu.make_async_copy(
            stage_ref.at[slot, half],
            out_ref.at[:, j, 0, :, pl.ds(pl.multiple_of(half * hid + tile * TILE, TILE), TILE)],
            sems.at[slot, half],
        )
        for half in range(2)
    ]


def staged(stage_ref, out_ref, sems, j, tile, tiles, first, compute):
    step = j * tiles + tile
    slot = step % 2

    @pl.when(step >= 2)
    def _():
        old = step - 2
        for copy in out_copies(
            stage_ref, out_ref, sems, slot, old // tiles, first + old % tiles
        ):
            copy.wait()

    compute(stage_ref.at[slot])
    for copy in out_copies(stage_ref, out_ref, sems, slot, j, first + tile):
        copy.start()

    @pl.when(step == 2 * tiles - 1)
    def _():
        old = step - 1
        for copy in out_copies(
            stage_ref, out_ref, sems, 1 - slot, old // tiles, first + old % tiles
        ):
            copy.wait()
        for copy in out_copies(stage_ref, out_ref, sems, slot, j, first + tile):
            copy.wait()


QUARTER = 1024


def row_copies(rows_ref, held_ref, sems, j):
    return [
        (
            rows_ref.at[j, :, pl.ds(k * QUARTER, QUARTER)],
            held_ref.at[j, :, pl.ds(k * QUARTER, QUARTER)],
            sems.at[j, k],
        )
        for k in range(held_ref.shape[2] // QUARTER)
    ]


def start_rows(rows_ref, held_ref, sems):
    for e in range(2):
        for copy in row_copies(rows_ref, held_ref, sems, e):
            pltpu.make_async_copy(*copy).start()


def whole_kernel(tiles, rows_ref, w_ref, gate_ref, up_ref, weight_ref, *rest):
    out_ref, sums_ref, total_ref, stage_ref, out_sems, held_ref, sems = rest
    j, tile = pl.program_id(0), pl.program_id(1)

    @pl.when((j == 0) & (tile == 0))
    def _():
        start_rows(rows_ref, held_ref, sems)

    @pl.when(tile == 0)
    def _():
        sums_ref[...] = jnp.zeros_like(sums_ref)

    for k in range(4):

        @pl.when(tile == 0)
        def _(k=k):
            pltpu.make_async_copy(*row_copies(rows_ref, held_ref, sems, j)[k]).wait()

        weight = jnp.concatenate([w_ref[4 * k + i, 0] for i in range(4)], axis=1)
        part = product(held_ref[j, :, k * QUARTER : (k + 1) * QUARTER], weight)
        total_ref[...] = part if k == 0 else total_ref[...] + part

    def compute(slot_ref):
        backward(total_ref, gate_ref, up_ref, weight_ref, slot_ref, sums_ref.at[0])

    staged(stage_ref, out_ref, out_sems, j, tile, tiles, 0, compute)


def whole(rows, w, saved, weights):
    _, slots, width = rows.shape
    sources, _, _, cap, both = saved.shape
    tiles = w.shape[2] // TILE
    shift = both // 2 // TILE
    tile = (sources, 1, 1, cap, TILE)
    return pl.pallas_call(
        functools.partial(whole_kernel, tiles),
        grid=(2, tiles),
        in_specs=[
            pl.BlockSpec(memory_space=pl.ANY),
            pl.BlockSpec((16, 1, TILE, SHARD), lambda j, h: (0, j, h, 0)),
            pl.BlockSpec(tile, lambda j, h: (0, j, 0, 0, h)),
            pl.BlockSpec(tile, lambda j, h: (0, j, 0, 0, h + shift)),
            pl.BlockSpec((1, slots, 128), lambda j, h: (j, 0, 0)),
        ],
        out_specs=[
            pl.BlockSpec(memory_space=pl.ANY),
            pl.BlockSpec((1, slots, 128), lambda j, h: (j, 0, 0)),
        ],
        out_shape=[
            jax.ShapeDtypeStruct(saved.shape, BF),
            jax.ShapeDtypeStruct((2, slots, 128), F32),
        ],
        scratch_shapes=[
            pltpu.VMEM((slots, TILE), F32),
            pltpu.VMEM((2, 2, sources, cap, TILE), BF),
            pltpu.SemaphoreType.DMA((2, 2)),
            pltpu.VMEM(rows.shape, BF),
            pltpu.SemaphoreType.DMA((2, width // QUARTER)),
        ],
        compiler_params=params(2),
        cost_estimate=pl.CostEstimate(
            flops=4 * slots * width * tiles * TILE,
            bytes_accessed=4 * slots * width + 4 * tiles * TILE * (width + 4 * slots),
            transcendentals=2 * slots * tiles * TILE,
        ),
        name="whole",
    )(rows, w, saved, saved, weights)


def columns(ref, j, order_ref, first):
    return jnp.concatenate(
        [
            ref[j, :, pl.ds(pl.multiple_of(order_ref[first + i] * SHARD, SHARD), SHARD)]
            for i in range(4)
        ],
        axis=1,
    )


def most_kernel(order_ref, rows_ref, *rest):
    blocks, (total_ref, held_ref, sems) = rest[:6], rest[6:]
    j, tile = pl.program_id(0), pl.program_id(1)

    @pl.when((j == 0) & (tile == 0))
    def _():
        start_rows(rows_ref, held_ref, sems)

    @pl.when(tile == 0)
    def _():
        for copy in row_copies(rows_ref, held_ref, sems, j):
            pltpu.make_async_copy(*copy).wait()

    for e in range(2):

        @pl.when(j == e)
        def _(e=e):
            for n, w_ref in enumerate(blocks[3 * e : 3 * e + 3]):
                weight = jnp.concatenate([w_ref[i] for i in range(4)], axis=1)
                part = product(columns(held_ref, e, order_ref, 16 * e + 4 * n), weight)
                total_ref[0] = part if n == 0 else total_ref[0] + part


def a_map(tiles, j, h, o):
    return 0, jnp.where(j == 0, h, tiles - 1), 0


def b_map(j, h, o):
    return 0, jnp.where(j == 0, 0, h), 0


def most(order, rows, blocks):
    _, slots, width = rows.shape
    tiles = blocks[0].shape[1] // TILE
    return pl.pallas_call(
        most_kernel,
        grid_spec=pltpu.PrefetchScalarGridSpec(
            num_scalar_prefetch=1,
            grid=(2, tiles),
            in_specs=[pl.BlockSpec(memory_space=pl.ANY)]
            + [pl.BlockSpec((4, TILE, SHARD), functools.partial(a_map, tiles))] * 3
            + [pl.BlockSpec((4, TILE, SHARD), b_map)] * 3,
            out_specs=pl.BlockSpec((1, slots, TILE), lambda j, h, o: (j, 0, h)),
            scratch_shapes=[
                pltpu.VMEM(rows.shape, BF),
                pltpu.SemaphoreType.DMA((2, width // QUARTER)),
            ],
        ),
        out_shape=jax.ShapeDtypeStruct((2, slots, tiles * TILE), F32),
        compiler_params=params(2),
        cost_estimate=pl.CostEstimate(
            flops=4 * slots * width * tiles * TILE * 3 // 4,
            bytes_accessed=4 * slots * width + 2 * tiles * TILE * (2 * width + 4 * slots),
            transcendentals=0,
        ),
        name="most",
    )(order, rows, *blocks)


def last_kernel(first, tiles, order_ref, *rest):
    columns_refs, blocks = rest[:4], rest[4:8]
    gate_ref, up_ref, weight_ref, most_ref, before_ref, plan_ref = rest[8:14]
    out_ref, grads_ref, total_ref, stage_ref, out_sems, sums_ref = rest[15:]
    j, tile = pl.program_id(0), pl.program_id(1)

    @pl.when(tile == 0)
    def _():
        sums_ref[...] = before_ref[0]

    rows = jnp.concatenate([ref[0] for ref in columns_refs], axis=1)
    for e in range(2):

        @pl.when(j == e)
        def _(e=e):
            a_ref, b_ref = blocks[2 * e : 2 * e + 2]
            weight = jnp.concatenate([a_ref[0], a_ref[1], b_ref[0], b_ref[1]], axis=1)
            total_ref[...] = most_ref[0] + product(rows, weight)

    def compute(slot_ref):
        backward(total_ref, gate_ref, up_ref, weight_ref, slot_ref, sums_ref)

    staged(stage_ref, out_ref, out_sems, j, tile, tiles, first, compute)

    @pl.when(tile == tiles - 1)
    def _():
        cap, tokens = gate_ref.shape[3], plan_ref.shape[-1]
        slot = lax.broadcasted_iota(jnp.int32, (cap, tokens), 0).astype(F32)
        for s in range(gate_ref.shape[0]):
            value = jnp.sum(sums_ref[s * cap : (s + 1) * cap, :], axis=1, keepdims=True)
            owned = slot == plan_ref[s, pl.ds(j, 1), :]
            grads_ref[s, pl.ds(j, 1), :] = jnp.sum(
                jnp.where(owned, value, 0.0), axis=0, keepdims=True
            )


def last(order, rows, blocks, saved, weights, partial, before, plans, out):
    _, slots, width = rows.shape
    sources, _, _, cap, both = saved.shape
    tiles = blocks[0].shape[1] // TILE
    shift = both // 2 // TILE
    first = shift - tiles
    tokens = plans.shape[-1]
    tile = (sources, 1, 1, cap, TILE)
    return pl.pallas_call(
        functools.partial(last_kernel, first, tiles),
        grid_spec=pltpu.PrefetchScalarGridSpec(
            num_scalar_prefetch=1,
            grid=(2, tiles),
            in_specs=[
                pl.BlockSpec(
                    (1, slots, SHARD), lambda j, h, o, i=i: (j, 0, o[16 * j + 12 + i])
                )
                for i in range(4)
            ]
            + [pl.BlockSpec((2, TILE, SHARD), functools.partial(a_map, tiles))] * 2
            + [pl.BlockSpec((2, TILE, SHARD), b_map)] * 2
            + [
                pl.BlockSpec(tile, lambda j, h, o: (0, j, 0, 0, first + h)),
                pl.BlockSpec(tile, lambda j, h, o: (0, j, 0, 0, first + h + shift)),
                pl.BlockSpec((1, slots, 128), lambda j, h, o: (j, 0, 0)),
                pl.BlockSpec((1, slots, TILE), lambda j, h, o: (j, 0, h)),
                pl.BlockSpec((1, slots, 128), lambda j, h, o: (j, 0, 0)),
                pl.BlockSpec((sources, 4, tokens), lambda j, h, o: (0, 0, 0)),
                pl.BlockSpec(memory_space=pl.ANY),
            ],
            out_specs=[
                pl.BlockSpec(memory_space=pl.ANY),
                pl.BlockSpec((sources, 2, tokens), lambda j, h, o: (0, 0, 0)),
            ],
            scratch_shapes=[
                pltpu.VMEM((slots, TILE), F32),
                pltpu.VMEM((2, 2, sources, cap, TILE), BF),
                pltpu.SemaphoreType.DMA((2, 2)),
                pltpu.VMEM((slots, 128), F32),
            ],
        ),
        out_shape=[
            jax.ShapeDtypeStruct(saved.shape, BF),
            jax.ShapeDtypeStruct((sources, 2, tokens), F32),
        ],
        input_output_aliases={15: 0},
        compiler_params=params(2),
        cost_estimate=pl.CostEstimate(
            flops=4 * slots * width * tiles * TILE // 4,
            bytes_accessed=2 * slots * width + 2 * tiles * TILE * (width + 12 * slots),
            transcendentals=2 * slots * tiles * TILE,
        ),
        name="last",
    )(
        order, rows, rows, rows, rows, *blocks, saved, saved, weights, partial, before,
        plans, out,
    )


def shards(grad_out, route_weights, routes, saved_gate_up, down_weight):
    n_outer = lax.axis_size("outer")
    cap = saved_gate_up.shape[3]
    hid = down_weight.shape[1]
    split = hid - WAVE_TILES * TILE
    inner, outer = lax.axis_index("inner"), lax.axis_index("outer")
    z, y, x, core = inner // 4, inner % 4, outer // 2, outer % 2

    gathered = lax.all_gather(down_weight[:, :split], "inner", axis=0, tiled=False)

    a, b = down_weight[0, split:], down_weight[1, split:]
    first = [along_x(grad_out, 1), along_x(grad_out, -1)]
    one = [along(a, "y", 1), along(a, "y", -1), along(b, "z", 1), along(b, "z", -1)]
    one += [along(a, "y", 2), along(b, "z", 2)]
    one, first = together(one, first)
    half = grad_out.shape[0] // 2
    second = [along_x(first[0][:half], 1), along_x(first[1][half:], -1)]
    block_a = jnp.stack([a, one[0], one[1], one[4]])
    block_b = jnp.stack([b, one[2], one[3], one[5]])
    three = [
        along(block_a, "z", 1), along(block_a, "z", -1), along(block_b, "y", 1), along(block_b, "y", -1)
    ]

    mine = jnp.stack([grad_out, *first, jnp.concatenate(second)])
    other = lax.ppermute(mine, "outer", [(i, i ^ 1) for i in range(n_outer)])
    mine, named, scales = lax.optimization_barrier((mine, routes.T, route_weights.T))
    plans = lax.all_to_all(
        plan(named, scales, n_outer), "outer", split_axis=0, concat_axis=0, tiled=True
    )
    steps = jnp.array([0, -1, 1, 2], jnp.int32)
    source = ((x + steps) % 4) * 2
    filled = fill(source + core, mine, plans, cap)
    filled = fill(source + 1 - core, other, plans, cap, filled)
    rows = filled[0].reshape(2, n_outer * cap, grad_out.shape[1])
    weights = filled[1].reshape(2, n_outer * cap, 128)
    out, sums = whole(rows, gathered, saved_gate_up, weights)

    three, (out, sums) = together(three, [out, sums])
    four = [
        along(three[0][:2], "z", 1), along(three[1][2:], "z", -1),
        along(three[2][:2], "y", 1), along(three[3][2:], "y", -1),
    ]
    (four,) = together(four)

    near_z, near_y = (z + steps) % 4, (y + steps) % 4
    order = jnp.concatenate(
        [
            (near_z[:, None] * 4 + near_y[None, :]).reshape(-1),
            (near_y[:, None] + near_z[None, :] * 4).reshape(-1),
        ]
    )
    partial = most(order, rows, [block_a, three[0], three[1], block_b, three[2], three[3]])
    out, grads = last(order, rows, four, saved_gate_up, weights, partial, sums, plans, out)
    returned = lax.all_to_all(grads, "outer", split_axis=0, concat_axis=0, tiled=True)
    return (out, pick(routes.T, returned).T)


def solution(mesh):
    in_specs = (
        P(("outer", "inner"), None),
        P(("outer", "inner"), None),
        P(("outer", "inner"), None),
        P(None, "outer", "inner", None, None),
        P("outer", None, "inner"),
    )
    out_specs = (P(None, "outer", "inner", None, None), P(("outer", "inner"), None))
    return jax.shard_map(shards, mesh=mesh, in_specs=in_specs, out_specs=out_specs, check_vma=False)
```

time: 281 us -> 211 us (0.75)
  waiting for transfers between devices: 126 us -> 55.6 us
  Pallas kernels: 0 us -> 68.9 us
  local copies, waits for them, and re-layouts: 54.4 us -> 12.1 us
  other arithmetic: 43.4 us -> 5.91 us
  starting transfers between devices: 15.3 us -> 42.4 us
  matrix products: 26.7 us -> 0 us
  blocking collectives: 0 us -> 11.2 us
    all_to_all x3 -> x1, waiting for transfers between devices: 126 us -> 4.17 us  [shards(): lax.all_to_all(plan(named, scales, n_outer), 'outer', split_axis=0, conca...]
    pallas_call x0 -> x7, Pallas kernels: none -> 68.9 us  [the longest x1 18.6 us: most(): pl.pallas_call(most_kernel, grid_spec=pltpu.PrefetchScalarGridSpec(num_sc...]
    ppermute x0 -> x19, waiting for transfers between devices: none -> 51.4 us  [the longest x14 40.8 us: along(): return lax.ppermute(x, 'inner', ring(axis, step))]
    ppermute x0 -> x19, starting transfers between devices: none -> 37.3 us  [the longest x14 29.6 us: along(): return lax.ppermute(x, 'inner', ring(axis, step))]
    scatter x2 -> x0, local copies, waits for them, and re-layouts: 27.6 us -> none  [the longest x1 20 us: shards(): jnp.zeros((experts * capacity, width), jnp.bfloat16).at[slot]]
    dot_general x1 -> x0, matrix products: 26.7 us -> none  [shards(): jnp.einsum('sjcd,jhd->sjch', recv_rows, gathered, preferred_element_type=...]
    concatenate x2 -> x1, other arithmetic: 24 us -> 0.59 us  [shards(): jnp.concatenate([(near_z[:, None] * 4 + near_y[None, :]).reshape(-1), (ne...]
    gather x2 -> x0, local copies, waits for them, and re-layouts: 13.8 us -> none  [the longest x1 7.61 us: shards(): grad_out[token_of]]
  transfers between devices with their start and end apart: 4 -> 21, of which waited for: 1 -> 9; matrix products, arithmetic and copies ran while one was open for 26% -> 6% of each run, Pallas kernels for 0% -> 24%
where the time goes in v1:
time: 211 us; the launch traced here: 210 us
  Pallas kernels  68.9 us (33%)
  waiting for transfers between devices  55.6 us (26%)
  starting transfers between devices  42.4 us (20%)
  between operations  14.2 us (7%)
  local copies, waits for them, and re-layouts  12.1 us (6%)
  blocking collectives  11.2 us (5%)
  other arithmetic  5.91 us (3%)
    ppermute x14, waiting for transfers between devices, along(): return lax.ppermute(x, 'inner', ring(axis, step))  40.8 us
    ppermute x14, starting transfers between devices, along(): return lax.ppermute(x, 'inner', ring(axis, step))  29.6 us
    pallas_call x1, Pallas kernels, most(): pl.pallas_call(most_kernel, grid_spec=pltpu.PrefetchScalarGridSpec(num_sc...  18.6 us
    pallas_call x1, Pallas kernels, whole(): pl.pallas_call(functools.partial(whole_kernel, tiles), grid=(2, tiles), i...  17.2 us
    pallas_call x1, Pallas kernels, last(): pl.pallas_call(functools.partial(last_kernel, first, tiles), grid_spec=pl...  16.4 us
    pallas_call x2, Pallas kernels, fill(): pl.pallas_call(fill_kernel, grid_spec=pltpu.PrefetchScalarGridSpec(num_sc...  14.1 us
    all_to_all x1, blocking collectives, shards(): lax.all_to_all(grads, 'outer', split_axis=0, concat_axis=0, tiled=True)  11.2 us
    ppermute x4, waiting for transfers between devices, along_x(): return lax.ppermute(x, 'outer', pairs)  10.6 us
  transfers between devices with their start and end apart: 21, of which 9 were waited for; matrix products, arithmetic and copies ran while one was open for 6% of the time, Pallas kernels for 24%

profile of v1, /device:TPU:1, one launch (start us, length us, event | category | flops | bytes accessed | tf_op | source)
XLA Modules:
  0.0 210.3 jit_solution(15825238127819844216)
XLA Ops:
  7.2 2.0 slice.31
  9.4 2.2 %collective-permute-start = (bf16[1024,256]{1,0:T(8,128)(2,1)S(1)}, bf16[1024,256]{1,0:T(8,128)(2,1)S(1)}, u32[]{:S(2)}, u32[]{:S(2)}) collective-permute-start(bf16[1024,256]{1,0:T(8,128)(2,1)S(1)} %get-tuple-element.63), channel_id=1, source_target_pairs={{0,1},{1,2},{2,3},{3,0},{4,5},{5,6},{6,7},{7,4},{8,9},{9,10},{10,1... | collective-permute-start | bytes 1572872 | tf_op jit(solution)/shard_map/ppermute | solution.py:30
  17.4 7.1 %collective-permute-done = bf16[1024,256]{1,0:T(8,128)(2,1)S(1)} collective-permute-done((bf16[1024,256]{1,0:T(8,128)(2,1)S(1)}, bf16[1024,256]{1,0:T(8,128)(2,1)S(1)}, u32[]{:S(2)}, u32[]{:S(2)}) %collective-permute-start) | collective-permute-done | bytes 524320 | tf_op jit(solution)/shard_map/ppermute | solution.py:30
  24.5 3.7 %collective-permute-start.3 = (bf16[1024,256]{1,0:T(8,128)(2,1)S(1)}, bf16[1024,256]{1,0:T(8,128)(2,1)S(1)}, u32[]{:S(2)}, u32[]{:S(2)}) collective-permute-start(bf16[1024,256]{1,0:T(8,128)(2,1)S(1)} %get-tuple-element.64), channel_id=1, source_target_pairs={{0,12},{1,13},{2,14},{3,15},{4,0},{5,1},{6,2},{7,3},{8,4},{9,5},{1... | collective-permute-start | bytes 1572872 | tf_op jit(solution)/shard_map/ppermute | solution.py:30
  30.3 15.8 %collective-permute-done.3 = bf16[1024,256]{1,0:T(8,128)(2,1)S(1)} collective-permute-done((bf16[1024,256]{1,0:T(8,128)(2,1)S(1)}, bf16[1024,256]{1,0:T(8,128)(2,1)S(1)}, u32[]{:S(2)}, u32[]{:S(2)}) %collective-permute-start.3) | collective-permute-done | bytes 524320 | tf_op jit(solution)/shard_map/ppermute | solution.py:30
  52.1 10.6 %collective-permute-done.8 = bf16[64,4096]{1,0:T(8,128)(2,1)S(1)} collective-permute-done((bf16[64,4096]{1,0:T(8,128)(2,1)S(1)}, bf16[64,4096]{1,0:T(8,128)(2,1)S(1)}, u32[]{:S(2)}, u32[]{:S(2)}) %collective-permute-start.8) | collective-permute-done | bytes 524320 | tf_op jit(solution)/shard_map/ppermute | solution.py:35
  62.8 2.3 %pad_maximum_fusion.tokens_ref = bf16[4,128,4096]{2,1,0:T(8,128)(2,1)} fusion(bf16[1,128,4096]{2,1,0:T(8,128)(2,1)S(1)} %maximum_bitcast_fusion, bf16[1,128,4096]{2,1,0:T(8,128)(2,1)S(1)} %bitcast.31, bf16[1,128,4096]{2,1,0:T(8,128)(2,1)S(1)} %bitcast.30, bf16[1,128,4096]{2,1,0:T(8,128)(2,1)S(1)} %bitcast.32), kind=kLoop, calls=%fused_computation | loop fusion | flops 6291456 | bytes 8388608 | tf_op jit(solution)/shard_map/stack | solution.py:490
  65.1 2.2 %collective-permute-start.10 = (bf16[4,128,4096]{2,1,0:T(8,128)(2,1)}, bf16[4,128,4096]{2,1,0:T(8,128)(2,1)}, u32[]{:S(2)}, u32[]{:S(2)}) collective-permute-start(bf16[4,128,4096]{2,1,0:T(8,128)(2,1)} %pad_maximum_fusion.tokens_ref), channel_id=1, source_target_pairs={{0,16},{16,0},{32,48},{48,32},{64,80},{80,64},{96,112},{112,96},{1... | collective-permute-start | bytes 12582920 | tf_op jit(solution)/shard_map/ppermute | solution.py:491
  67.6 9.9 %collective-permute-start.11 = (bf16[4,1024,256]{2,1,0:T(8,128)(2,1)S(1)}, bf16[4,1024,256]{2,1,0:T(8,128)(2,1)}, u32[]{:S(2)}, u32[]{:S(2)}) collective-permute-start(bf16[4,1024,256]{2,1,0:T(8,128)(2,1)S(1)} %pad_maximum_fusion.1.rest_0_), channel_id=1, source_target_pairs={{0,4},{1,5},{2,6},{3,7},{4,8},{5,9},{6,10},{7,11},{8,12},{9,13},{1... | collective-permute-start | bytes 6291464 | tf_op jit(solution)/shard_map/ppermute | solution.py:30
  80.3 2.0 collective-permute-start.14
  84.3 5.1 %all-to-all-start = ((f32[8,4,128]{2,1,0:T(4,128)}), f32[8,4,128]{2,1,0:T(4,128)S(1)}, u32[]{:S(2)}, u32[]{:S(2)}) async-start(f32[8,4,128]{2,1,0:T(4,128)} %plan.1), calls=%async_computation | async-start | bytes 32768 | tf_op jit(solution)/shard_map/all_to_all | solution.py:493
  89.9 4.2 %all-to-all-done.plan_ref.rest_13_ = f32[8,4,128]{2,1,0:T(4,128)S(1)} async-done(((f32[8,4,128]{2,1,0:T(4,128)}), f32[8,4,128]{2,1,0:T(4,128)S(1)}, u32[]{:S(2)}, u32[]{:S(2)}) %all-to-all-start) | async-done | bytes 16416 | tf_op jit(solution)/shard_map/all_to_all | solution.py:493
  94.7 7.0 %fill.2 = (bf16[2,8,96,4096]{3,2,1,0:T(8,128)(2,1)}, f32[2,8,96,128]{3,2,1,0:T(8,128)}) custom-call(s32[4]{0:T(128)} %get-tuple-element.60.source_ref, bf16[4,128,4096]{2,1,0:T(8,128)(2,1)} %pad_maximum_fusion.tokens_ref, f32[8,4,128]{2,1,0:T(4,128)} %copy-done.6), custom_call_target="tpu_custom_call" | custom-call | flops 805306368 | bytes 10485760 | tf_op jit(solution)/shard_map/fill/pallas_call | solution.py:119
  101.7 7.0 %fill.3 = (bf16[2,8,96,4096]{3,2,1,0:T(8,128)(2,1)}, f32[2,8,96,128]{3,2,1,0:T(8,128)}) custom-call(s32[4]{0:T(128)} %add_subtract_fusion.source_ref, bf16[4,128,4096]{2,1,0:T(8,128)(2,1)} %collective-permute-done.10.tokens_ref, f32[8,4,128]{2,1,0:T(4,128)} %copy-done.6, ...), custom_call_target="tpu_custom_call", output_to_operand_aliasing={{0}: (3, {}), {1}: (4, {})} | custom-call | flops 805306368 | bytes 10485760 | tf_op jit(solution)/shard_map/fill/pallas_call | solution.py:119
  108.8 17.2 %whole.1 = (bf16[8,2,1,96,3072]{4,3,2,1,0:T(8,128)(2,1)}, f32[2,768,128]{2,1,0:T(8,128)}) custom-call(bf16[2,768,4096]{2,1,0:T(8,128)(2,1)} %bitcast.21, bf16[16,2,512,256]{3,2,1,0:T(8,128)(2,1)} %bitcast.27, bf16[8,2,1,96,3072]{4,3,2,1,0:T(8,128)(2,1)} %rest_9_.1, bf16[8,2,1,96,3072]{4,3,2,1,0:T(8,128)(2,1)} %rest_9_.1, f32[2,768,128]{2,1,0:T(8,128)} %bitcast.28), custom_call_target="tpu_custom_call" | custom-call | flops 6442450944 | bytes 27262976 | tf_op jit(solution)/shard_map/whole/pallas_call | solution.py:268
  125.9 11.9 %collective-permute-done.11.rest_1_ = bf16[4,1024,256]{2,1,0:T(8,128)(2,1)} collective-permute-done((bf16[4,1024,256]{2,1,0:T(8,128)(2,1)S(1)}, bf16[4,1024,256]{2,1,0:T(8,128)(2,1)}, u32[]{:S(2)}, u32[]{:S(2)}) %collective-permute-start.11) | collective-permute-done | bytes 2097184 | tf_op jit(solution)/shard_map/ppermute | solution.py:30
  137.9 2.3 %slice.32 = bf16[2,1024,256]{2,1,0:T(8,128)(2,1)} slice(bf16[4,1024,256]{2,1,0:T(8,128)(2,1)} %collective-permute-done.11.rest_1_), slice={[0:2], [0:1024], [0:256]} | slice | bytes 2097152 | tf_op jit(solution)/shard_map/slice | solution.py:506
  141.0 2.3 %slice.33 = bf16[2,1024,256]{2,1,0:T(8,128)(2,1)} slice(bf16[4,1024,256]{2,1,0:T(8,128)(2,1)} %collective-permute-done.12.rest_2_), slice={[2:4], [0:1024], [0:256]} | slice | bytes 2097152 | tf_op jit(solution)/shard_map/slice | solution.py:506
  145.1 2.3 %slice.34 = bf16[2,1024,256]{2,1,0:T(8,128)(2,1)} slice(bf16[4,1024,256]{2,1,0:T(8,128)(2,1)} %collective-permute-done.13.rest_4_), slice={[0:2], [0:1024], [0:256]} | slice | bytes 2097152 | tf_op jit(solution)/shard_map/slice | solution.py:507
  148.6 2.3 %slice.35 = bf16[2,1024,256]{2,1,0:T(8,128)(2,1)} slice(bf16[4,1024,256]{2,1,0:T(8,128)(2,1)} %collective-permute-done.14.rest_5_), slice={[2:4], [0:1024], [0:256]} | slice | bytes 2097152 | tf_op jit(solution)/shard_map/slice | solution.py:507
  153.2 18.6 %most.1.rest_11_ = f32[2,768,1024]{2,1,0:T(8,128)} custom-call(s32[32]{0:T(128)} %pad_add_fusion.order_ref, bf16[2,768,4096]{2,1,0:T(8,128)(2,1)} %bitcast.22, bf16[4,1024,256]{2,1,0:T(8,128)(2,1)} %copy-done, bf16[4,1024,256]{2,1,0:T(8,128)(2,1)} %collective-permute-done.11.rest_1_, bf16[4,1024,256]{2,1,0:T(8,128)(2,1)} %collective-permute-done.12.rest_2_, ...), custom_call_target="tpu_custom_call" | custom-call | flops 9663676416 | bytes 35651584 | tf_op jit(solution)/shard_map/most/pallas_call | solution.py:347
  172.5 2.1 collective-permute-done.18.rest_7_
  174.6 16.4 %last.1 = (bf16[8,2,1,96,3072]{4,3,2,1,0:T(8,128)(2,1)}, f32[8,2,128]{2,1,0:T(2,128)}) custom-call(s32[32]{0:T(128)} %pad_add_fusion.order_ref, bf16[2,768,4096]{2,1,0:T(8,128)(2,1)} %bitcast.23, bf16[2,768,4096]{2,1,0:T(8,128)(2,1)} %bitcast.24, bf16[2,768,4096]{2,1,0:T(8,128)(2,1)} %bitcast.25, ...), custom_call_target="tpu_custom_call", output_to_operand_aliasing={{0}: (15, {})} | custom-call | flops 3221225472 | bytes 33554432 | tf_op jit(solution)/shard_map/last/pallas_call | solution.py:416
  191.0 11.2 %all_to_all.10.grads_ref = f32[8,2,128]{2,1,0:T(2,128)} all-to-all(f32[8,2,128]{2,1,0:T(2,128)} %get-tuple-element.59), channel_id=1, replica_groups=mesh['outer'=8,'inner'=16] {'outer'}, dimensions={0} | all-to-all | bytes 16384 | tf_op jit(solution)/shard_map/all_to_all | solution.py:520
  (61 shorter events, 28.6 us)
Async XLA Ops:
  7.2 101.6 %all-gather.3.cloned.1.call-start = ((), (), s32[]{:S(2)}) async-start(), calls=%async_computation.2 | async-start | bytes 8912896 | tf_op jit(solution)/shard_map/all_gather | solution.py:475
  9.2 5.5 %copy-start.5 = (bf16[128,4096]{1,0:T(8,128)(2,1)S(1)}, bf16[128,4096]{1,0:T(8,128)(2,1)}, u32[]{:S(2)}) copy-start(bf16[128,4096]{1,0:T(8,128)(2,1)} %param.6) | copy-start | bytes 3145732
  9.4 15.1 %collective-permute-start = (bf16[1024,256]{1,0:T(8,128)(2,1)S(1)}, bf16[1024,256]{1,0:T(8,128)(2,1)S(1)}, u32[]{:S(2)}, u32[]{:S(2)}) collective-permute-start(bf16[1024,256]{1,0:T(8,128)(2,1)S(1)} %get-tuple-element.63), channel_id=1, source_target_pairs={{0,1},{1,2},{2,3},{3,0},{4,5},{5,6},{6,7},{7,4},{8,9},{9,10},{10,1... | collective-permute-start | bytes 1572872 | tf_op jit(solution)/shard_map/ppermute | solution.py:30
  11.6 16.6 %collective-permute-start.1 = (bf16[1024,256]{1,0:T(8,128)(2,1)S(1)}, bf16[1024,256]{1,0:T(8,128)(2,1)S(1)}, u32[]{:S(2)}, u32[]{:S(2)}) collective-permute-start(bf16[1024,256]{1,0:T(8,128)(2,1)S(1)} %get-tuple-element.63), channel_id=1, source_target_pairs={{0,3},{1,0},{2,1},{3,2},{4,7},{5,4},{6,5},{7,6},{8,11},{9,8},{10,9... | collective-permute-start | bytes 1572872 | tf_op jit(solution)/shard_map/ppermute | solution.py:30
  13.1 16.7 %collective-permute-start.2 = (bf16[1024,256]{1,0:T(8,128)(2,1)S(1)}, bf16[1024,256]{1,0:T(8,128)(2,1)S(1)}, u32[]{:S(2)}, u32[]{:S(2)}) collective-permute-start(bf16[1024,256]{1,0:T(8,128)(2,1)S(1)} %get-tuple-element.64), channel_id=1, source_target_pairs={{0,4},{1,5},{2,6},{3,7},{4,8},{5,9},{6,10},{7,11},{8,12},{9,13},{1... | collective-permute-start | bytes 1572872 | tf_op jit(solution)/shard_map/ppermute | solution.py:30
  14.7 34.5 %collective-permute-start.6 = (bf16[128,4096]{1,0:T(8,128)(2,1)S(1)}, bf16[128,4096]{1,0:T(8,128)(2,1)S(1)}, u32[]{:S(2)}, u32[]{:S(2)}) collective-permute-start(bf16[128,4096]{1,0:T(8,128)(2,1)S(1)} %copy-done.5), channel_id=1, source_target_pairs={{0,32},{16,48},{32,64},{48,80},{64,96},{80,112},{96,0},{112,16},{1... | collective-permute-start | bytes 3145736 | tf_op jit(solution)/shard_map/ppermute | solution.py:35
  15.9 33.3 %collective-permute-start.7 = (bf16[128,4096]{1,0:T(8,128)(2,1)S(1)}, bf16[128,4096]{1,0:T(8,128)(2,1)S(1)}, u32[]{:S(2)}, u32[]{:S(2)}) collective-permute-start(bf16[128,4096]{1,0:T(8,128)(2,1)S(1)} %copy-done.5), channel_id=1, source_target_pairs={{0,96},{16,112},{32,0},{48,16},{64,32},{80,48},{96,64},{112,80},{1... | collective-permute-start | bytes 3145736 | tf_op jit(solution)/shard_map/ppermute | solution.py:35
  24.5 21.5 %collective-permute-start.3 = (bf16[1024,256]{1,0:T(8,128)(2,1)S(1)}, bf16[1024,256]{1,0:T(8,128)(2,1)S(1)}, u32[]{:S(2)}, u32[]{:S(2)}) collective-permute-start(bf16[1024,256]{1,0:T(8,128)(2,1)S(1)} %get-tuple-element.64), channel_id=1, source_target_pairs={{0,12},{1,13},{2,14},{3,15},{4,0},{5,1},{6,2},{7,3},{8,4},{9,5},{1... | collective-permute-start | bytes 1572872 | tf_op jit(solution)/shard_map/ppermute | solution.py:30
  28.2 19.2 %collective-permute-start.4 = (bf16[1024,256]{1,0:T(8,128)(2,1)S(1)}, bf16[1024,256]{1,0:T(8,128)(2,1)S(1)}, u32[]{:S(2)}, u32[]{:S(2)}) collective-permute-start(bf16[1024,256]{1,0:T(8,128)(2,1)S(1)} %get-tuple-element.63), channel_id=1, source_target_pairs={{0,2},{1,3},{2,0},{3,1},{4,6},{5,7},{6,4},{7,5},{8,10},{9,11},{10,... | collective-permute-start | bytes 1572872 | tf_op jit(solution)/shard_map/ppermute | solution.py:30
  29.7 19.5 %collective-permute-start.5 = (bf16[1024,256]{1,0:T(8,128)(2,1)S(1)}, bf16[1024,256]{1,0:T(8,128)(2,1)S(1)}, u32[]{:S(2)}, u32[]{:S(2)}) collective-permute-start(bf16[1024,256]{1,0:T(8,128)(2,1)S(1)} %get-tuple-element.64), channel_id=1, source_target_pairs={{0,8},{1,9},{2,10},{3,11},{4,12},{5,13},{6,14},{7,15},{8,0},{9,1},... | collective-permute-start | bytes 1572872 | tf_op jit(solution)/shard_map/ppermute | solution.py:30
  49.3 13.5 %collective-permute-start.8 = (bf16[64,4096]{1,0:T(8,128)(2,1)S(1)}, bf16[64,4096]{1,0:T(8,128)(2,1)S(1)}, u32[]{:S(2)}, u32[]{:S(2)}) collective-permute-start(bf16[64,4096]{1,0:T(8,128)(2,1)S(1)} %slice.29), channel_id=1, source_target_pairs={{0,32},{16,48},{32,64},{48,80},{64,96},{80,112},{96,0},{112,16},{1... | collective-permute-start | bytes 1572872 | tf_op jit(solution)/shard_map/ppermute | solution.py:35
  50.6 12.2 %collective-permute-start.9 = (bf16[64,4096]{1,0:T(8,128)(2,1)S(1)}, bf16[64,4096]{1,0:T(8,128)(2,1)S(1)}, u32[]{:S(2)}, u32[]{:S(2)}) collective-permute-start(bf16[64,4096]{1,0:T(8,128)(2,1)S(1)} %slice.30), channel_id=1, source_target_pairs={{0,96},{16,112},{32,0},{48,16},{64,32},{80,48},{96,64},{112,80},{1... | collective-permute-start | bytes 1572872 | tf_op jit(solution)/shard_map/ppermute | solution.py:35
  65.1 36.6 %collective-permute-start.10 = (bf16[4,128,4096]{2,1,0:T(8,128)(2,1)}, bf16[4,128,4096]{2,1,0:T(8,128)(2,1)}, u32[]{:S(2)}, u32[]{:S(2)}) collective-permute-start(bf16[4,128,4096]{2,1,0:T(8,128)(2,1)} %pad_maximum_fusion.tokens_ref), channel_id=1, source_target_pairs={{0,16},{16,0},{32,48},{48,32},{64,80},{80,64},{96,112},{112,96},{1... | collective-permute-start | bytes 12582920 | tf_op jit(solution)/shard_map/ppermute | solution.py:491
  67.6 12.0 %copy-start = (bf16[4,1024,256]{2,1,0:T(8,128)(2,1)}, bf16[4,1024,256]{2,1,0:T(8,128)(2,1)S(1)}, u32[]{:S(2)}) copy-start(bf16[4,1024,256]{2,1,0:T(8,128)(2,1)S(1)} %pad_maximum_fusion.1.rest_0_) | copy-start | bytes 6291460
  67.6 70.3 %collective-permute-start.11 = (bf16[4,1024,256]{2,1,0:T(8,128)(2,1)S(1)}, bf16[4,1024,256]{2,1,0:T(8,128)(2,1)}, u32[]{:S(2)}, u32[]{:S(2)}) collective-permute-start(bf16[4,1024,256]{2,1,0:T(8,128)(2,1)S(1)} %pad_maximum_fusion.1.rest_0_), channel_id=1, source_target_pairs={{0,4},{1,5},{2,6},{3,7},{4,8},{5,9},{6,10},{7,11},{8,12},{9,13},{1... | collective-permute-start | bytes 6291464 | tf_op jit(solution)/shard_map/ppermute | solution.py:30
  77.5 60.4 %collective-permute-start.12 = (bf16[4,1024,256]{2,1,0:T(8,128)(2,1)S(1)}, bf16[4,1024,256]{2,1,0:T(8,128)(2,1)}, u32[]{:S(2)}, u32[]{:S(2)}) collective-permute-start(bf16[4,1024,256]{2,1,0:T(8,128)(2,1)S(1)} %pad_maximum_fusion.1.rest_0_), channel_id=1, source_target_pairs={{0,12},{1,13},{2,14},{3,15},{4,0},{5,1},{6,2},{7,3},{8,4},{9,5},{1... | collective-permute-start | bytes 6291464 | tf_op jit(solution)/shard_map/ppermute | solution.py:30
  78.1 4.3 %copy-start.7 = (s32[4]{0:T(128)S(1)}, s32[4]{0:T(128)}, u32[]{:S(2)}) copy-start(s32[4]{0:T(128)} %constant.75.clone) | copy-start | bytes 52
  79.7 58.2 %collective-permute-start.13 = (bf16[4,1024,256]{2,1,0:T(8,128)(2,1)}, bf16[4,1024,256]{2,1,0:T(8,128)(2,1)}, u32[]{:S(2)}, u32[]{:S(2)}) collective-permute-start(bf16[4,1024,256]{2,1,0:T(8,128)(2,1)} %pad_maximum_fusion.2.rest_3_), channel_id=1, source_target_pairs={{0,1},{1,2},{2,3},{3,0},{4,5},{5,6},{6,7},{7,4},{8,9},{9,10},{10,1... | collective-permute-start | bytes 6291464 | tf_op jit(solution)/shard_map/ppermute | solution.py:30
  80.3 57.5 %collective-permute-start.14 = (bf16[4,1024,256]{2,1,0:T(8,128)(2,1)}, bf16[4,1024,256]{2,1,0:T(8,128)(2,1)}, u32[]{:S(2)}, u32[]{:S(2)}) collective-permute-start(bf16[4,1024,256]{2,1,0:T(8,128)(2,1)} %pad_maximum_fusion.2.rest_3_), channel_id=1, source_target_pairs={{0,3},{1,0},{2,1},{3,2},{4,7},{5,4},{6,5},{7,6},{8,11},{9,8},{10,9... | collective-permute-start | bytes 6291464 | tf_op jit(solution)/shard_map/ppermute | solution.py:30
  84.3 9.8 %all-to-all-start = ((f32[8,4,128]{2,1,0:T(4,128)}), f32[8,4,128]{2,1,0:T(4,128)S(1)}, u32[]{:S(2)}, u32[]{:S(2)}) async-start(f32[8,4,128]{2,1,0:T(4,128)} %plan.1), calls=%async_computation | async-start | bytes 32768 | tf_op jit(solution)/shard_map/all_to_all | solution.py:493
  140.2 31.6 %collective-permute-start.15 = (bf16[2,1024,256]{2,1,0:T(8,128)(2,1)}, bf16[2,1024,256]{2,1,0:T(8,128)(2,1)S(1)}, u32[]{:S(2)}, u32[]{:S(2)}) collective-permute-start(bf16[2,1024,256]{2,1,0:T(8,128)(2,1)} %slice.32), channel_id=1, source_target_pairs={{0,4},{1,5},{2,6},{3,7},{4,8},{5,9},{6,10},{7,11},{8,12},{9,13},{1... | collective-permute-start | bytes 3145736 | tf_op jit(solution)/shard_map/ppermute | solution.py:30
  143.2 28.6 %collective-permute-start.16 = (bf16[2,1024,256]{2,1,0:T(8,128)(2,1)}, bf16[2,1024,256]{2,1,0:T(8,128)(2,1)S(1)}, u32[]{:S(2)}, u32[]{:S(2)}) collective-permute-start(bf16[2,1024,256]{2,1,0:T(8,128)(2,1)} %slice.33), channel_id=1, source_target_pairs={{0,12},{1,13},{2,14},{3,15},{4,0},{5,1},{6,2},{7,3},{8,4},{9,5},{1... | collective-permute-start | bytes 3145736 | tf_op jit(solution)/shard_map/ppermute | solution.py:30
  147.4 25.1 %collective-permute-start.17 = (bf16[2,1024,256]{2,1,0:T(8,128)(2,1)}, bf16[2,1024,256]{2,1,0:T(8,128)(2,1)S(1)}, u32[]{:S(2)}, u32[]{:S(2)}) collective-permute-start(bf16[2,1024,256]{2,1,0:T(8,128)(2,1)} %slice.34), channel_id=1, source_target_pairs={{0,1},{1,2},{2,3},{3,0},{4,5},{5,6},{6,7},{7,4},{8,9},{9,10},{10,1... | collective-permute-start | bytes 3145736 | tf_op jit(solution)/shard_map/ppermute | solution.py:30
  150.9 23.7 %collective-permute-start.18 = (bf16[2,1024,256]{2,1,0:T(8,128)(2,1)}, bf16[2,1024,256]{2,1,0:T(8,128)(2,1)}, u32[]{:S(2)}, u32[]{:S(2)}) collective-permute-start(bf16[2,1024,256]{2,1,0:T(8,128)(2,1)} %slice.35), channel_id=1, source_target_pairs={{0,3},{1,0},{2,1},{3,2},{4,7},{5,4},{6,5},{7,6},{8,11},{9,8},{10,9... | collective-permute-start | bytes 3145736 | tf_op jit(solution)/shard_map/ppermute | solution.py:30
  (5 other events, 10.3 us)
Sparse Core Ops, SparseCore 0:
  10.1 96.3 all-gather.2

commit v2 on v1

--- a/solution.py
+++ b/solution.py
@@ -9,10 +9,13 @@
 
 BF = jnp.bfloat16
 F32 = jnp.float32
+PARTS = 2
 SHARD = 256
 TILE = 512
 WAVE_TILES = 2
 VMEM = 56 * 1024 * 1024
+MOST_VMEM = 32 * 1024 * 1024
+LAST_VMEM = 50 * 1024 * 1024
 
 
 def ring(axis, step):
@@ -30,18 +33,22 @@
     return lax.ppermute(x, "inner", ring(axis, step))
 
 
-def along_x(x, step):
-    pairs = [(a * 2 + c, ((a + step) % 4) * 2 + c) for a in range(4) for c in range(2)]
+def along_x(x):
+    pairs = [(a * 2 + c, ((a + 1 - 2 * c) % 4) * 2 + c) for a in range(4) for c in range(2)]
     return lax.ppermute(x, "outer", pairs)
+
+
+def other_core(x):
+    return lax.ppermute(x, "outer", [(i, i ^ 1) for i in range(8)])
 
 
 def together(*groups):
     return [list(g) for g in lax.optimization_barrier(tuple(tuple(g) for g in groups))]
 
 
-def params(steps):
+def params(steps, vmem=VMEM):
     return pltpu.CompilerParams(
-        dimension_semantics=("arbitrary",) * steps, vmem_limit_bytes=VMEM
+        dimension_semantics=("arbitrary",) * steps, vmem_limit_bytes=vmem
     )
 
 
@@ -90,8 +97,7 @@
     )(routes, grads)
 
 
-def fill_kernel(source_ref, tokens_ref, plan_ref, *rest):
-    rows_ref, weight_ref = rest[-2:]
+def fill_block(tokens_ref, plan_ref, rows_ref, weight_ref):
     tokens = plan_ref.shape[-1]
     cap = rows_ref.shape[2]
     slot = lax.broadcasted_iota(jnp.int32, (cap, tokens), 0).astype(F32)
@@ -112,30 +118,46 @@
         rows_ref[1, 0, :, c : c + step] = rows[cap:].astype(BF)
 
 
-def fill(sources, tokens, plans, cap, earlier=None):
-    count, rows, width = tokens.shape
-    n_outer = plans.shape[0]
-    extra = [] if earlier is None else list(earlier)
+def fill_kernel(starts, source_ref, *refs):
+    tokens_refs, (plan_ref, rows_ref, weight_ref) = refs[:-3], refs[-3:]
+    q = pl.program_id(0)
+    for n, tokens_ref in enumerate(tokens_refs):
+
+        @pl.when((q >= starts[n]) & (q < starts[n + 1]))
+        def _(tokens_ref=tokens_ref):
+            fill_block(tokens_ref, plan_ref, rows_ref, weight_ref)
+
+
+def fill(sources, tokens, plans, cap):
+    _, rows, width = tokens[0].shape
+    starts = [0]
+    for part in tokens:
+        starts.append(starts[-1] + part.shape[0])
+    count = starts[-1]
     return pl.pallas_call(
-        fill_kernel,
+        functools.partial(fill_kernel, starts),
         grid_spec=pltpu.PrefetchScalarGridSpec(
             num_scalar_prefetch=1,
             grid=(count,),
             in_specs=[
-                pl.BlockSpec((1, rows, width), lambda q, src: (q, 0, 0)),
-                pl.BlockSpec((1, 4, rows), lambda q, src: (src[q], 0, 0)),
+                pl.BlockSpec(
+                    (1, rows, width),
+                    lambda q, src, lo=starts[n], top=part.shape[0] - 1: (
+                        jnp.clip(q - lo, 0, top), 0, 0
+                    ),
+                )
+                for n, part in enumerate(tokens)
             ]
-            + [pl.BlockSpec(memory_space=pl.ANY)] * len(extra),
+            + [pl.BlockSpec((1, 4, rows), lambda q, src: (src[q], 0, 0))],
             out_specs=[
                 pl.BlockSpec((2, 1, cap, width), lambda q, src: (0, src[q], 0, 0)),
                 pl.BlockSpec((2, 1, cap, 128), lambda q, src: (0, src[q], 0, 0)),
             ],
         ),
         out_shape=[
-            jax.ShapeDtypeStruct((2, n_outer, cap, width), BF),
-            jax.ShapeDtypeStruct((2, n_outer, cap, 128), F32),
+            jax.ShapeDtypeStruct((2, count, cap, width), BF),
+            jax.ShapeDtypeStruct((2, count, cap, 128), F32),
         ],
-        input_output_aliases={3: 0, 4: 1} if extra else {},
         compiler_params=params(1),
         cost_estimate=pl.CostEstimate(
             flops=2 * count * 2 * cap * rows * width,
@@ -143,7 +165,7 @@
             transcendentals=0,
         ),
         name="fill",
-    )(sources, tokens, plans, *extra)
+    )(sources, *tokens, plans)
 
 
 def product(rows, weight):
@@ -152,10 +174,11 @@
     )
 
 
-def backward(total_ref, gate_ref, up_ref, weight_ref, out_ref, sums_ref):
-    sources, cap = gate_ref.shape[0], gate_ref.shape[3]
-    for s in range(sources):
+def backward(total_ref, gate_ref, up_ref, weight_ref, out_ref, sums_ref, sources):
+    cap = gate_ref.shape[3]
+    for s in sources:
         at = slice(s * cap, (s + 1) * cap)
+        weight = weight_ref[0, at, :]
         for c in range(0, TILE, 128):
             cols = slice(c, c + 128)
             carried = total_ref[at, cols]
@@ -164,12 +187,14 @@
             sigma = 0.5 * jnp.tanh(0.5 * gate) + 0.5
             active = gate * sigma
             hidden = (active * upper).astype(BF).astype(F32)
-            sums_ref[at, :] += carried * hidden
-            scaled = weight_ref[0, at, :] * carried
+            part = carried * hidden
+            sums = part if c == 0 else sums + part
+            scaled = weight * carried
             out_ref[0, s, :, cols] = (
                 scaled * upper * (sigma + active * (1.0 - sigma))
             ).astype(BF)
             out_ref[1, s, :, cols] = (scaled * active).astype(BF)
+        sums_ref[at, :] += sums
 
 
 def out_copies(stage_ref, out_ref, sems, slot, j, tile):
@@ -254,7 +279,10 @@
         total_ref[...] = part if k == 0 else total_ref[...] + part
 
     def compute(slot_ref):
-        backward(total_ref, gate_ref, up_ref, weight_ref, slot_ref, sums_ref.at[0])
+        backward(
+            total_ref, gate_ref, up_ref, weight_ref, slot_ref, sums_ref.at[0],
+            range(gate_ref.shape[0]),
+        )
 
     staged(stage_ref, out_ref, out_sems, j, tile, tiles, 0, compute)
 
@@ -359,7 +387,7 @@
             ],
         ),
         out_shape=jax.ShapeDtypeStruct((2, slots, tiles * TILE), F32),
-        compiler_params=params(2),
+        compiler_params=params(2, MOST_VMEM),
         cost_estimate=pl.CostEstimate(
             flops=4 * slots * width * tiles * TILE * 3 // 4,
             bytes_accessed=4 * slots * width + 2 * tiles * TILE * (2 * width + 4 * slots),
@@ -379,17 +407,30 @@
     def _():
         sums_ref[...] = before_ref[0]
 
-    rows = jnp.concatenate([ref[0] for ref in columns_refs], axis=1)
-    for e in range(2):
-
-        @pl.when(j == e)
-        def _(e=e):
-            a_ref, b_ref = blocks[2 * e : 2 * e + 2]
-            weight = jnp.concatenate([a_ref[0], a_ref[1], b_ref[0], b_ref[1]], axis=1)
-            total_ref[...] = most_ref[0] + product(rows, weight)
+    sources, cap = gate_ref.shape[0], gate_ref.shape[3]
+    group = sources // PARTS
 
     def compute(slot_ref):
-        backward(total_ref, gate_ref, up_ref, weight_ref, slot_ref, sums_ref)
+        for e in range(2):
+
+            @pl.when(j == e)
+            def _(e=e):
+                a_ref, b_ref = blocks[2 * e : 2 * e + 2]
+                weight = jnp.concatenate([a_ref[0], a_ref[1], b_ref[0], b_ref[1]], axis=1)
+
+                def multiply(n):
+                    at = slice(n * group * cap, (n + 1) * group * cap)
+                    rows = jnp.concatenate([ref[0, at, :] for ref in columns_refs], axis=1)
+                    total_ref[at, :] = most_ref[0, at, :] + product(rows, weight)
+
+                multiply(0)
+                for n in range(PARTS):
+                    if n + 1 < PARTS:
+                        multiply(n + 1)
+                    backward(
+                        total_ref, gate_ref, up_ref, weight_ref, slot_ref, sums_ref,
+                        range(n * group, (n + 1) * group),
+                    )
 
     staged(stage_ref, out_ref, out_sems, j, tile, tiles, first, compute)
 
@@ -451,7 +492,7 @@
             jax.ShapeDtypeStruct((sources, 2, tokens), F32),
         ],
         input_output_aliases={15: 0},
-        compiler_params=params(2),
+        compiler_params=params(2, LAST_VMEM),
         cost_estimate=pl.CostEstimate(
             flops=4 * slots * width * tiles * TILE // 4,
             bytes_accessed=2 * slots * width + 2 * tiles * TILE * (width + 12 * slots),
@@ -464,6 +505,36 @@
     )
 
 
+def halves_kernel(*refs):
+    blocks, parts, held, sems = refs[:4], refs[4:8], refs[8:12], refs[12]
+    reads = [
+        pltpu.make_async_copy(blocks[n].at[pl.ds(2 * (n % 2), 2)], held[n], sems.at[0, n])
+        for n in range(4)
+    ]
+    writes = [pltpu.make_async_copy(held[n], parts[n], sems.at[1, n]) for n in range(4)]
+    for copy in reads:
+        copy.start()
+    for read, write in zip(reads, writes):
+        read.wait()
+        write.start()
+    for copy in writes:
+        copy.wait()
+
+
+def halves(blocks):
+    _, tall, wide = blocks[0].shape
+    return pl.pallas_call(
+        halves_kernel,
+        in_specs=[pl.BlockSpec(memory_space=pl.ANY)] * 4,
+        out_specs=[pl.BlockSpec(memory_space=pl.ANY)] * 4,
+        out_shape=[jax.ShapeDtypeStruct((2, tall, wide), BF)] * 4,
+        scratch_shapes=[pltpu.VMEM((2, tall, wide), BF)] * 4
+        + [pltpu.SemaphoreType.DMA((2, 4))],
+        compiler_params=pltpu.CompilerParams(vmem_limit_bytes=VMEM),
+        name="halves",
+    )(*blocks)
+
+
 def shards(grad_out, route_weights, routes, saved_gate_up, down_weight):
     n_outer = lax.axis_size("outer")
     cap = saved_gate_up.shape[3]
@@ -471,40 +542,50 @@
     split = hid - WAVE_TILES * TILE
     inner, outer = lax.axis_index("inner"), lax.axis_index("outer")
     z, y, x, core = inner // 4, inner % 4, outer // 2, outer % 2
+    steps = jnp.array([0, -1, 1, 2], jnp.int32)
 
     gathered = lax.all_gather(down_weight[:, :split], "inner", axis=0, tiled=False)
 
     a, b = down_weight[0, split:], down_weight[1, split:]
-    first = [along_x(grad_out, 1), along_x(grad_out, -1)]
+    pair = jnp.stack([grad_out, other_core(grad_out)])
+    pair, (a, b) = lax.optimization_barrier((pair, (a, b)))
     one = [along(a, "y", 1), along(a, "y", -1), along(b, "z", 1), along(b, "z", -1)]
-    one += [along(a, "y", 2), along(b, "z", 2)]
-    one, first = together(one, first)
-    half = grad_out.shape[0] // 2
-    second = [along_x(first[0][:half], 1), along_x(first[1][half:], -1)]
-    block_a = jnp.stack([a, one[0], one[1], one[4]])
-    block_b = jnp.stack([b, one[2], one[3], one[5]])
+    near = along_x(pair)
+    one, (near,) = together(one, [near])
+    two = [along(one[0], "y", 1), along(one[3], "z", -1)]
+    far = along_x(near[0])
+    near_other = other_core(near)
+    two, (far, near_other, named, scales) = together(
+        two, [far, near_other, routes.T, route_weights.T]
+    )
+    block_a = jnp.stack([a, one[0], one[1], two[0]])
+    block_b = jnp.stack([b, one[2], one[3], two[1]])
     three = [
         along(block_a, "z", 1), along(block_a, "z", -1), along(block_b, "y", 1), along(block_b, "y", -1)
     ]
 
-    mine = jnp.stack([grad_out, *first, jnp.concatenate(second)])
-    other = lax.ppermute(mine, "outer", [(i, i ^ 1) for i in range(n_outer)])
-    mine, named, scales = lax.optimization_barrier((mine, routes.T, route_weights.T))
+    far_other = other_core(far)
     plans = lax.all_to_all(
         plan(named, scales, n_outer), "outer", split_axis=0, concat_axis=0, tiled=True
     )
-    steps = jnp.array([0, -1, 1, 2], jnp.int32)
-    source = ((x + steps) % 4) * 2
-    filled = fill(source + core, mine, plans, cap)
-    filled = fill(source + 1 - core, other, plans, cap, filled)
+    came, went = (x + 2 * core - 1) % 4, (x + 1 - 2 * core) % 4
+    opposite = (x + 2) % 4
+    source = jnp.stack(
+        [
+            2 * x + core, 2 * x + 1 - core, 2 * came + core, 2 * came + 1 - core,
+            2 * went + 1 - core, 2 * went + core, 2 * opposite + core, 2 * opposite + 1 - core,
+        ]
+    )
+    filled = fill(source, [pair, near, near_other, far[None], far_other[None]], plans, cap)
     rows = filled[0].reshape(2, n_outer * cap, grad_out.shape[1])
     weights = filled[1].reshape(2, n_outer * cap, 128)
     out, sums = whole(rows, gathered, saved_gate_up, weights)
 
     three, (out, sums) = together(three, [out, sums])
+    parts = halves(three)
     four = [
-        along(three[0][:2], "z", 1), along(three[1][2:], "z", -1),
-        along(three[2][:2], "y", 1), along(three[3][2:], "y", -1),
+        along(parts[0], "z", 1), along(parts[1], "z", -1),
+        along(parts[2], "y", 1), along(parts[3], "y", -1),
     ]
     (four,) = together(four)
 

time: 211 us -> 202 us (0.957)
  waiting for transfers between devices: 55.6 us -> 69.1 us
  starting transfers between devices: 42.4 us -> 32.1 us
  local copies, waits for them, and re-layouts: 12.1 us -> 7.51 us
  other arithmetic: 5.91 us -> 2.25 us
    ppermute x14, waiting for transfers between devices: 40.8 us -> 52.9 us  [along(): return lax.ppermute(x, 'inner', ring(axis, step))]
    ppermute x4 -> x2, waiting for transfers between devices: 10.6 us -> 0.01 us  [along_x(): return lax.ppermute(x, 'outer', pairs)]
    all_gather x1, waiting for transfers between devices: 0.01 us -> 9.83 us  [shards(): lax.all_gather(down_weight[:, :split], 'inner', axis=0, tiled=False)]
    slice x7 -> x0, local copies, waits for them, and re-layouts: 9.34 us -> none  [the longest x1 2.31 us: shards(): three[2][:2]]
    ppermute x14, starting transfers between devices: 29.6 us -> 23.1 us  [along(): return lax.ppermute(x, 'inner', ring(axis, step))]
    unnamed x16 -> x24, local copies, waits for them, and re-layouts: 0.63 us -> 4.58 us
    pallas_call x1, Pallas kernels: 16.4 us -> 13.8 us  [last(): pl.pallas_call(functools.partial(last_kernel, first, tiles), grid_spec=pl...]
    ppermute x4 -> x2, starting transfers between devices: 5.49 us -> 3.03 us  [along_x(): return lax.ppermute(x, 'outer', pairs)]
  transfers between devices with their start and end apart: 21 -> 21, of which waited for: 9 -> 13; matrix products, arithmetic and copies ran while one was open for 6% -> 2% of each run, Pallas kernels for 24% -> 24%
where the time goes in v2:
time: 202 us; the launch traced here: 201 us
  waiting for transfers between devices  69.1 us (34%)
  Pallas kernels  66.8 us (33%)
  starting transfers between devices  32.1 us (16%)
  between operations  14.3 us (7%)
  blocking collectives  9.43 us (5%)
  local copies, waits for them, and re-layouts  7.51 us (4%)
  other arithmetic  2.25 us (1%)
    ppermute x14, waiting for transfers between devices, along(): return lax.ppermute(x, 'inner', ring(axis, step))  52.9 us
    ppermute x14, starting transfers between devices, along(): return lax.ppermute(x, 'inner', ring(axis, step))  23.1 us
    pallas_call x1, Pallas kernels, most(): pl.pallas_call(most_kernel, grid_spec=pltpu.PrefetchScalarGridSpec(num_sc...  17.5 us
    pallas_call x1, Pallas kernels, whole(): pl.pallas_call(functools.partial(whole_kernel, tiles), grid=(2, tiles), i...  16.9 us
    pallas_call x1, Pallas kernels, last(): pl.pallas_call(functools.partial(last_kernel, first, tiles), grid_spec=pl...  13.8 us
    pallas_call x1, Pallas kernels, fill(): pl.pallas_call(functools.partial(fill_kernel, starts), grid_spec=pltpu.Pr...  12.5 us
    all_gather x1, waiting for transfers between devices, shards(): lax.all_gather(down_weight[:, :split], 'inner', axis=0, tiled=False)  9.83 us
    all_to_all x1, blocking collectives, shards(): lax.all_to_all(grads, 'outer', split_axis=0, concat_axis=0, tiled=True)  9.43 us
  transfers between devices with their start and end apart: 21, of which 13 were waited for; matrix products, arithmetic and copies ran while one was open for 2% of the time, Pallas kernels for 24%

profile of v2, /device:TPU:1, one launch (start us, length us, event | category | flops | bytes accessed | tf_op | source)
XLA Modules:
  0.0 201.4 jit_solution(9004956628191742522)
XLA Ops:
  7.2 2.0 %slice.15 = bf16[2,512,256]{2,1,0:T(8,128)(2,1)} slice(bf16[2,1536,256]{2,1,0:T(8,128)(2,1)} %param.10), slice={[0:2], [0:512], [0:256]} | slice | bytes 1048576 | tf_op jit(solution)/shard_map/slice | solution.py:547
  10.8 2.4 %collective-permute-done = bf16[128,4096]{1,0:T(8,128)(2,1)S(1)} collective-permute-done((bf16[128,4096]{1,0:T(8,128)(2,1)}, bf16[128,4096]{1,0:T(8,128)(2,1)S(1)}, u32[]{:S(2)}, u32[]{:S(2)}) %collective-permute-start) | collective-permute-done | bytes 1048608 | tf_op jit(solution)/shard_map/ppermute | solution.py:42
  13.5 2.6 %collective-permute-start.5 = (bf16[2,128,4096]{2,1,0:T(8,128)(2,1)S(1)}, bf16[2,128,4096]{2,1,0:T(8,128)(2,1)S(1)}, u32[]{:S(2)}, u32[]{:S(2)}) collective-permute-start(bf16[2,128,4096]{2,1,0:T(8,128)(2,1)S(1)} %pad_maximum_fusion.refs_0_), channel_id=1, source_target_pairs={{0,32},{16,112},{32,64},{48,16},{64,96},{80,48},{96,0},{112,80},{1... | collective-permute-start | bytes 6291464 | tf_op jit(solution)/shard_map/ppermute | solution.py:38
  18.9 1.6 collective-permute-start.3
  20.5 2.1 %collective-permute-start.4 = (bf16[1024,256]{1,0:T(8,128)(2,1)S(1)}, bf16[1024,256]{1,0:T(8,128)(2,1)S(1)}, u32[]{:S(2)}, u32[]{:S(2)}) collective-permute-start(bf16[1024,256]{1,0:T(8,128)(2,1)S(1)} %get-tuple-element.38), channel_id=1, source_target_pairs={{0,12},{1,13},{2,14},{3,15},{4,0},{5,1},{6,2},{7,3},{8,4},{9,5},{1... | collective-permute-start | bytes 1572872 | tf_op jit(solution)/shard_map/ppermute | solution.py:33
  22.6 12.1 %collective-permute-done.1 = bf16[1024,256]{1,0:T(8,128)(2,1)S(1)} collective-permute-done((bf16[1024,256]{1,0:T(8,128)(2,1)S(1)}, bf16[1024,256]{1,0:T(8,128)(2,1)S(1)}, u32[]{:S(2)}, u32[]{:S(2)}) %collective-permute-start.1) | collective-permute-done | bytes 524320 | tf_op jit(solution)/shard_map/ppermute | solution.py:33
  36.4 5.5 %collective-permute-done.3 = bf16[1024,256]{1,0:T(8,128)(2,1)S(1)} collective-permute-done((bf16[1024,256]{1,0:T(8,128)(2,1)S(1)}, bf16[1024,256]{1,0:T(8,128)(2,1)S(1)}, u32[]{:S(2)}, u32[]{:S(2)}) %collective-permute-start.3) | collective-permute-done | bytes 524320 | tf_op jit(solution)/shard_map/ppermute | solution.py:33
  44.0 3.8 %collective-permute-start.7 = (bf16[1024,256]{1,0:T(8,128)(2,1)S(1)}, bf16[1024,256]{1,0:T(8,128)(2,1)S(1)}, u32[]{:S(2)}, u32[]{:S(2)}) collective-permute-start(bf16[1024,256]{1,0:T(8,128)(2,1)S(1)} %collective-permute-done.4), channel_id=1, source_target_pairs={{0,12},{1,13},{2,14},{3,15},{4,0},{5,1},{6,2},{7,3},{8,4},{9,5},{1... | collective-permute-start | bytes 1572872 | tf_op jit(solution)/shard_map/ppermute | solution.py:33
  47.7 16.2 %collective-permute-done.6 = bf16[1024,256]{1,0:T(8,128)(2,1)S(1)} collective-permute-done((bf16[1024,256]{1,0:T(8,128)(2,1)S(1)}, bf16[1024,256]{1,0:T(8,128)(2,1)S(1)}, u32[]{:S(2)}, u32[]{:S(2)}) %collective-permute-start.6) | collective-permute-done | bytes 524320 | tf_op jit(solution)/shard_map/ppermute | solution.py:33
  63.9 4.8 %collective-permute-done.7 = bf16[1024,256]{1,0:T(8,128)(2,1)S(1)} collective-permute-done((bf16[1024,256]{1,0:T(8,128)(2,1)S(1)}, bf16[1024,256]{1,0:T(8,128)(2,1)S(1)}, u32[]{:S(2)}, u32[]{:S(2)}) %collective-permute-start.7) | collective-permute-done | bytes 524320 | tf_op jit(solution)/shard_map/ppermute | solution.py:33
  74.7 3.5 %collective-permute-start.12 = (bf16[4,1024,256]{2,1,0:T(8,128)(2,1)}, bf16[4,1024,256]{2,1,0:T(8,128)(2,1)}, u32[]{:S(2)}, u32[]{:S(2)}) collective-permute-start(bf16[4,1024,256]{2,1,0:T(8,128)(2,1)} %pad_maximum_fusion.1.rest_0_), channel_id=1, source_target_pairs={{0,12},{1,13},{2,14},{3,15},{4,0},{5,1},{6,2},{7,3},{8,4},{9,5},{1... | collective-permute-start | bytes 6291464 | tf_op jit(solution)/shard_map/ppermute | solution.py:33
  80.1 3.5 %all-to-all-start = ((f32[8,4,128]{2,1,0:T(4,128)}), f32[8,4,128]{2,1,0:T(4,128)S(1)}, u32[]{:S(2)}, u32[]{:S(2)}) async-start(f32[8,4,128]{2,1,0:T(4,128)} %plan.1), calls=%async_computation | async-start | bytes 32768 | tf_op jit(solution)/shard_map/all_to_all | solution.py:568
  84.3 3.9 %all-to-all-done.refs_5_.rest_13_ = f32[8,4,128]{2,1,0:T(4,128)S(1)} async-done(((f32[8,4,128]{2,1,0:T(4,128)}), f32[8,4,128]{2,1,0:T(4,128)S(1)}, u32[]{:S(2)}, u32[]{:S(2)}) %all-to-all-start) | async-done | bytes 16416 | tf_op jit(solution)/shard_map/all_to_all | solution.py:568
  88.8 12.5 %fill.1 = (bf16[2,8,96,4096]{3,2,1,0:T(8,128)(2,1)}, f32[2,8,96,128]{3,2,1,0:T(8,128)}) custom-call(s32[8]{0:T(128)} %stack.74.source_ref, bf16[2,128,4096]{2,1,0:T(8,128)(2,1)} %copy-done.5, bf16[2,128,4096]{2,1,0:T(8,128)(2,1)} %copy-done.6, bf16[2,128,4096]{2,1,0:T(8,128)(2,1)} %copy-done.7, bf16[1,128,4096]{2,1,0:T(8,128)(2,1)} %bitcast.43, ...), custom_call_target="tpu_custom_call" | custom-call | flops 1610612736 | bytes 20971520 | tf_op jit(solution)/shard_map/fill/pallas_call | solution.py:137
  101.3 9.8 %all-gather.3.cloned.1.call-done = bf16[32,512,256]{2,1,0:T(8,128)(2,1)} async-done(((bf16[2,512,256]{2,1,0:T(8,128)(2,1)}), bf16[32,512,256]{2,1,0:T(8,128)(2,1)}) %all-gather.3.cloned.1.call-update) | async-done | bytes 8388624 | tf_op jit(solution)/shard_map/all_gather | solution.py:547
  111.1 16.9 %whole.1 = (bf16[8,2,1,96,3072]{4,3,2,1,0:T(8,128)(2,1)}, f32[2,768,128]{2,1,0:T(8,128)}) custom-call(bf16[2,768,4096]{2,1,0:T(8,128)(2,1)} %bitcast.34, bf16[16,2,512,256]{3,2,1,0:T(8,128)(2,1)} %bitcast.40, bf16[8,2,1,96,3072]{4,3,2,1,0:T(8,128)(2,1)} %rest_9_.1, bf16[8,2,1,96,3072]{4,3,2,1,0:T(8,128)(2,1)} %rest_9_.1, f32[2,768,128]{2,1,0:T(8,128)} %bitcast.32), custom_call_target="tpu_custom_call" | custom-call | flops 6442450944 | bytes 27262976 | tf_op jit(solution)/shard_map/whole/pallas_call | solution.py:296
  128.1 9.4 %collective-permute-done.13.refs_2_.rest_4_ = bf16[4,1024,256]{2,1,0:T(8,128)(2,1)} collective-permute-done((bf16[4,1024,256]{2,1,0:T(8,128)(2,1)S(1)}, bf16[4,1024,256]{2,1,0:T(8,128)(2,1)}, u32[]{:S(2)}, u32[]{:S(2)}) %collective-permute-start.13) | collective-permute-done | bytes 2097184 | tf_op jit(solution)/shard_map/ppermute | solution.py:33
  137.8 3.3 %halves.1 = (bf16[2,1024,256]{2,1,0:T(8,128)(2,1)}, bf16[2,1024,256]{2,1,0:T(8,128)(2,1)}, bf16[2,1024,256]{2,1,0:T(8,128)(2,1)}, bf16[2,1024,256]{2,1,0:T(8,128)(2,1)}) custom-call(bf16[4,1024,256]{2,1,0:T(8,128)(2,1)} %collective-permute-done.11.refs_0_.rest_1_, bf16[4,1024,256]{2,1,0:T(8,128)(2,1)} %collective-permute-done.12.refs_1_.rest_2_, ...), custom_call_target="tpu_custom_call" | custom-call | tf_op jit(solution)/shard_map/halves/pallas_call | solution.py:526
  142.0 2.7 %collective-permute-start.16 = (bf16[2,1024,256]{2,1,0:T(8,128)(2,1)}, bf16[2,1024,256]{2,1,0:T(8,128)(2,1)}, u32[]{:S(2)}, u32[]{:S(2)}) collective-permute-start(bf16[2,1024,256]{2,1,0:T(8,128)(2,1)} %get-tuple-element.59), channel_id=1, source_target_pairs={{0,12},{1,13},{2,14},{3,15},{4,0},{5,1},{6,2},{7,3},{8,4},{9,5},{1... | collective-permute-start | bytes 3145736 | tf_op jit(solution)/shard_map/ppermute | solution.py:33
  147.7 17.5 %most.1.rest_11_ = f32[2,768,1024]{2,1,0:T(8,128)S(1)} custom-call(s32[32]{0:T(128)S(1)} %pad_add_fusion.order_ref, bf16[2,768,4096]{2,1,0:T(8,128)(2,1)} %bitcast.35, bf16[4,1024,256]{2,1,0:T(8,128)(2,1)} %pad_maximum_fusion.1.rest_0_, bf16[4,1024,256]{2,1,0:T(8,128)(2,1)} %collective-permute-done.11.refs_0_.rest_1_, ...), custom_call_target="tpu_custom_call" | custom-call | flops 9663676416 | bytes 35651584 | tf_op jit(solution)/shard_map/most/pallas_call | solution.py:375
  165.2 2.6 %copy-done = f32[2,768,1024]{2,1,0:T(8,128)} copy-done((f32[2,768,1024]{2,1,0:T(8,128)}, f32[2,768,1024]{2,1,0:T(8,128)S(1)}, u32[]{:S(2)}) %copy-start) | copy-done | bytes 6291480
  167.9 2.1 %collective-permute-done.17.rest_6_ = bf16[2,1024,256]{2,1,0:T(8,128)(2,1)} collective-permute-done((bf16[2,1024,256]{2,1,0:T(8,128)(2,1)}, bf16[2,1024,256]{2,1,0:T(8,128)(2,1)}, u32[]{:S(2)}, u32[]{:S(2)}) %collective-permute-start.17) | collective-permute-done | bytes 1048608 | tf_op jit(solution)/shard_map/ppermute | solution.py:33
  170.0 13.8 %last.1 = (bf16[8,2,1,96,3072]{4,3,2,1,0:T(8,128)(2,1)}, f32[8,2,128]{2,1,0:T(2,128)S(1)}) custom-call(s32[32]{0:T(128)S(1)} %pad_add_fusion.order_ref, bf16[2,768,4096]{2,1,0:T(8,128)(2,1)} %bitcast.36, bf16[2,768,4096]{2,1,0:T(8,128)(2,1)} %bitcast.37, bf16[2,768,4096]{2,1,0:T(8,128)(2,1)} %bitcast.38, ...), custom_call_target="tpu_custom_call", output_to_operand_aliasing={{0}: (15, {})} | custom-call | flops 3221225472 | bytes 33554432 | tf_op jit(solution)/shard_map/last/pallas_call | solution.py:457
  183.8 9.4 %all_to_all.10.grads_ref = f32[8,2,128]{2,1,0:T(2,128)} all-to-all(f32[8,2,128]{2,1,0:T(2,128)S(1)} %get-tuple-element.69), channel_id=1, replica_groups=mesh['outer'=8,'inner'=16] {'outer'}, dimensions={0} | all-to-all | bytes 16384 | tf_op jit(solution)/shard_map/all_to_all | solution.py:601
  (63 shorter events, 22.9 us)
Async XLA Ops:
  7.2 103.9 %all-gather.3.cloned.1.call-start = ((), (), s32[]{:S(2)}) async-start(), calls=%async_computation.2 | async-start | bytes 8912896 | tf_op jit(solution)/shard_map/all_gather | solution.py:547
  9.3 4.0 %collective-permute-start = (bf16[128,4096]{1,0:T(8,128)(2,1)}, bf16[128,4096]{1,0:T(8,128)(2,1)S(1)}, u32[]{:S(2)}, u32[]{:S(2)}) collective-permute-start(bf16[128,4096]{1,0:T(8,128)(2,1)} %param.6), channel_id=1, source_target_pairs={{0,16},{16,0},{32,48},{48,32},{64,80},{80,64},{96,112},{112,96},{1... | collective-permute-start | bytes 3145736 | tf_op jit(solution)/shard_map/ppermute | solution.py:42
  13.5 56.9 %copy-start.5 = (bf16[2,128,4096]{2,1,0:T(8,128)(2,1)}, bf16[2,128,4096]{2,1,0:T(8,128)(2,1)S(1)}, u32[]{:S(2)}) copy-start(bf16[2,128,4096]{2,1,0:T(8,128)(2,1)S(1)} %pad_maximum_fusion.refs_0_) | copy-start | bytes 6291460
  13.5 29.0 %collective-permute-start.5 = (bf16[2,128,4096]{2,1,0:T(8,128)(2,1)S(1)}, bf16[2,128,4096]{2,1,0:T(8,128)(2,1)S(1)}, u32[]{:S(2)}, u32[]{:S(2)}) collective-permute-start(bf16[2,128,4096]{2,1,0:T(8,128)(2,1)S(1)} %pad_maximum_fusion.refs_0_), channel_id=1, source_target_pairs={{0,32},{16,112},{32,64},{48,16},{64,96},{80,48},{96,0},{112,80},{1... | collective-permute-start | bytes 6291464 | tf_op jit(solution)/shard_map/ppermute | solution.py:38
  16.1 18.6 %collective-permute-start.1 = (bf16[1024,256]{1,0:T(8,128)(2,1)S(1)}, bf16[1024,256]{1,0:T(8,128)(2,1)S(1)}, u32[]{:S(2)}, u32[]{:S(2)}) collective-permute-start(bf16[1024,256]{1,0:T(8,128)(2,1)S(1)} %get-tuple-element.37), channel_id=1, source_target_pairs={{0,1},{1,2},{2,3},{3,0},{4,5},{5,6},{6,7},{7,4},{8,9},{9,10},{10,1... | collective-permute-start | bytes 1572872 | tf_op jit(solution)/shard_map/ppermute | solution.py:33
  17.4 18.9 %collective-permute-start.2 = (bf16[1024,256]{1,0:T(8,128)(2,1)S(1)}, bf16[1024,256]{1,0:T(8,128)(2,1)S(1)}, u32[]{:S(2)}, u32[]{:S(2)}) collective-permute-start(bf16[1024,256]{1,0:T(8,128)(2,1)S(1)} %get-tuple-element.37), channel_id=1, source_target_pairs={{0,3},{1,0},{2,1},{3,2},{4,7},{5,4},{6,5},{7,6},{8,11},{9,8},{10,9... | collective-permute-start | bytes 1572872 | tf_op jit(solution)/shard_map/ppermute | solution.py:33
  18.9 23.0 %collective-permute-start.3 = (bf16[1024,256]{1,0:T(8,128)(2,1)S(1)}, bf16[1024,256]{1,0:T(8,128)(2,1)S(1)}, u32[]{:S(2)}, u32[]{:S(2)}) collective-permute-start(bf16[1024,256]{1,0:T(8,128)(2,1)S(1)} %get-tuple-element.38), channel_id=1, source_target_pairs={{0,4},{1,5},{2,6},{3,7},{4,8},{5,9},{6,10},{7,11},{8,12},{9,13},{1... | collective-permute-start | bytes 1572872 | tf_op jit(solution)/shard_map/ppermute | solution.py:33
  20.5 22.0 %collective-permute-start.4 = (bf16[1024,256]{1,0:T(8,128)(2,1)S(1)}, bf16[1024,256]{1,0:T(8,128)(2,1)S(1)}, u32[]{:S(2)}, u32[]{:S(2)}) collective-permute-start(bf16[1024,256]{1,0:T(8,128)(2,1)S(1)} %get-tuple-element.38), channel_id=1, source_target_pairs={{0,12},{1,13},{2,14},{3,15},{4,0},{5,1},{6,2},{7,3},{8,4},{9,5},{1... | collective-permute-start | bytes 1572872 | tf_op jit(solution)/shard_map/ppermute | solution.py:33
  42.5 26.2 %copy-start.6 = (bf16[2,128,4096]{2,1,0:T(8,128)(2,1)}, bf16[2,128,4096]{2,1,0:T(8,128)(2,1)S(1)}, u32[]{:S(2)}) copy-start(bf16[2,128,4096]{2,1,0:T(8,128)(2,1)S(1)} %collective-permute-done.5.refs_1_) | copy-start | bytes 6291460
  42.5 26.2 %collective-permute-start.9 = (bf16[2,128,4096]{2,1,0:T(8,128)(2,1)S(1)}, bf16[2,128,4096]{2,1,0:T(8,128)(2,1)S(1)}, u32[]{:S(2)}, u32[]{:S(2)}) collective-permute-start(bf16[2,128,4096]{2,1,0:T(8,128)(2,1)S(1)} %collective-permute-done.5.refs_1_), channel_id=1, source_target_pairs={{0,16},{16,0},{32,48},{48,32},{64,80},{80,64},{96,112},{112,96},{1... | collective-permute-start | bytes 6291464 | tf_op jit(solution)/shard_map/ppermute | solution.py:42
  43.3 25.5 %collective-permute-start.8 = (bf16[128,4096]{1,0:T(8,128)(2,1)S(1)}, bf16[128,4096]{1,0:T(8,128)(2,1)S(1)}, u32[]{:S(2)}, u32[]{:S(2)}) collective-permute-start(bf16[128,4096]{1,0:T(8,128)(2,1)S(1)} %slice_bitcast_fusion), channel_id=1, source_target_pairs={{0,32},{16,112},{32,64},{48,16},{64,96},{80,48},{96,0},{112,80},{1... | collective-permute-start | bytes 3145736 | tf_op jit(solution)/shard_map/ppermute | solution.py:38
  43.7 20.2 %collective-permute-start.6 = (bf16[1024,256]{1,0:T(8,128)(2,1)S(1)}, bf16[1024,256]{1,0:T(8,128)(2,1)S(1)}, u32[]{:S(2)}, u32[]{:S(2)}) collective-permute-start(bf16[1024,256]{1,0:T(8,128)(2,1)S(1)} %collective-permute-done.1), channel_id=1, source_target_pairs={{0,1},{1,2},{2,3},{3,0},{4,5},{5,6},{6,7},{7,4},{8,9},{9,10},{10,1... | collective-permute-start | bytes 1572872 | tf_op jit(solution)/shard_map/ppermute | solution.py:33
  44.0 24.8 %collective-permute-start.7 = (bf16[1024,256]{1,0:T(8,128)(2,1)S(1)}, bf16[1024,256]{1,0:T(8,128)(2,1)S(1)}, u32[]{:S(2)}, u32[]{:S(2)}) collective-permute-start(bf16[1024,256]{1,0:T(8,128)(2,1)S(1)} %collective-permute-done.4), channel_id=1, source_target_pairs={{0,12},{1,13},{2,14},{3,15},{4,0},{5,1},{6,2},{7,3},{8,4},{9,5},{1... | collective-permute-start | bytes 1572872 | tf_op jit(solution)/shard_map/ppermute | solution.py:33
  70.4 67.2 %collective-permute-start.13 = (bf16[4,1024,256]{2,1,0:T(8,128)(2,1)S(1)}, bf16[4,1024,256]{2,1,0:T(8,128)(2,1)}, u32[]{:S(2)}, u32[]{:S(2)}) collective-permute-start(bf16[4,1024,256]{2,1,0:T(8,128)(2,1)S(1)} %pad_maximum_fusion.2.rest_3_), channel_id=1, source_target_pairs={{0,1},{1,2},{2,3},{3,0},{4,5},{5,6},{6,7},{7,4},{8,9},{9,10},{10,1... | collective-permute-start | bytes 6291464 | tf_op jit(solution)/shard_map/ppermute | solution.py:33
  71.6 65.9 %collective-permute-start.14 = (bf16[4,1024,256]{2,1,0:T(8,128)(2,1)S(1)}, bf16[4,1024,256]{2,1,0:T(8,128)(2,1)}, u32[]{:S(2)}, u32[]{:S(2)}) collective-permute-start(bf16[4,1024,256]{2,1,0:T(8,128)(2,1)S(1)} %pad_maximum_fusion.2.rest_3_), channel_id=1, source_target_pairs={{0,3},{1,0},{2,1},{3,2},{4,7},{5,4},{6,5},{7,6},{8,11},{9,8},{10,9... | collective-permute-start | bytes 6291464 | tf_op jit(solution)/shard_map/ppermute | solution.py:33
  74.7 62.8 %collective-permute-start.11 = (bf16[4,1024,256]{2,1,0:T(8,128)(2,1)}, bf16[4,1024,256]{2,1,0:T(8,128)(2,1)}, u32[]{:S(2)}, u32[]{:S(2)}) collective-permute-start(bf16[4,1024,256]{2,1,0:T(8,128)(2,1)} %pad_maximum_fusion.1.rest_0_), channel_id=1, source_target_pairs={{0,4},{1,5},{2,6},{3,7},{4,8},{5,9},{6,10},{7,11},{8,12},{9,13},{1... | collective-permute-start | bytes 6291464 | tf_op jit(solution)/shard_map/ppermute | solution.py:33
  74.7 63.1 %collective-permute-start.12 = (bf16[4,1024,256]{2,1,0:T(8,128)(2,1)}, bf16[4,1024,256]{2,1,0:T(8,128)(2,1)}, u32[]{:S(2)}, u32[]{:S(2)}) collective-permute-start(bf16[4,1024,256]{2,1,0:T(8,128)(2,1)} %pad_maximum_fusion.1.rest_0_), channel_id=1, source_target_pairs={{0,12},{1,13},{2,14},{3,15},{4,0},{5,1},{6,2},{7,3},{8,4},{9,5},{1... | collective-permute-start | bytes 6291464 | tf_op jit(solution)/shard_map/ppermute | solution.py:33
  78.3 9.9 %collective-permute-start.10 = (bf16[128,4096]{1,0:T(8,128)(2,1)S(1)}, bf16[128,4096]{1,0:T(8,128)(2,1)}, u32[]{:S(2)}, u32[]{:S(2)}) collective-permute-start(bf16[128,4096]{1,0:T(8,128)(2,1)S(1)} %collective-permute-done.8), channel_id=1, source_target_pairs={{0,16},{16,0},{32,48},{48,32},{64,80},{80,64},{96,112},{112,96},{1... | collective-permute-start | bytes 3145736 | tf_op jit(solution)/shard_map/ppermute | solution.py:42
  80.1 8.1 %all-to-all-start = ((f32[8,4,128]{2,1,0:T(4,128)}), f32[8,4,128]{2,1,0:T(4,128)S(1)}, u32[]{:S(2)}, u32[]{:S(2)}) async-start(f32[8,4,128]{2,1,0:T(4,128)} %plan.1), calls=%async_computation | async-start | bytes 32768 | tf_op jit(solution)/shard_map/all_to_all | solution.py:568
  141.1 26.8 %collective-permute-start.15 = (bf16[2,1024,256]{2,1,0:T(8,128)(2,1)}, bf16[2,1024,256]{2,1,0:T(8,128)(2,1)S(1)}, u32[]{:S(2)}, u32[]{:S(2)}) collective-permute-start(bf16[2,1024,256]{2,1,0:T(8,128)(2,1)} %get-tuple-element.58), channel_id=1, source_target_pairs={{0,4},{1,5},{2,6},{3,7},{4,8},{5,9},{6,10},{7,11},{8,12},{9,13},{1... | collective-permute-start | bytes 3145736 | tf_op jit(solution)/shard_map/ppermute | solution.py:33
  142.0 25.9 %collective-permute-start.16 = (bf16[2,1024,256]{2,1,0:T(8,128)(2,1)}, bf16[2,1024,256]{2,1,0:T(8,128)(2,1)}, u32[]{:S(2)}, u32[]{:S(2)}) collective-permute-start(bf16[2,1024,256]{2,1,0:T(8,128)(2,1)} %get-tuple-element.59), channel_id=1, source_target_pairs={{0,12},{1,13},{2,14},{3,15},{4,0},{5,1},{6,2},{7,3},{8,4},{9,5},{1... | collective-permute-start | bytes 3145736 | tf_op jit(solution)/shard_map/ppermute | solution.py:33
  144.7 25.3 %collective-permute-start.17 = (bf16[2,1024,256]{2,1,0:T(8,128)(2,1)}, bf16[2,1024,256]{2,1,0:T(8,128)(2,1)}, u32[]{:S(2)}, u32[]{:S(2)}) collective-permute-start(bf16[2,1024,256]{2,1,0:T(8,128)(2,1)} %get-tuple-element.60), channel_id=1, source_target_pairs={{0,1},{1,2},{2,3},{3,0},{4,5},{5,6},{6,7},{7,4},{8,9},{9,10},{10,1... | collective-permute-start | bytes 3145736 | tf_op jit(solution)/shard_map/ppermute | solution.py:33
  145.9 24.1 %collective-permute-start.18 = (bf16[2,1024,256]{2,1,0:T(8,128)(2,1)}, bf16[2,1024,256]{2,1,0:T(8,128)(2,1)}, u32[]{:S(2)}, u32[]{:S(2)}) collective-permute-start(bf16[2,1024,256]{2,1,0:T(8,128)(2,1)} %get-tuple-element.61), channel_id=1, source_target_pairs={{0,3},{1,0},{2,1},{3,2},{4,7},{5,4},{6,5},{7,6},{8,11},{9,8},{10,9... | collective-permute-start | bytes 3145736 | tf_op jit(solution)/shard_map/ppermute | solution.py:33
  147.7 22.4 %copy-start.4 = (f32[8,4,128]{2,1,0:T(4,128)S(1)}, f32[8,4,128]{2,1,0:T(4,128)}, u32[]{:S(2)}) copy-start(f32[8,4,128]{2,1,0:T(4,128)} %copy-done.3) | copy-start | bytes 49156
  (9 other events, 88.9 us)
Sparse Core Ops, SparseCore 0:
  10.2 100.9 all-gather.2

commit v3 on v2

--- a/solution.py
+++ b/solution.py
@@ -552,14 +552,16 @@
     one = [along(a, "y", 1), along(a, "y", -1), along(b, "z", 1), along(b, "z", -1)]
     near = along_x(pair)
     one, (near,) = together(one, [near])
-    two = [along(one[0], "y", 1), along(one[3], "z", -1)]
+    cut = a.shape[0] // 2
+    two = [
+        along(one[0][:cut], "y", 1), along(one[1][cut:], "y", -1),
+        along(one[2][:cut], "z", 1), along(one[3][cut:], "z", -1),
+    ]
     far = along_x(near[0])
+    two, (far, named, scales) = together(two, [far, routes.T, route_weights.T])
     near_other = other_core(near)
-    two, (far, near_other, named, scales) = together(
-        two, [far, near_other, routes.T, route_weights.T]
-    )
-    block_a = jnp.stack([a, one[0], one[1], two[0]])
-    block_b = jnp.stack([b, one[2], one[3], two[1]])
+    block_a = jnp.stack([a, one[0], one[1], jnp.concatenate(two[:2])])
+    block_b = jnp.stack([b, one[2], one[3], jnp.concatenate(two[2:])])
     three = [
         along(block_a, "z", 1), along(block_a, "z", -1), along(block_b, "y", 1), along(block_b, "y", -1)
     ]

time: 202 us -> 201 us (level)
  waiting for transfers between devices: 69.1 us -> 62.9 us
  starting transfers between devices: 32.1 us -> 35.4 us
    ppermute x14 -> x16, waiting for transfers between devices: 52.9 us -> 44.6 us  [along(): return lax.ppermute(x, 'inner', ring(axis, step))]
    ppermute x14 -> x16, starting transfers between devices: 23.1 us -> 24 us  [along(): return lax.ppermute(x, 'inner', ring(axis, step))]
    unnamed x24 -> x22, local copies, waits for them, and re-layouts: 4.58 us -> 4.22 us
  transfers between devices with their start and end apart: 21 -> 23, of which waited for: 13 -> 14; matrix products, arithmetic and copies ran while one was open for 2% -> 2% of each run, Pallas kernels for 24% -> 24%
where the time goes in v3:
time: 201 us; the launch traced here: 200 us
  Pallas kernels  66.8 us (33%)
  waiting for transfers between devices  62.9 us (31%)
  starting transfers between devices  35.4 us (18%)
  between operations  14.3 us (7%)
  blocking collectives  10 us (5%)
  local copies, waits for them, and re-layouts  8.4 us (4%)
  other arithmetic  2.33 us (1%)
    ppermute x16, waiting for transfers between devices, along(): return lax.ppermute(x, 'inner', ring(axis, step))  44.6 us
    ppermute x16, starting transfers between devices, along(): return lax.ppermute(x, 'inner', ring(axis, step))  24 us
    pallas_call x1, Pallas kernels, most(): pl.pallas_call(most_kernel, grid_spec=pltpu.PrefetchScalarGridSpec(num_sc...  17.5 us
    pallas_call x1, Pallas kernels, whole(): pl.pallas_call(functools.partial(whole_kernel, tiles), grid=(2, tiles), i...  16.9 us
    pallas_call x1, Pallas kernels, last(): pl.pallas_call(functools.partial(last_kernel, first, tiles), grid_spec=pl...  13.8 us
    pallas_call x1, Pallas kernels, fill(): pl.pallas_call(functools.partial(fill_kernel, starts), grid_spec=pltpu.Pr...  12.5 us
    all_gather x1, waiting for transfers between devices, shards(): lax.all_gather(down_weight[:, :split], 'inner', axis=0, tiled=False)  11.8 us
    all_to_all x1, blocking collectives, shards(): lax.all_to_all(grads, 'outer', split_axis=0, concat_axis=0, tiled=True)  10 us
  transfers between devices with their start and end apart: 23, of which 14 were waited for; matrix products, arithmetic and copies ran while one was open for 2% of the time, Pallas kernels for 24%

profile of v3, /device:TPU:1, one launch (start us, length us, event | category | flops | bytes accessed | tf_op | source)
XLA Modules:
  0.0 200.1 jit_solution(11458308174299258400)
XLA Ops:
  10.8 2.4 %collective-permute-done = bf16[128,4096]{1,0:T(8,128)(2,1)S(1)} collective-permute-done((bf16[128,4096]{1,0:T(8,128)(2,1)}, bf16[128,4096]{1,0:T(8,128)(2,1)S(1)}, u32[]{:S(2)}, u32[]{:S(2)}) %collective-permute-start) | collective-permute-done | bytes 1048608 | tf_op jit(solution)/shard_map/ppermute | solution.py:42
  13.5 2.6 %collective-permute-start.5 = (bf16[2,128,4096]{2,1,0:T(8,128)(2,1)S(1)}, bf16[2,128,4096]{2,1,0:T(8,128)(2,1)}, u32[]{:S(2)}, u32[]{:S(2)}) collective-permute-start(bf16[2,128,4096]{2,1,0:T(8,128)(2,1)S(1)} %pad_maximum_fusion.refs_0_), channel_id=1, source_target_pairs={{0,32},{16,112},{32,64},{48,16},{64,96},{80,48},{96,0},{112,80},{1... | collective-permute-start | bytes 6291464 | tf_op jit(solution)/shard_map/ppermute | solution.py:38
  20.5 2.1 %collective-permute-start.4 = (bf16[1024,256]{1,0:T(8,128)(2,1)S(1)}, bf16[1024,256]{1,0:T(8,128)(2,1)S(1)}, u32[]{:S(2)}, u32[]{:S(2)}) collective-permute-start(bf16[1024,256]{1,0:T(8,128)(2,1)S(1)} %get-tuple-element.39), channel_id=1, source_target_pairs={{0,12},{1,13},{2,14},{3,15},{4,0},{5,1},{6,2},{7,3},{8,4},{9,5},{1... | collective-permute-start | bytes 1572872 | tf_op jit(solution)/shard_map/ppermute | solution.py:33
  22.6 12.1 %collective-permute-done.1 = bf16[1024,256]{1,0:T(8,128)(2,1)S(1)} collective-permute-done((bf16[1024,256]{1,0:T(8,128)(2,1)S(1)}, bf16[1024,256]{1,0:T(8,128)(2,1)S(1)}, u32[]{:S(2)}, u32[]{:S(2)}) %collective-permute-start.1) | collective-permute-done | bytes 524320 | tf_op jit(solution)/shard_map/ppermute | solution.py:33
  36.4 5.5 %collective-permute-done.3 = bf16[1024,256]{1,0:T(8,128)(2,1)S(1)} collective-permute-done((bf16[1024,256]{1,0:T(8,128)(2,1)S(1)}, bf16[1024,256]{1,0:T(8,128)(2,1)S(1)}, u32[]{:S(2)}, u32[]{:S(2)}) %collective-permute-start.3) | collective-permute-done | bytes 524320 | tf_op jit(solution)/shard_map/ppermute | solution.py:33
  44.0 3.8 %collective-permute-start.10 = (bf16[512,256]{1,0:T(8,128)(2,1)S(1)}, bf16[512,256]{1,0:T(8,128)(2,1)S(1)}, u32[]{:S(2)}, u32[]{:S(2)}) collective-permute-start(bf16[512,256]{1,0:T(8,128)(2,1)S(1)} %slice.29), channel_id=1, source_target_pairs={{0,12},{1,13},{2,14},{3,15},{4,0},{5,1},{6,2},{7,3},{8,4},{9,5},{1... | collective-permute-start | bytes 786440 | tf_op jit(solution)/shard_map/ppermute | solution.py:33
  50.8 5.9 %collective-permute-done.10 = bf16[512,256]{1,0:T(8,128)(2,1)S(1)} collective-permute-done((bf16[512,256]{1,0:T(8,128)(2,1)S(1)}, bf16[512,256]{1,0:T(8,128)(2,1)S(1)}, u32[]{:S(2)}, u32[]{:S(2)}) %collective-permute-start.10) | collective-permute-done | bytes 262176 | tf_op jit(solution)/shard_map/ppermute | solution.py:33
  56.7 3.3 %collective-permute-done.7 = bf16[512,256]{1,0:T(8,128)(2,1)S(1)} collective-permute-done((bf16[512,256]{1,0:T(8,128)(2,1)S(1)}, bf16[512,256]{1,0:T(8,128)(2,1)S(1)}, u32[]{:S(2)}, u32[]{:S(2)}) %collective-permute-start.7) | collective-permute-done | bytes 262176 | tf_op jit(solution)/shard_map/ppermute | solution.py:33
  62.0 3.2 %collective-permute-done.9 = bf16[512,256]{1,0:T(8,128)(2,1)S(1)} collective-permute-done((bf16[512,256]{1,0:T(8,128)(2,1)S(1)}, bf16[512,256]{1,0:T(8,128)(2,1)S(1)}, u32[]{:S(2)}, u32[]{:S(2)}) %collective-permute-start.9) | collective-permute-done | bytes 262176 | tf_op jit(solution)/shard_map/ppermute | solution.py:33
  65.2 2.1 %collective-permute-start.12 = (bf16[128,4096]{1,0:T(8,128)(2,1)S(1)}, bf16[128,4096]{1,0:T(8,128)(2,1)S(1)}, u32[]{:S(2)}, u32[]{:S(2)}) collective-permute-start(bf16[128,4096]{1,0:T(8,128)(2,1)S(1)} %collective-permute-done.11), channel_id=1, source_target_pairs={{0,16},{16,0},{32,48},{48,32},{64,80},{80,64},{96,112},{112,96},{1... | collective-permute-start | bytes 3145736 | tf_op jit(solution)/shard_map/ppermute | solution.py:42
  67.7 2.7 %collective-permute-start.16 = (bf16[4,1024,256]{2,1,0:T(8,128)(2,1)S(1)}, bf16[4,1024,256]{2,1,0:T(8,128)(2,1)}, u32[]{:S(2)}, u32[]{:S(2)}) collective-permute-start(bf16[4,1024,256]{2,1,0:T(8,128)(2,1)S(1)} %pad_maximum_fusion.2.rest_3_), channel_id=1, source_target_pairs={{0,3},{1,0},{2,1},{3,2},{4,7},{5,4},{6,5},{7,6},{8,11},{9,8},{10,9... | collective-permute-start | bytes 6291464 | tf_op jit(solution)/shard_map/ppermute | solution.py:33
  73.1 2.7 %collective-permute-start.14 = (bf16[4,1024,256]{2,1,0:T(8,128)(2,1)}, bf16[4,1024,256]{2,1,0:T(8,128)(2,1)}, u32[]{:S(2)}, u32[]{:S(2)}) collective-permute-start(bf16[4,1024,256]{2,1,0:T(8,128)(2,1)} %pad_maximum_fusion.1.rest_0_), channel_id=1, source_target_pairs={{0,12},{1,13},{2,14},{3,15},{4,0},{5,1},{6,2},{7,3},{8,4},{9,5},{1... | collective-permute-start | bytes 6291464 | tf_op jit(solution)/shard_map/ppermute | solution.py:33
  77.2 4.9 %all-to-all-start = ((f32[8,4,128]{2,1,0:T(4,128)}), f32[8,4,128]{2,1,0:T(4,128)S(1)}, u32[]{:S(2)}, u32[]{:S(2)}) async-start(f32[8,4,128]{2,1,0:T(4,128)} %plan.1), calls=%async_computation | async-start | bytes 32768 | tf_op jit(solution)/shard_map/all_to_all | solution.py:570
  82.7 4.1 %all-to-all-done.refs_5_.rest_13_ = f32[8,4,128]{2,1,0:T(4,128)S(1)} async-done(((f32[8,4,128]{2,1,0:T(4,128)}), f32[8,4,128]{2,1,0:T(4,128)S(1)}, u32[]{:S(2)}, u32[]{:S(2)}) %all-to-all-start) | async-done | bytes 16416 | tf_op jit(solution)/shard_map/all_to_all | solution.py:570
  87.4 12.5 %fill.1 = (bf16[2,8,96,4096]{3,2,1,0:T(8,128)(2,1)}, f32[2,8,96,128]{3,2,1,0:T(8,128)}) custom-call(s32[8]{0:T(128)} %stack.74.source_ref, bf16[2,128,4096]{2,1,0:T(8,128)(2,1)} %copy-done.5, bf16[2,128,4096]{2,1,0:T(8,128)(2,1)} %collective-permute-done.5.refs_1_, bf16[2,128,4096]{2,1,0:T(8,128)(2,1)} %collective-permute-done.6.refs_2_, ...), custom_call_target="tpu_custom_call" | custom-call | flops 1610612736 | bytes 20971520 | tf_op jit(solution)/shard_map/fill/pallas_call | solution.py:137
  99.9 11.8 %all-gather.3.cloned.1.call-done = bf16[32,512,256]{2,1,0:T(8,128)(2,1)} async-done(((bf16[2,512,256]{2,1,0:T(8,128)(2,1)}), bf16[32,512,256]{2,1,0:T(8,128)(2,1)}) %all-gather.3.cloned.1.call-update) | async-done | bytes 8388624 | tf_op jit(solution)/shard_map/all_gather | solution.py:547
  111.7 16.9 %whole.1 = (bf16[8,2,1,96,3072]{4,3,2,1,0:T(8,128)(2,1)}, f32[2,768,128]{2,1,0:T(8,128)}) custom-call(bf16[2,768,4096]{2,1,0:T(8,128)(2,1)} %bitcast.36, bf16[16,2,512,256]{3,2,1,0:T(8,128)(2,1)} %bitcast.42, bf16[8,2,1,96,3072]{4,3,2,1,0:T(8,128)(2,1)} %rest_9_.1, bf16[8,2,1,96,3072]{4,3,2,1,0:T(8,128)(2,1)} %rest_9_.1, f32[2,768,128]{2,1,0:T(8,128)} %bitcast.34), custom_call_target="tpu_custom_call" | custom-call | flops 6442450944 | bytes 27262976 | tf_op jit(solution)/shard_map/whole/pallas_call | solution.py:296
  128.7 7.2 %collective-permute-done.15.refs_2_.rest_4_ = bf16[4,1024,256]{2,1,0:T(8,128)(2,1)} collective-permute-done((bf16[4,1024,256]{2,1,0:T(8,128)(2,1)S(1)}, bf16[4,1024,256]{2,1,0:T(8,128)(2,1)}, u32[]{:S(2)}, u32[]{:S(2)}) %collective-permute-start.15) | collective-permute-done | bytes 2097184 | tf_op jit(solution)/shard_map/ppermute | solution.py:33
  137.3 3.3 %halves.1 = (bf16[2,1024,256]{2,1,0:T(8,128)(2,1)}, bf16[2,1024,256]{2,1,0:T(8,128)(2,1)}, bf16[2,1024,256]{2,1,0:T(8,128)(2,1)}, bf16[2,1024,256]{2,1,0:T(8,128)(2,1)}) custom-call(bf16[4,1024,256]{2,1,0:T(8,128)(2,1)} %collective-permute-done.13.refs_0_.rest_1_, bf16[4,1024,256]{2,1,0:T(8,128)(2,1)} %collective-permute-done.14.refs_1_.rest_2_, ...), custom_call_target="tpu_custom_call" | custom-call | tf_op jit(solution)/shard_map/halves/pallas_call | solution.py:526
  140.7 2.7 %collective-permute-start.18 = (bf16[2,1024,256]{2,1,0:T(8,128)(2,1)}, bf16[2,1024,256]{2,1,0:T(8,128)(2,1)}, u32[]{:S(2)}, u32[]{:S(2)}) collective-permute-start(bf16[2,1024,256]{2,1,0:T(8,128)(2,1)} %get-tuple-element.61), channel_id=1, source_target_pairs={{0,12},{1,13},{2,14},{3,15},{4,0},{5,1},{6,2},{7,3},{8,4},{9,5},{1... | collective-permute-start | bytes 3145736 | tf_op jit(solution)/shard_map/ppermute | solution.py:33
  146.4 17.5 %most.1.rest_11_ = f32[2,768,1024]{2,1,0:T(8,128)S(1)} custom-call(s32[32]{0:T(128)S(1)} %pad_add_fusion.order_ref, bf16[2,768,4096]{2,1,0:T(8,128)(2,1)} %bitcast.37, bf16[4,1024,256]{2,1,0:T(8,128)(2,1)} %pad_maximum_fusion.1.rest_0_, bf16[4,1024,256]{2,1,0:T(8,128)(2,1)} %collective-permute-done.13.refs_0_.rest_1_, ...), custom_call_target="tpu_custom_call" | custom-call | flops 9663676416 | bytes 35651584 | tf_op jit(solution)/shard_map/most/pallas_call | solution.py:375
  163.9 2.6 %copy-done = f32[2,768,1024]{2,1,0:T(8,128)} copy-done((f32[2,768,1024]{2,1,0:T(8,128)}, f32[2,768,1024]{2,1,0:T(8,128)S(1)}, u32[]{:S(2)}) %copy-start) | copy-done | bytes 6291480
  168.1 13.8 %last.1 = (bf16[8,2,1,96,3072]{4,3,2,1,0:T(8,128)(2,1)}, f32[8,2,128]{2,1,0:T(2,128)S(1)}) custom-call(s32[32]{0:T(128)S(1)} %pad_add_fusion.order_ref, bf16[2,768,4096]{2,1,0:T(8,128)(2,1)} %bitcast.38, bf16[2,768,4096]{2,1,0:T(8,128)(2,1)} %bitcast.39, bf16[2,768,4096]{2,1,0:T(8,128)(2,1)} %bitcast.40, ...), custom_call_target="tpu_custom_call", output_to_operand_aliasing={{0}: (15, {})} | custom-call | flops 3221225472 | bytes 33554432 | tf_op jit(solution)/shard_map/last/pallas_call | solution.py:457
  181.9 10.0 %all_to_all.10.grads_ref = f32[8,2,128]{2,1,0:T(2,128)} all-to-all(f32[8,2,128]{2,1,0:T(2,128)S(1)} %get-tuple-element.71), channel_id=1, replica_groups=mesh['outer'=8,'inner'=16] {'outer'}, dimensions={0} | all-to-all | bytes 16384 | tf_op jit(solution)/shard_map/all_to_all | solution.py:603
  (71 shorter events, 30.1 us)
Async XLA Ops:
  7.2 104.5 %all-gather.3.cloned.1.call-start = ((), (), s32[]{:S(2)}) async-start(), calls=%async_computation.2 | async-start | bytes 8912896 | tf_op jit(solution)/shard_map/all_gather | solution.py:547
  9.3 4.0 %collective-permute-start = (bf16[128,4096]{1,0:T(8,128)(2,1)}, bf16[128,4096]{1,0:T(8,128)(2,1)S(1)}, u32[]{:S(2)}, u32[]{:S(2)}) collective-permute-start(bf16[128,4096]{1,0:T(8,128)(2,1)} %param.6), channel_id=1, source_target_pairs={{0,16},{16,0},{32,48},{48,32},{64,80},{80,64},{96,112},{112,96},{1... | collective-permute-start | bytes 3145736 | tf_op jit(solution)/shard_map/ppermute | solution.py:42
  13.5 37.2 %copy-start.5 = (bf16[2,128,4096]{2,1,0:T(8,128)(2,1)}, bf16[2,128,4096]{2,1,0:T(8,128)(2,1)S(1)}, u32[]{:S(2)}) copy-start(bf16[2,128,4096]{2,1,0:T(8,128)(2,1)S(1)} %pad_maximum_fusion.refs_0_) | copy-start | bytes 6291460
  13.5 29.0 %collective-permute-start.5 = (bf16[2,128,4096]{2,1,0:T(8,128)(2,1)S(1)}, bf16[2,128,4096]{2,1,0:T(8,128)(2,1)}, u32[]{:S(2)}, u32[]{:S(2)}) collective-permute-start(bf16[2,128,4096]{2,1,0:T(8,128)(2,1)S(1)} %pad_maximum_fusion.refs_0_), channel_id=1, source_target_pairs={{0,32},{16,112},{32,64},{48,16},{64,96},{80,48},{96,0},{112,80},{1... | collective-permute-start | bytes 6291464 | tf_op jit(solution)/shard_map/ppermute | solution.py:38
  16.1 18.6 %collective-permute-start.1 = (bf16[1024,256]{1,0:T(8,128)(2,1)S(1)}, bf16[1024,256]{1,0:T(8,128)(2,1)S(1)}, u32[]{:S(2)}, u32[]{:S(2)}) collective-permute-start(bf16[1024,256]{1,0:T(8,128)(2,1)S(1)} %get-tuple-element.38), channel_id=1, source_target_pairs={{0,1},{1,2},{2,3},{3,0},{4,5},{5,6},{6,7},{7,4},{8,9},{9,10},{10,1... | collective-permute-start | bytes 1572872 | tf_op jit(solution)/shard_map/ppermute | solution.py:33
  17.4 18.9 %collective-permute-start.2 = (bf16[1024,256]{1,0:T(8,128)(2,1)S(1)}, bf16[1024,256]{1,0:T(8,128)(2,1)S(1)}, u32[]{:S(2)}, u32[]{:S(2)}) collective-permute-start(bf16[1024,256]{1,0:T(8,128)(2,1)S(1)} %get-tuple-element.38), channel_id=1, source_target_pairs={{0,3},{1,0},{2,1},{3,2},{4,7},{5,4},{6,5},{7,6},{8,11},{9,8},{10,9... | collective-permute-start | bytes 1572872 | tf_op jit(solution)/shard_map/ppermute | solution.py:33
  18.8 23.0 %collective-permute-start.3 = (bf16[1024,256]{1,0:T(8,128)(2,1)S(1)}, bf16[1024,256]{1,0:T(8,128)(2,1)S(1)}, u32[]{:S(2)}, u32[]{:S(2)}) collective-permute-start(bf16[1024,256]{1,0:T(8,128)(2,1)S(1)} %get-tuple-element.39), channel_id=1, source_target_pairs={{0,4},{1,5},{2,6},{3,7},{4,8},{5,9},{6,10},{7,11},{8,12},{9,13},{1... | collective-permute-start | bytes 1572872 | tf_op jit(solution)/shard_map/ppermute | solution.py:33
  20.5 22.0 %collective-permute-start.4 = (bf16[1024,256]{1,0:T(8,128)(2,1)S(1)}, bf16[1024,256]{1,0:T(8,128)(2,1)S(1)}, u32[]{:S(2)}, u32[]{:S(2)}) collective-permute-start(bf16[1024,256]{1,0:T(8,128)(2,1)S(1)} %get-tuple-element.39), channel_id=1, source_target_pairs={{0,12},{1,13},{2,14},{3,15},{4,0},{5,1},{6,2},{7,3},{8,4},{9,5},{1... | collective-permute-start | bytes 1572872 | tf_op jit(solution)/shard_map/ppermute | solution.py:33
  43.8 21.4 %collective-permute-start.11 = (bf16[128,4096]{1,0:T(8,128)(2,1)S(1)}, bf16[128,4096]{1,0:T(8,128)(2,1)S(1)}, u32[]{:S(2)}, u32[]{:S(2)}) collective-permute-start(bf16[128,4096]{1,0:T(8,128)(2,1)S(1)} %slice_bitcast_fusion), channel_id=1, source_target_pairs={{0,32},{16,112},{32,64},{48,16},{64,96},{80,48},{96,0},{112,80},{1... | collective-permute-start | bytes 3145736 | tf_op jit(solution)/shard_map/ppermute | solution.py:38
  44.0 12.7 %collective-permute-start.10 = (bf16[512,256]{1,0:T(8,128)(2,1)S(1)}, bf16[512,256]{1,0:T(8,128)(2,1)S(1)}, u32[]{:S(2)}, u32[]{:S(2)}) collective-permute-start(bf16[512,256]{1,0:T(8,128)(2,1)S(1)} %slice.29), channel_id=1, source_target_pairs={{0,12},{1,13},{2,14},{3,15},{4,0},{5,1},{6,2},{7,3},{8,4},{9,5},{1... | collective-permute-start | bytes 786440 | tf_op jit(solution)/shard_map/ppermute | solution.py:33
  47.8 12.2 %collective-permute-start.7 = (bf16[512,256]{1,0:T(8,128)(2,1)S(1)}, bf16[512,256]{1,0:T(8,128)(2,1)S(1)}, u32[]{:S(2)}, u32[]{:S(2)}) collective-permute-start(bf16[512,256]{1,0:T(8,128)(2,1)S(1)} %slice.26), channel_id=1, source_target_pairs={{0,1},{1,2},{2,3},{3,0},{4,5},{5,6},{6,7},{7,4},{8,9},{9,10},{10,1... | collective-permute-start | bytes 786440 | tf_op jit(solution)/shard_map/ppermute | solution.py:33
  48.9 13.1 %collective-permute-start.8 = (bf16[512,256]{1,0:T(8,128)(2,1)S(1)}, bf16[512,256]{1,0:T(8,128)(2,1)S(1)}, u32[]{:S(2)}, u32[]{:S(2)}) collective-permute-start(bf16[512,256]{1,0:T(8,128)(2,1)S(1)} %slice.27), channel_id=1, source_target_pairs={{0,3},{1,0},{2,1},{3,2},{4,7},{5,4},{6,5},{7,6},{8,11},{9,8},{10,9... | collective-permute-start | bytes 786440 | tf_op jit(solution)/shard_map/ppermute | solution.py:33
  50.7 14.5 %collective-permute-start.9 = (bf16[512,256]{1,0:T(8,128)(2,1)S(1)}, bf16[512,256]{1,0:T(8,128)(2,1)S(1)}, u32[]{:S(2)}, u32[]{:S(2)}) collective-permute-start(bf16[512,256]{1,0:T(8,128)(2,1)S(1)} %slice.28), channel_id=1, source_target_pairs={{0,4},{1,5},{2,6},{3,7},{4,8},{5,9},{6,10},{7,11},{8,12},{9,13},{1... | collective-permute-start | bytes 786440 | tf_op jit(solution)/shard_map/ppermute | solution.py:33
  65.2 6.9 %collective-permute-start.12 = (bf16[128,4096]{1,0:T(8,128)(2,1)S(1)}, bf16[128,4096]{1,0:T(8,128)(2,1)S(1)}, u32[]{:S(2)}, u32[]{:S(2)}) collective-permute-start(bf16[128,4096]{1,0:T(8,128)(2,1)S(1)} %collective-permute-done.11), channel_id=1, source_target_pairs={{0,16},{16,0},{32,48},{48,32},{64,80},{80,64},{96,112},{112,96},{1... | collective-permute-start | bytes 3145736 | tf_op jit(solution)/shard_map/ppermute | solution.py:42
  67.2 19.6 %collective-permute-start.6 = (bf16[2,128,4096]{2,1,0:T(8,128)(2,1)}, bf16[2,128,4096]{2,1,0:T(8,128)(2,1)}, u32[]{:S(2)}, u32[]{:S(2)}) collective-permute-start(bf16[2,128,4096]{2,1,0:T(8,128)(2,1)} %collective-permute-done.5.refs_1_), channel_id=1, source_target_pairs={{0,16},{16,0},{32,48},{48,32},{64,80},{80,64},{96,112},{112,96},{1... | collective-permute-start | bytes 6291464 | tf_op jit(solution)/shard_map/ppermute | solution.py:42
  67.7 68.2 %collective-permute-start.15 = (bf16[4,1024,256]{2,1,0:T(8,128)(2,1)S(1)}, bf16[4,1024,256]{2,1,0:T(8,128)(2,1)}, u32[]{:S(2)}, u32[]{:S(2)}) collective-permute-start(bf16[4,1024,256]{2,1,0:T(8,128)(2,1)S(1)} %pad_maximum_fusion.2.rest_3_), channel_id=1, source_target_pairs={{0,1},{1,2},{2,3},{3,0},{4,5},{5,6},{6,7},{7,4},{8,9},{9,10},{10,1... | collective-permute-start | bytes 6291464 | tf_op jit(solution)/shard_map/ppermute | solution.py:33
  67.7 68.1 %collective-permute-start.16 = (bf16[4,1024,256]{2,1,0:T(8,128)(2,1)S(1)}, bf16[4,1024,256]{2,1,0:T(8,128)(2,1)}, u32[]{:S(2)}, u32[]{:S(2)}) collective-permute-start(bf16[4,1024,256]{2,1,0:T(8,128)(2,1)S(1)} %pad_maximum_fusion.2.rest_3_), channel_id=1, source_target_pairs={{0,3},{1,0},{2,1},{3,2},{4,7},{5,4},{6,5},{7,6},{8,11},{9,8},{10,9... | collective-permute-start | bytes 6291464 | tf_op jit(solution)/shard_map/ppermute | solution.py:33
  72.1 65.2 %collective-permute-start.13 = (bf16[4,1024,256]{2,1,0:T(8,128)(2,1)}, bf16[4,1024,256]{2,1,0:T(8,128)(2,1)}, u32[]{:S(2)}, u32[]{:S(2)}) collective-permute-start(bf16[4,1024,256]{2,1,0:T(8,128)(2,1)} %pad_maximum_fusion.1.rest_0_), channel_id=1, source_target_pairs={{0,4},{1,5},{2,6},{3,7},{4,8},{5,9},{6,10},{7,11},{8,12},{9,13},{1... | collective-permute-start | bytes 6291464 | tf_op jit(solution)/shard_map/ppermute | solution.py:33
  73.1 64.3 %collective-permute-start.14 = (bf16[4,1024,256]{2,1,0:T(8,128)(2,1)}, bf16[4,1024,256]{2,1,0:T(8,128)(2,1)}, u32[]{:S(2)}, u32[]{:S(2)}) collective-permute-start(bf16[4,1024,256]{2,1,0:T(8,128)(2,1)} %pad_maximum_fusion.1.rest_0_), channel_id=1, source_target_pairs={{0,12},{1,13},{2,14},{3,15},{4,0},{5,1},{6,2},{7,3},{8,4},{9,5},{1... | collective-permute-start | bytes 6291464 | tf_op jit(solution)/shard_map/ppermute | solution.py:33
  77.2 9.6 %all-to-all-start = ((f32[8,4,128]{2,1,0:T(4,128)}), f32[8,4,128]{2,1,0:T(4,128)S(1)}, u32[]{:S(2)}, u32[]{:S(2)}) async-start(f32[8,4,128]{2,1,0:T(4,128)} %plan.1), calls=%async_computation | async-start | bytes 32768 | tf_op jit(solution)/shard_map/all_to_all | solution.py:570
  140.7 25.9 %collective-permute-start.17 = (bf16[2,1024,256]{2,1,0:T(8,128)(2,1)}, bf16[2,1024,256]{2,1,0:T(8,128)(2,1)S(1)}, u32[]{:S(2)}, u32[]{:S(2)}) collective-permute-start(bf16[2,1024,256]{2,1,0:T(8,128)(2,1)} %get-tuple-element.60), channel_id=1, source_target_pairs={{0,4},{1,5},{2,6},{3,7},{4,8},{5,9},{6,10},{7,11},{8,12},{9,13},{1... | collective-permute-start | bytes 3145736 | tf_op jit(solution)/shard_map/ppermute | solution.py:33
  140.7 25.8 %collective-permute-start.18 = (bf16[2,1024,256]{2,1,0:T(8,128)(2,1)}, bf16[2,1024,256]{2,1,0:T(8,128)(2,1)}, u32[]{:S(2)}, u32[]{:S(2)}) collective-permute-start(bf16[2,1024,256]{2,1,0:T(8,128)(2,1)} %get-tuple-element.61), channel_id=1, source_target_pairs={{0,12},{1,13},{2,14},{3,15},{4,0},{5,1},{6,2},{7,3},{8,4},{9,5},{1... | collective-permute-start | bytes 3145736 | tf_op jit(solution)/shard_map/ppermute | solution.py:33
  143.4 24.7 %collective-permute-start.19 = (bf16[2,1024,256]{2,1,0:T(8,128)(2,1)}, bf16[2,1024,256]{2,1,0:T(8,128)(2,1)}, u32[]{:S(2)}, u32[]{:S(2)}) collective-permute-start(bf16[2,1024,256]{2,1,0:T(8,128)(2,1)} %get-tuple-element.62), channel_id=1, source_target_pairs={{0,1},{1,2},{2,3},{3,0},{4,5},{5,6},{6,7},{7,4},{8,9},{9,10},{10,1... | collective-permute-start | bytes 3145736 | tf_op jit(solution)/shard_map/ppermute | solution.py:33
  144.5 23.6 %collective-permute-start.20 = (bf16[2,1024,256]{2,1,0:T(8,128)(2,1)}, bf16[2,1024,256]{2,1,0:T(8,128)(2,1)}, u32[]{:S(2)}, u32[]{:S(2)}) collective-permute-start(bf16[2,1024,256]{2,1,0:T(8,128)(2,1)} %get-tuple-element.63), channel_id=1, source_target_pairs={{0,3},{1,0},{2,1},{3,2},{4,7},{5,4},{6,5},{7,6},{8,11},{9,8},{10,9... | collective-permute-start | bytes 3145736 | tf_op jit(solution)/shard_map/ppermute | solution.py:33
  (10 other events, 93.2 us)
Sparse Core Ops, SparseCore 0:
  10.2 101.5 all-gather.2

commit v4 on v3

--- a/solution.py
+++ b/solution.py
@@ -547,38 +547,34 @@
     gathered = lax.all_gather(down_weight[:, :split], "inner", axis=0, tiled=False)
 
     a, b = down_weight[0, split:], down_weight[1, split:]
-    pair = jnp.stack([grad_out, other_core(grad_out)])
-    pair, (a, b) = lax.optimization_barrier((pair, (a, b)))
     one = [along(a, "y", 1), along(a, "y", -1), along(b, "z", 1), along(b, "z", -1)]
-    near = along_x(pair)
-    one, (near,) = together(one, [near])
+    one, (next_one,) = together(one, [along_x(grad_out)])
     cut = a.shape[0] // 2
     two = [
         along(one[0][:cut], "y", 1), along(one[1][cut:], "y", -1),
         along(one[2][:cut], "z", 1), along(one[3][cut:], "z", -1),
     ]
-    far = along_x(near[0])
-    two, (far, named, scales) = together(two, [far, routes.T, route_weights.T])
-    near_other = other_core(near)
+    two, (next_two, named, scales) = together(
+        two, [along_x(next_one), routes.T, route_weights.T]
+    )
     block_a = jnp.stack([a, one[0], one[1], jnp.concatenate(two[:2])])
     block_b = jnp.stack([b, one[2], one[3], jnp.concatenate(two[2:])])
     three = [
         along(block_a, "z", 1), along(block_a, "z", -1), along(block_b, "y", 1), along(block_b, "y", -1)
     ]
 
-    far_other = other_core(far)
+    near = jnp.stack([grad_out, next_one, next_two])
+    last_one = along_x(next_two)[None]
+    near_other, last_other = other_core(near), other_core(last_one)
     plans = lax.all_to_all(
         plan(named, scales, n_outer), "outer", split_axis=0, concat_axis=0, tiled=True
     )
-    came, went = (x + 2 * core - 1) % 4, (x + 1 - 2 * core) % 4
-    opposite = (x + 2) % 4
+    back = 2 * core - 1
     source = jnp.stack(
-        [
-            2 * x + core, 2 * x + 1 - core, 2 * came + core, 2 * came + 1 - core,
-            2 * went + 1 - core, 2 * went + core, 2 * opposite + core, 2 * opposite + 1 - core,
-        ]
-    )
-    filled = fill(source, [pair, near, near_other, far[None], far_other[None]], plans, cap)
+        [((x + n * back) % 4) * 2 + core for n in range(4)]
+        + [((x - n * back) % 4) * 2 + 1 - core for n in range(4)]
+    )
+    filled = fill(source, [near, last_one, near_other, last_other], plans, cap)
     rows = filled[0].reshape(2, n_outer * cap, grad_out.shape[1])
     weights = filled[1].reshape(2, n_outer * cap, 128)
     out, sums = whole(rows, gathered, saved_gate_up, weights)

time: 201 us -> 195 us (0.970)
  waiting for transfers between devices: 62.9 us -> 50 us
  starting transfers between devices: 35.4 us -> 42.1 us
    all_gather x1, waiting for transfers between devices: 11.8 us -> 0.01 us  [shards(): lax.all_gather(down_weight[:, :split], 'inner', axis=0, tiled=False)]
    ppermute x2 -> x3, waiting for transfers between devices: 0.01 us -> 11.3 us  [along_x(): return lax.ppermute(x, 'outer', pairs)]
    ppermute x16, waiting for transfers between devices: 44.6 us -> 34.7 us  [along(): return lax.ppermute(x, 'inner', ring(axis, step))]
    ppermute x3 -> x2, starting transfers between devices: 3.64 us -> 8.17 us  [other_core(): return lax.ppermute(x, 'outer', [(i, i ^ 1) for i in range(8)])]
    ppermute x3 -> x2, waiting for transfers between devices: 2.43 us -> 0.01 us  [other_core(): return lax.ppermute(x, 'outer', [(i, i ^ 1) for i in range(8)])]
    ppermute x2 -> x3, starting transfers between devices: 2.78 us -> 4.59 us  [along_x(): return lax.ppermute(x, 'outer', pairs)]
    unnamed x22 -> x20, local copies, waits for them, and re-layouts: 4.22 us -> 4.23 us
  transfers between devices with their start and end apart: 23 -> 23, of which waited for: 14 -> 11; matrix products, arithmetic and copies ran while one was open for 2% -> 3% of each run, Pallas kernels for 24% -> 25%
where the time goes in v4:
time: 195 us
  Pallas kernels  66.3 us (34%)
  waiting for transfers between devices  50 us (26%)
  starting transfers between devices  42.1 us (22%)
  between operations  14.3 us (7%)
  blocking collectives  10.9 us (6%)
  local copies, waits for them, and re-layouts  7.27 us (4%)
  other arithmetic  4.13 us (2%)
    ppermute x16, waiting for transfers between devices, along(): return lax.ppermute(x, 'inner', ring(axis, step))  34.7 us
    ppermute x16, starting transfers between devices, along(): return lax.ppermute(x, 'inner', ring(axis, step))  24.8 us
    pallas_call x1, Pallas kernels, most(): pl.pallas_call(most_kernel, grid_spec=pltpu.PrefetchScalarGridSpec(num_sc...  17.4 us
    pallas_call x1, Pallas kernels, whole(): pl.pallas_call(functools.partial(whole_kernel, tiles), grid=(2, tiles), i...  16.9 us
    pallas_call x1, Pallas kernels, last(): pl.pallas_call(functools.partial(last_kernel, first, tiles), grid_spec=pl...  13.8 us
    pallas_call x1, Pallas kernels, fill(): pl.pallas_call(functools.partial(fill_kernel, starts), grid_spec=pltpu.Pr...  12.1 us
    ppermute x3, waiting for transfers between devices, along_x(): return lax.ppermute(x, 'outer', pairs)  11.3 us
    all_to_all x1, blocking collectives, shards(): lax.all_to_all(grads, 'outer', split_axis=0, concat_axis=0, tiled=True)  10.9 us
  transfers between devices with their start and end apart: 23, of which 11 were waited for; matrix products, arithmetic and copies ran while one was open for 3% of the time, Pallas kernels for 25%

profile of v4, /device:TPU:1, one launch (start us, length us, event | category | flops | bytes accessed | tf_op | source)
XLA Modules:
  0.0 195.0 jit_solution(17040267691327625290)
XLA Ops:
  9.2 3.4 %collective-permute-start.4 = (bf16[128,4096]{1,0:T(8,128)(2,1)}, bf16[128,4096]{1,0:T(8,128)(2,1)S(1)}, u32[]{:S(2)}, u32[]{:S(2)}) collective-permute-start(bf16[128,4096]{1,0:T(8,128)(2,1)} %param.6), channel_id=1, source_target_pairs={{0,32},{16,112},{32,64},{48,16},{64,96},{80,48},{96,0},{112,80},{1... | collective-permute-start | bytes 3145736 | tf_op jit(solution)/shard_map/ppermute | solution.py:38
  17.3 2.1 %collective-permute-start.3 = (bf16[1024,256]{1,0:T(8,128)(2,1)S(1)}, bf16[1024,256]{1,0:T(8,128)(2,1)S(1)}, u32[]{:S(2)}, u32[]{:S(2)}) collective-permute-start(bf16[1024,256]{1,0:T(8,128)(2,1)S(1)} %get-tuple-element.68), channel_id=1, source_target_pairs={{0,12},{1,13},{2,14},{3,15},{4,0},{5,1},{6,2},{7,3},{8,4},{9,5},{1... | collective-permute-start | bytes 1572872 | tf_op jit(solution)/shard_map/ppermute | solution.py:33
  19.4 8.6 %collective-permute-done = bf16[1024,256]{1,0:T(8,128)(2,1)S(1)} collective-permute-done((bf16[1024,256]{1,0:T(8,128)(2,1)S(1)}, bf16[1024,256]{1,0:T(8,128)(2,1)S(1)}, u32[]{:S(2)}, u32[]{:S(2)}) %collective-permute-start) | collective-permute-done | bytes 524320 | tf_op jit(solution)/shard_map/ppermute | solution.py:33
  29.7 5.3 %collective-permute-done.2 = bf16[1024,256]{1,0:T(8,128)(2,1)S(1)} collective-permute-done((bf16[1024,256]{1,0:T(8,128)(2,1)S(1)}, bf16[1024,256]{1,0:T(8,128)(2,1)S(1)}, u32[]{:S(2)}, u32[]{:S(2)}) %collective-permute-start.2) | collective-permute-done | bytes 524320 | tf_op jit(solution)/shard_map/ppermute | solution.py:33
  36.5 2.7 %collective-permute-start.6 = (bf16[512,256]{1,0:T(8,128)(2,1)S(1)}, bf16[512,256]{1,0:T(8,128)(2,1)S(1)}, u32[]{:S(2)}, u32[]{:S(2)}) collective-permute-start(bf16[512,256]{1,0:T(8,128)(2,1)S(1)} %slice.24), channel_id=1, source_target_pairs={{0,3},{1,0},{2,1},{3,2},{4,7},{5,4},{6,5},{7,6},{8,11},{9,8},{10,9... | collective-permute-start | bytes 786440 | tf_op jit(solution)/shard_map/ppermute | solution.py:33
  39.4 3.6 %collective-permute-start.8 = (bf16[512,256]{1,0:T(8,128)(2,1)S(1)}, bf16[512,256]{1,0:T(8,128)(2,1)S(1)}, u32[]{:S(2)}, u32[]{:S(2)}) collective-permute-start(bf16[512,256]{1,0:T(8,128)(2,1)S(1)} %slice.26), channel_id=1, source_target_pairs={{0,12},{1,13},{2,14},{3,15},{4,0},{5,1},{6,2},{7,3},{8,4},{9,5},{1... | collective-permute-start | bytes 786440 | tf_op jit(solution)/shard_map/ppermute | solution.py:33
  44.5 2.8 %collective-permute-done.7 = bf16[512,256]{1,0:T(8,128)(2,1)S(1)} collective-permute-done((bf16[512,256]{1,0:T(8,128)(2,1)S(1)}, bf16[512,256]{1,0:T(8,128)(2,1)S(1)}, u32[]{:S(2)}, u32[]{:S(2)}) %collective-permute-start.7) | collective-permute-done | bytes 262176 | tf_op jit(solution)/shard_map/ppermute | solution.py:33
  47.3 3.0 %collective-permute-done.9 = bf16[128,4096]{1,0:T(8,128)(2,1)S(1)} collective-permute-done((bf16[128,4096]{1,0:T(8,128)(2,1)S(1)}, bf16[128,4096]{1,0:T(8,128)(2,1)S(1)}, u32[]{:S(2)}, u32[]{:S(2)}) %collective-permute-start.9) | collective-permute-done | bytes 1048608 | tf_op jit(solution)/shard_map/ppermute | solution.py:38
  51.5 2.0 %pad_maximum_fusion.refs_0_ = bf16[3,128,4096]{2,1,0:T(8,128)(2,1)} fusion(bf16[1,128,4096]{2,1,0:T(8,128)(2,1)S(1)} %bitcast.47, bf16[1,128,4096]{2,1,0:T(8,128)(2,1)S(1)} %bitcast.46, bf16[1,128,4096]{2,1,0:T(8,128)(2,1)S(1)} %bitcast.45), kind=kLoop, calls=%fused_computation | loop fusion | flops 3145728 | bytes 6291456 | tf_op jit(solution)/shard_map/stack | solution.py:566
  53.5 2.5 %collective-permute-start.11 = (bf16[3,128,4096]{2,1,0:T(8,128)(2,1)}, bf16[3,128,4096]{2,1,0:T(8,128)(2,1)}, u32[]{:S(2)}, u32[]{:S(2)}) collective-permute-start(bf16[3,128,4096]{2,1,0:T(8,128)(2,1)} %pad_maximum_fusion.refs_0_), channel_id=1, source_target_pairs={{0,16},{16,0},{32,48},{48,32},{64,80},{80,64},{96,112},{112,96},{1... | collective-permute-start | bytes 9437192 | tf_op jit(solution)/shard_map/ppermute | solution.py:42
  56.0 8.3 %collective-permute-done.10 = bf16[128,4096]{1,0:T(8,128)(2,1)S(1)} collective-permute-done((bf16[128,4096]{1,0:T(8,128)(2,1)S(1)}, bf16[128,4096]{1,0:T(8,128)(2,1)S(1)}, u32[]{:S(2)}, u32[]{:S(2)}) %collective-permute-start.10) | collective-permute-done | bytes 1048608 | tf_op jit(solution)/shard_map/ppermute | solution.py:38
  64.4 5.7 %collective-permute-start.12 = (bf16[1,128,4096]{2,1,0:T(8,128)(2,1)S(1)}, bf16[1,128,4096]{2,1,0:T(8,128)(2,1)S(1)}, u32[]{:S(2)}, u32[]{:S(2)}) collective-permute-start(bf16[1,128,4096]{2,1,0:T(8,128)(2,1)S(1)} %bitcast.43), channel_id=1, source_target_pairs={{0,16},{16,0},{32,48},{48,32},{64,80},{80,64},{96,112},{112,96},{1... | collective-permute-start | bytes 3145736 | tf_op jit(solution)/shard_map/ppermute | solution.py:42
  71.1 2.8 %collective-permute-start.14 = (bf16[4,1024,256]{2,1,0:T(8,128)(2,1)S(1)}, bf16[4,1024,256]{2,1,0:T(8,128)(2,1)}, u32[]{:S(2)}, u32[]{:S(2)}) collective-permute-start(bf16[4,1024,256]{2,1,0:T(8,128)(2,1)S(1)} %pad_maximum_fusion.1.rest_0_), channel_id=1, source_target_pairs={{0,12},{1,13},{2,14},{3,15},{4,0},{5,1},{6,2},{7,3},{8,4},{9,5},{1... | collective-permute-start | bytes 6291464 | tf_op jit(solution)/shard_map/ppermute | solution.py:33
  76.6 2.7 %collective-permute-start.16 = (bf16[4,1024,256]{2,1,0:T(8,128)(2,1)}, bf16[4,1024,256]{2,1,0:T(8,128)(2,1)}, u32[]{:S(2)}, u32[]{:S(2)}) collective-permute-start(bf16[4,1024,256]{2,1,0:T(8,128)(2,1)} %pad_maximum_fusion.2.rest_3_), channel_id=1, source_target_pairs={{0,3},{1,0},{2,1},{3,2},{4,7},{5,4},{6,5},{7,6},{8,11},{9,8},{10,9... | collective-permute-start | bytes 6291464 | tf_op jit(solution)/shard_map/ppermute | solution.py:33
  80.7 4.5 %all-to-all-start = ((f32[8,4,128]{2,1,0:T(4,128)}), f32[8,4,128]{2,1,0:T(4,128)S(1)}, u32[]{:S(2)}, u32[]{:S(2)}) async-start(f32[8,4,128]{2,1,0:T(4,128)} %plan.1), calls=%async_computation | async-start | bytes 32768 | tf_op jit(solution)/shard_map/all_to_all | solution.py:569
  86.0 3.9 %all-to-all-done.refs_4_.rest_13_ = f32[8,4,128]{2,1,0:T(4,128)S(1)} async-done(((f32[8,4,128]{2,1,0:T(4,128)}), f32[8,4,128]{2,1,0:T(4,128)S(1)}, u32[]{:S(2)}, u32[]{:S(2)}) %all-to-all-start) | async-done | bytes 16416 | tf_op jit(solution)/shard_map/all_to_all | solution.py:569
  90.5 12.1 %fill.1 = (bf16[2,8,96,4096]{3,2,1,0:T(8,128)(2,1)}, f32[2,8,96,128]{3,2,1,0:T(8,128)}) custom-call(s32[8]{0:T(128)} %stack.71.source_ref, bf16[3,128,4096]{2,1,0:T(8,128)(2,1)} %pad_maximum_fusion.refs_0_, bf16[1,128,4096]{2,1,0:T(8,128)(2,1)} %bitcast.44, bf16[3,128,4096]{2,1,0:T(8,128)(2,1)} %collective-permute-done.11.refs_2_, ...), custom_call_target="tpu_custom_call" | custom-call | flops 1610612736 | bytes 20971520 | tf_op jit(solution)/shard_map/fill/pallas_call | solution.py:137
  102.6 16.9 %whole.1 = (bf16[8,2,1,96,3072]{4,3,2,1,0:T(8,128)(2,1)}, f32[2,768,128]{2,1,0:T(8,128)}) custom-call(bf16[2,768,4096]{2,1,0:T(8,128)(2,1)} %bitcast.32, bf16[16,2,512,256]{3,2,1,0:T(8,128)(2,1)} %bitcast.38, bf16[8,2,1,96,3072]{4,3,2,1,0:T(8,128)(2,1)} %rest_9_.1, bf16[8,2,1,96,3072]{4,3,2,1,0:T(8,128)(2,1)} %rest_9_.1, f32[2,768,128]{2,1,0:T(8,128)} %bitcast.30), custom_call_target="tpu_custom_call" | custom-call | flops 6442450944 | bytes 27262976 | tf_op jit(solution)/shard_map/whole/pallas_call | solution.py:296
  119.6 11.5 %collective-permute-done.13.refs_0_.rest_1_ = bf16[4,1024,256]{2,1,0:T(8,128)(2,1)} collective-permute-done((bf16[4,1024,256]{2,1,0:T(8,128)(2,1)S(1)}, bf16[4,1024,256]{2,1,0:T(8,128)(2,1)}, u32[]{:S(2)}, u32[]{:S(2)}) %collective-permute-start.13) | collective-permute-done | bytes 2097184 | tf_op jit(solution)/shard_map/ppermute | solution.py:33
  131.1 3.4 %halves.1 = (bf16[2,1024,256]{2,1,0:T(8,128)(2,1)}, bf16[2,1024,256]{2,1,0:T(8,128)(2,1)}, bf16[2,1024,256]{2,1,0:T(8,128)(2,1)}, bf16[2,1024,256]{2,1,0:T(8,128)(2,1)}) custom-call(bf16[4,1024,256]{2,1,0:T(8,128)(2,1)} %collective-permute-done.13.refs_0_.rest_1_, bf16[4,1024,256]{2,1,0:T(8,128)(2,1)} %collective-permute-done.14.refs_1_.rest_2_, ...), custom_call_target="tpu_custom_call" | custom-call | tf_op jit(solution)/shard_map/halves/pallas_call | solution.py:526
  140.2 17.4 %most.1.rest_11_ = f32[2,768,1024]{2,1,0:T(8,128)S(1)} custom-call(s32[32]{0:T(128)S(1)} %pad_add_fusion.order_ref, bf16[2,768,4096]{2,1,0:T(8,128)(2,1)} %bitcast.33, bf16[4,1024,256]{2,1,0:T(8,128)(2,1)S(1)} %pad_maximum_fusion.1.rest_0_, bf16[4,1024,256]{2,1,0:T(8,128)(2,1)} %collective-permute-done.13.refs_0_.rest_1_, ...), custom_call_target="tpu_custom_call" | custom-call | flops 9663676416 | bytes 35651584 | tf_op jit(solution)/shard_map/most/pallas_call | solution.py:375
  157.7 2.6 %copy-done = f32[2,768,1024]{2,1,0:T(8,128)} copy-done((f32[2,768,1024]{2,1,0:T(8,128)}, f32[2,768,1024]{2,1,0:T(8,128)S(1)}, u32[]{:S(2)}) %copy-start) | copy-done | bytes 6291480
  162.2 13.8 %last.1 = (bf16[8,2,1,96,3072]{4,3,2,1,0:T(8,128)(2,1)}, f32[8,2,128]{2,1,0:T(2,128)S(1)}) custom-call(s32[32]{0:T(128)S(1)} %pad_add_fusion.order_ref, bf16[2,768,4096]{2,1,0:T(8,128)(2,1)} %bitcast.34, bf16[2,768,4096]{2,1,0:T(8,128)(2,1)} %bitcast.35, bf16[2,768,4096]{2,1,0:T(8,128)(2,1)} %bitcast.36, ...), custom_call_target="tpu_custom_call", output_to_operand_aliasing={{0}: (15, {})} | custom-call | flops 3221225472 | bytes 33554432 | tf_op jit(solution)/shard_map/last/pallas_call | solution.py:457
  176.0 10.9 %all_to_all.10.grads_ref = f32[8,2,128]{2,1,0:T(2,128)} all-to-all(f32[8,2,128]{2,1,0:T(2,128)S(1)} %get-tuple-element.65), channel_id=1, replica_groups=mesh['outer'=8,'inner'=16] {'outer'}, dimensions={0} | all-to-all | bytes 16384 | tf_op jit(solution)/shard_map/all_to_all | solution.py:599
  (68 shorter events, 28.2 us)
Async XLA Ops:
  7.2 95.5 %all-gather.3.cloned.1.call-start = ((), (), s32[]{:S(2)}) async-start(), calls=%async_computation.2 | async-start | bytes 8912896 | tf_op jit(solution)/shard_map/all_gather | solution.py:547
  9.2 42.3 %copy-start.8 = (bf16[128,4096]{1,0:T(8,128)(2,1)S(1)}, bf16[128,4096]{1,0:T(8,128)(2,1)}, u32[]{:S(2)}) copy-start(bf16[128,4096]{1,0:T(8,128)(2,1)} %param.6) | copy-start | bytes 3145732
  9.2 27.1 %collective-permute-start.4 = (bf16[128,4096]{1,0:T(8,128)(2,1)}, bf16[128,4096]{1,0:T(8,128)(2,1)S(1)}, u32[]{:S(2)}, u32[]{:S(2)}) collective-permute-start(bf16[128,4096]{1,0:T(8,128)(2,1)} %param.6), channel_id=1, source_target_pairs={{0,32},{16,112},{32,64},{48,16},{64,96},{80,48},{96,0},{112,80},{1... | collective-permute-start | bytes 3145736 | tf_op jit(solution)/shard_map/ppermute | solution.py:38
  12.8 15.3 %collective-permute-start = (bf16[1024,256]{1,0:T(8,128)(2,1)S(1)}, bf16[1024,256]{1,0:T(8,128)(2,1)S(1)}, u32[]{:S(2)}, u32[]{:S(2)}) collective-permute-start(bf16[1024,256]{1,0:T(8,128)(2,1)S(1)} %get-tuple-element.67), channel_id=1, source_target_pairs={{0,1},{1,2},{2,3},{3,0},{4,5},{5,6},{6,7},{7,4},{8,9},{9,10},{10,1... | collective-permute-start | bytes 1572872 | tf_op jit(solution)/shard_map/ppermute | solution.py:33
  14.1 15.6 %collective-permute-start.1 = (bf16[1024,256]{1,0:T(8,128)(2,1)S(1)}, bf16[1024,256]{1,0:T(8,128)(2,1)S(1)}, u32[]{:S(2)}, u32[]{:S(2)}) collective-permute-start(bf16[1024,256]{1,0:T(8,128)(2,1)S(1)} %get-tuple-element.67), channel_id=1, source_target_pairs={{0,3},{1,0},{2,1},{3,2},{4,7},{5,4},{6,5},{7,6},{8,11},{9,8},{10,9... | collective-permute-start | bytes 1572872 | tf_op jit(solution)/shard_map/ppermute | solution.py:33
  15.6 19.3 %collective-permute-start.2 = (bf16[1024,256]{1,0:T(8,128)(2,1)S(1)}, bf16[1024,256]{1,0:T(8,128)(2,1)S(1)}, u32[]{:S(2)}, u32[]{:S(2)}) collective-permute-start(bf16[1024,256]{1,0:T(8,128)(2,1)S(1)} %get-tuple-element.68), channel_id=1, source_target_pairs={{0,4},{1,5},{2,6},{3,7},{4,8},{5,9},{6,10},{7,11},{8,12},{9,13},{1... | collective-permute-start | bytes 1572872 | tf_op jit(solution)/shard_map/ppermute | solution.py:33
  17.3 19.1 %collective-permute-start.3 = (bf16[1024,256]{1,0:T(8,128)(2,1)S(1)}, bf16[1024,256]{1,0:T(8,128)(2,1)S(1)}, u32[]{:S(2)}, u32[]{:S(2)}) collective-permute-start(bf16[1024,256]{1,0:T(8,128)(2,1)S(1)} %get-tuple-element.68), channel_id=1, source_target_pairs={{0,12},{1,13},{2,14},{3,15},{4,0},{5,1},{6,2},{7,3},{8,4},{9,5},{1... | collective-permute-start | bytes 1572872 | tf_op jit(solution)/shard_map/ppermute | solution.py:33
  36.4 13.9 %collective-permute-start.9 = (bf16[128,4096]{1,0:T(8,128)(2,1)S(1)}, bf16[128,4096]{1,0:T(8,128)(2,1)S(1)}, u32[]{:S(2)}, u32[]{:S(2)}) collective-permute-start(bf16[128,4096]{1,0:T(8,128)(2,1)S(1)} %collective-permute-done.4), channel_id=1, source_target_pairs={{0,32},{16,112},{32,64},{48,16},{64,96},{80,48},{96,0},{112,80},{1... | collective-permute-start | bytes 3145736 | tf_op jit(solution)/shard_map/ppermute | solution.py:38
  36.4 8.1 %collective-permute-start.5 = (bf16[512,256]{1,0:T(8,128)(2,1)S(1)}, bf16[512,256]{1,0:T(8,128)(2,1)S(1)}, u32[]{:S(2)}, u32[]{:S(2)}) collective-permute-start(bf16[512,256]{1,0:T(8,128)(2,1)S(1)} %slice.23), channel_id=1, source_target_pairs={{0,1},{1,2},{2,3},{3,0},{4,5},{5,6},{6,7},{7,4},{8,9},{9,10},{10,1... | collective-permute-start | bytes 786440 | tf_op jit(solution)/shard_map/ppermute | solution.py:33
  36.5 8.0 %collective-permute-start.6 = (bf16[512,256]{1,0:T(8,128)(2,1)S(1)}, bf16[512,256]{1,0:T(8,128)(2,1)S(1)}, u32[]{:S(2)}, u32[]{:S(2)}) collective-permute-start(bf16[512,256]{1,0:T(8,128)(2,1)S(1)} %slice.24), channel_id=1, source_target_pairs={{0,3},{1,0},{2,1},{3,2},{4,7},{5,4},{6,5},{7,6},{8,11},{9,8},{10,9... | collective-permute-start | bytes 786440 | tf_op jit(solution)/shard_map/ppermute | solution.py:33
  39.3 8.1 %collective-permute-start.7 = (bf16[512,256]{1,0:T(8,128)(2,1)S(1)}, bf16[512,256]{1,0:T(8,128)(2,1)S(1)}, u32[]{:S(2)}, u32[]{:S(2)}) collective-permute-start(bf16[512,256]{1,0:T(8,128)(2,1)S(1)} %slice.25), channel_id=1, source_target_pairs={{0,4},{1,5},{2,6},{3,7},{4,8},{5,9},{6,10},{7,11},{8,12},{9,13},{1... | collective-permute-start | bytes 786440 | tf_op jit(solution)/shard_map/ppermute | solution.py:33
  39.4 8.0 %collective-permute-start.8 = (bf16[512,256]{1,0:T(8,128)(2,1)S(1)}, bf16[512,256]{1,0:T(8,128)(2,1)S(1)}, u32[]{:S(2)}, u32[]{:S(2)}) collective-permute-start(bf16[512,256]{1,0:T(8,128)(2,1)S(1)} %slice.26), channel_id=1, source_target_pairs={{0,12},{1,13},{2,14},{3,15},{4,0},{5,1},{6,2},{7,3},{8,4},{9,5},{1... | collective-permute-start | bytes 786440 | tf_op jit(solution)/shard_map/ppermute | solution.py:33
  50.3 14.0 %collective-permute-start.10 = (bf16[128,4096]{1,0:T(8,128)(2,1)S(1)}, bf16[128,4096]{1,0:T(8,128)(2,1)S(1)}, u32[]{:S(2)}, u32[]{:S(2)}) collective-permute-start(bf16[128,4096]{1,0:T(8,128)(2,1)S(1)} %collective-permute-done.9), channel_id=1, source_target_pairs={{0,32},{16,112},{32,64},{48,16},{64,96},{80,48},{96,0},{112,80},{1... | collective-permute-start | bytes 3145736 | tf_op jit(solution)/shard_map/ppermute | solution.py:38
  53.5 36.4 %collective-permute-start.11 = (bf16[3,128,4096]{2,1,0:T(8,128)(2,1)}, bf16[3,128,4096]{2,1,0:T(8,128)(2,1)}, u32[]{:S(2)}, u32[]{:S(2)}) collective-permute-start(bf16[3,128,4096]{2,1,0:T(8,128)(2,1)} %pad_maximum_fusion.refs_0_), channel_id=1, source_target_pairs={{0,16},{16,0},{32,48},{48,32},{64,80},{80,64},{96,112},{112,96},{1... | collective-permute-start | bytes 9437192 | tf_op jit(solution)/shard_map/ppermute | solution.py:42
  64.4 11.2 %collective-permute-start.12 = (bf16[1,128,4096]{2,1,0:T(8,128)(2,1)S(1)}, bf16[1,128,4096]{2,1,0:T(8,128)(2,1)S(1)}, u32[]{:S(2)}, u32[]{:S(2)}) collective-permute-start(bf16[1,128,4096]{2,1,0:T(8,128)(2,1)S(1)} %bitcast.43), channel_id=1, source_target_pairs={{0,16},{16,0},{32,48},{48,32},{64,80},{80,64},{96,112},{112,96},{1... | collective-permute-start | bytes 3145736 | tf_op jit(solution)/shard_map/ppermute | solution.py:42
  70.4 60.7 %collective-permute-start.13 = (bf16[4,1024,256]{2,1,0:T(8,128)(2,1)S(1)}, bf16[4,1024,256]{2,1,0:T(8,128)(2,1)}, u32[]{:S(2)}, u32[]{:S(2)}) collective-permute-start(bf16[4,1024,256]{2,1,0:T(8,128)(2,1)S(1)} %pad_maximum_fusion.1.rest_0_), channel_id=1, source_target_pairs={{0,4},{1,5},{2,6},{3,7},{4,8},{5,9},{6,10},{7,11},{8,12},{9,13},{1... | collective-permute-start | bytes 6291464 | tf_op jit(solution)/shard_map/ppermute | solution.py:33
  71.1 60.0 %collective-permute-start.14 = (bf16[4,1024,256]{2,1,0:T(8,128)(2,1)S(1)}, bf16[4,1024,256]{2,1,0:T(8,128)(2,1)}, u32[]{:S(2)}, u32[]{:S(2)}) collective-permute-start(bf16[4,1024,256]{2,1,0:T(8,128)(2,1)S(1)} %pad_maximum_fusion.1.rest_0_), channel_id=1, source_target_pairs={{0,12},{1,13},{2,14},{3,15},{4,0},{5,1},{6,2},{7,3},{8,4},{9,5},{1... | collective-permute-start | bytes 6291464 | tf_op jit(solution)/shard_map/ppermute | solution.py:33
  75.6 55.5 %collective-permute-start.15 = (bf16[4,1024,256]{2,1,0:T(8,128)(2,1)}, bf16[4,1024,256]{2,1,0:T(8,128)(2,1)}, u32[]{:S(2)}, u32[]{:S(2)}) collective-permute-start(bf16[4,1024,256]{2,1,0:T(8,128)(2,1)} %pad_maximum_fusion.2.rest_3_), channel_id=1, source_target_pairs={{0,1},{1,2},{2,3},{3,0},{4,5},{5,6},{6,7},{7,4},{8,9},{9,10},{10,1... | collective-permute-start | bytes 6291464 | tf_op jit(solution)/shard_map/ppermute | solution.py:33
  76.6 54.5 %collective-permute-start.16 = (bf16[4,1024,256]{2,1,0:T(8,128)(2,1)}, bf16[4,1024,256]{2,1,0:T(8,128)(2,1)}, u32[]{:S(2)}, u32[]{:S(2)}) collective-permute-start(bf16[4,1024,256]{2,1,0:T(8,128)(2,1)} %pad_maximum_fusion.2.rest_3_), channel_id=1, source_target_pairs={{0,3},{1,0},{2,1},{3,2},{4,7},{5,4},{6,5},{7,6},{8,11},{9,8},{10,9... | collective-permute-start | bytes 6291464 | tf_op jit(solution)/shard_map/ppermute | solution.py:33
  80.7 9.3 %all-to-all-start = ((f32[8,4,128]{2,1,0:T(4,128)}), f32[8,4,128]{2,1,0:T(4,128)S(1)}, u32[]{:S(2)}, u32[]{:S(2)}) async-start(f32[8,4,128]{2,1,0:T(4,128)} %plan.1), calls=%async_computation | async-start | bytes 32768 | tf_op jit(solution)/shard_map/all_to_all | solution.py:569
  134.5 25.8 %collective-permute-start.17 = (bf16[2,1024,256]{2,1,0:T(8,128)(2,1)}, bf16[2,1024,256]{2,1,0:T(8,128)(2,1)S(1)}, u32[]{:S(2)}, u32[]{:S(2)}) collective-permute-start(bf16[2,1024,256]{2,1,0:T(8,128)(2,1)} %get-tuple-element.54), channel_id=1, source_target_pairs={{0,4},{1,5},{2,6},{3,7},{4,8},{5,9},{6,10},{7,11},{8,12},{9,13},{1... | collective-permute-start | bytes 3145736 | tf_op jit(solution)/shard_map/ppermute | solution.py:33
  135.4 24.9 %collective-permute-start.18 = (bf16[2,1024,256]{2,1,0:T(8,128)(2,1)}, bf16[2,1024,256]{2,1,0:T(8,128)(2,1)}, u32[]{:S(2)}, u32[]{:S(2)}) collective-permute-start(bf16[2,1024,256]{2,1,0:T(8,128)(2,1)} %get-tuple-element.55), channel_id=1, source_target_pairs={{0,12},{1,13},{2,14},{3,15},{4,0},{5,1},{6,2},{7,3},{8,4},{9,5},{1... | collective-permute-start | bytes 3145736 | tf_op jit(solution)/shard_map/ppermute | solution.py:33
  137.2 25.0 %collective-permute-start.19 = (bf16[2,1024,256]{2,1,0:T(8,128)(2,1)}, bf16[2,1024,256]{2,1,0:T(8,128)(2,1)}, u32[]{:S(2)}, u32[]{:S(2)}) collective-permute-start(bf16[2,1024,256]{2,1,0:T(8,128)(2,1)} %get-tuple-element.56), channel_id=1, source_target_pairs={{0,1},{1,2},{2,3},{3,0},{4,5},{5,6},{6,7},{7,4},{8,9},{9,10},{10,1... | collective-permute-start | bytes 3145736 | tf_op jit(solution)/shard_map/ppermute | solution.py:33
  138.4 23.8 %collective-permute-start.20 = (bf16[2,1024,256]{2,1,0:T(8,128)(2,1)}, bf16[2,1024,256]{2,1,0:T(8,128)(2,1)}, u32[]{:S(2)}, u32[]{:S(2)}) collective-permute-start(bf16[2,1024,256]{2,1,0:T(8,128)(2,1)} %get-tuple-element.57), channel_id=1, source_target_pairs={{0,3},{1,0},{2,1},{3,2},{4,7},{5,4},{6,5},{7,6},{8,11},{9,8},{10,9... | collective-permute-start | bytes 3145736 | tf_op jit(solution)/shard_map/ppermute | solution.py:33
  (9 other events, 92.9 us)
Sparse Core Ops, SparseCore 0:
  10.1 87.1 all-gather.2

commit v5 on v4

--- a/solution.py
+++ b/solution.py
@@ -33,8 +33,10 @@
     return lax.ppermute(x, "inner", ring(axis, step))
 
 
-def along_x(x):
-    pairs = [(a * 2 + c, ((a + 1 - 2 * c) % 4) * 2 + c) for a in range(4) for c in range(2)]
+def along_x(x, way=1):
+    pairs = [
+        (a * 2 + c, ((a + way * (1 - 2 * c)) % 4) * 2 + c) for a in range(4) for c in range(2)
+    ]
     return lax.ppermute(x, "outer", pairs)
 
 
@@ -548,14 +550,14 @@
 
     a, b = down_weight[0, split:], down_weight[1, split:]
     one = [along(a, "y", 1), along(a, "y", -1), along(b, "z", 1), along(b, "z", -1)]
-    one, (next_one,) = together(one, [along_x(grad_out)])
+    one, (next_one, mine) = together(one, [along_x(grad_out), grad_out])
     cut = a.shape[0] // 2
     two = [
         along(one[0][:cut], "y", 1), along(one[1][cut:], "y", -1),
         along(one[2][:cut], "z", 1), along(one[3][cut:], "z", -1),
     ]
-    two, (next_two, named, scales) = together(
-        two, [along_x(next_one), routes.T, route_weights.T]
+    two, (next_two, last_one, named, scales) = together(
+        two, [along_x(next_one), along_x(mine, -1), routes.T, route_weights.T]
     )
     block_a = jnp.stack([a, one[0], one[1], jnp.concatenate(two[:2])])
     block_b = jnp.stack([b, one[2], one[3], jnp.concatenate(two[2:])])
@@ -564,7 +566,7 @@
     ]
 
     near = jnp.stack([grad_out, next_one, next_two])
-    last_one = along_x(next_two)[None]
+    last_one = last_one[None]
     near_other, last_other = other_core(near), other_core(last_one)
     plans = lax.all_to_all(
         plan(named, scales, n_outer), "outer", split_axis=0, concat_axis=0, tiled=True

time: 195 us -> 197 us (1.010)
  waiting for transfers between devices: 50 us -> 57.7 us
  starting transfers between devices: 42.1 us -> 36.4 us
    ppermute x16, waiting for transfers between devices: 34.7 us -> 47.5 us  [along(): return lax.ppermute(x, 'inner', ring(axis, step))]
    ppermute x3, waiting for transfers between devices: 11.3 us -> 3.03 us  [along_x(): return lax.ppermute(x, 'outer', pairs)]
    ppermute x2, starting transfers between devices: 8.17 us -> 2.39 us  [other_core(): return lax.ppermute(x, 'outer', [(i, i ^ 1) for i in range(8)])]
  transfers between devices with their start and end apart: 23 -> 23, of which waited for: 11 -> 17; matrix products, arithmetic and copies ran while one was open for 3% -> 3% of each run, Pallas kernels for 25% -> 24%
where the time goes in v5:
time: 197 us
  Pallas kernels  66.4 us (34%)
  waiting for transfers between devices  57.7 us (29%)
  starting transfers between devices  36.4 us (18%)
  between operations  14.3 us (7%)
  blocking collectives  10.5 us (5%)
  local copies, waits for them, and re-layouts  7.27 us (4%)
  other arithmetic  4.13 us (2%)
    ppermute x16, waiting for transfers between devices, along(): return lax.ppermute(x, 'inner', ring(axis, step))  47.5 us
    ppermute x16, starting transfers between devices, along(): return lax.ppermute(x, 'inner', ring(axis, step))  25.5 us
    pallas_call x1, Pallas kernels, most(): pl.pallas_call(most_kernel, grid_spec=pltpu.PrefetchScalarGridSpec(num_sc...  17.5 us
    pallas_call x1, Pallas kernels, whole(): pl.pallas_call(functools.partial(whole_kernel, tiles), grid=(2, tiles), i...  16.9 us
    pallas_call x1, Pallas kernels, last(): pl.pallas_call(functools.partial(last_kernel, first, tiles), grid_spec=pl...  13.8 us
    pallas_call x1, Pallas kernels, fill(): pl.pallas_call(functools.partial(fill_kernel, starts), grid_spec=pltpu.Pr...  12.1 us
    all_to_all x1, blocking collectives, shards(): lax.all_to_all(grads, 'outer', split_axis=0, concat_axis=0, tiled=True)  10.5 us
    ppermute x3, starting transfers between devices, along_x(): return lax.ppermute(x, 'outer', pairs)  4.84 us
  transfers between devices with their start and end apart: 23, of which 17 were waited for; matrix products, arithmetic and copies ran while one was open for 3% of the time, Pallas kernels for 24%

profile of v5, /device:TPU:1, one launch (start us, length us, event | category | flops | bytes accessed | tf_op | source)
XLA Modules:
  0.0 196.7 jit_solution(5646658372513479581)
XLA Ops:
  9.2 3.4 %collective-permute-start.4 = (bf16[128,4096]{1,0:T(8,128)(2,1)}, bf16[128,4096]{1,0:T(8,128)(2,1)S(1)}, u32[]{:S(2)}, u32[]{:S(2)}) collective-permute-start(bf16[128,4096]{1,0:T(8,128)(2,1)} %param.6), channel_id=1, source_target_pairs={{0,32},{16,112},{32,64},{48,16},{64,96},{80,48},{96,0},{112,80},{1... | collective-permute-start | bytes 3145736 | tf_op jit(solution)/shard_map/ppermute | solution.py:40
  17.3 2.1 %collective-permute-start.3 = (bf16[1024,256]{1,0:T(8,128)(2,1)S(1)}, bf16[1024,256]{1,0:T(8,128)(2,1)S(1)}, u32[]{:S(2)}, u32[]{:S(2)}) collective-permute-start(bf16[1024,256]{1,0:T(8,128)(2,1)S(1)} %get-tuple-element.72), channel_id=1, source_target_pairs={{0,12},{1,13},{2,14},{3,15},{4,0},{5,1},{6,2},{7,3},{8,4},{9,5},{1... | collective-permute-start | bytes 1572872 | tf_op jit(solution)/shard_map/ppermute | solution.py:33
  19.4 8.6 %collective-permute-done = bf16[1024,256]{1,0:T(8,128)(2,1)S(1)} collective-permute-done((bf16[1024,256]{1,0:T(8,128)(2,1)S(1)}, bf16[1024,256]{1,0:T(8,128)(2,1)S(1)}, u32[]{:S(2)}, u32[]{:S(2)}) %collective-permute-start) | collective-permute-done | bytes 524320 | tf_op jit(solution)/shard_map/ppermute | solution.py:33
  29.7 5.3 %collective-permute-done.2 = bf16[1024,256]{1,0:T(8,128)(2,1)S(1)} collective-permute-done((bf16[1024,256]{1,0:T(8,128)(2,1)S(1)}, bf16[1024,256]{1,0:T(8,128)(2,1)S(1)}, u32[]{:S(2)}, u32[]{:S(2)}) %collective-permute-start.2) | collective-permute-done | bytes 524320 | tf_op jit(solution)/shard_map/ppermute | solution.py:33
  37.9 2.7 %collective-permute-start.6 = (bf16[512,256]{1,0:T(8,128)(2,1)S(1)}, bf16[512,256]{1,0:T(8,128)(2,1)S(1)}, u32[]{:S(2)}, u32[]{:S(2)}) collective-permute-start(bf16[512,256]{1,0:T(8,128)(2,1)S(1)} %slice.24), channel_id=1, source_target_pairs={{0,3},{1,0},{2,1},{3,2},{4,7},{5,4},{6,5},{7,6},{8,11},{9,8},{10,9... | collective-permute-start | bytes 786440 | tf_op jit(solution)/shard_map/ppermute | solution.py:33
  40.8 3.8 %collective-permute-done.5 = bf16[512,256]{1,0:T(8,128)(2,1)S(1)} collective-permute-done((bf16[512,256]{1,0:T(8,128)(2,1)S(1)}, bf16[512,256]{1,0:T(8,128)(2,1)S(1)}, u32[]{:S(2)}, u32[]{:S(2)}) %collective-permute-start.5) | collective-permute-done | bytes 262176 | tf_op jit(solution)/shard_map/ppermute | solution.py:33
  44.6 3.5 %collective-permute-start.8 = (bf16[512,256]{1,0:T(8,128)(2,1)S(1)}, bf16[512,256]{1,0:T(8,128)(2,1)S(1)}, u32[]{:S(2)}, u32[]{:S(2)}) collective-permute-start(bf16[512,256]{1,0:T(8,128)(2,1)S(1)} %slice.26), channel_id=1, source_target_pairs={{0,12},{1,13},{2,14},{3,15},{4,0},{5,1},{6,2},{7,3},{8,4},{9,5},{1... | collective-permute-start | bytes 786440 | tf_op jit(solution)/shard_map/ppermute | solution.py:33
  48.3 9.5 %collective-permute-done.8 = bf16[512,256]{1,0:T(8,128)(2,1)S(1)} collective-permute-done((bf16[512,256]{1,0:T(8,128)(2,1)S(1)}, bf16[512,256]{1,0:T(8,128)(2,1)S(1)}, u32[]{:S(2)}, u32[]{:S(2)}) %collective-permute-start.8) | collective-permute-done | bytes 262176 | tf_op jit(solution)/shard_map/ppermute | solution.py:33
  62.8 2.4 %collective-permute-start.11 = (bf16[3,128,4096]{2,1,0:T(8,128)(2,1)}, bf16[3,128,4096]{2,1,0:T(8,128)(2,1)}, u32[]{:S(2)}, u32[]{:S(2)}) collective-permute-start(bf16[3,128,4096]{2,1,0:T(8,128)(2,1)} %pad_maximum_fusion.refs_0_), channel_id=1, source_target_pairs={{0,16},{16,0},{32,48},{48,32},{64,80},{80,64},{96,112},{112,96},{1... | collective-permute-start | bytes 9437192 | tf_op jit(solution)/shard_map/ppermute | solution.py:44
  65.6 2.7 %collective-permute-start.16 = (bf16[4,1024,256]{2,1,0:T(8,128)(2,1)S(1)}, bf16[4,1024,256]{2,1,0:T(8,128)(2,1)}, u32[]{:S(2)}, u32[]{:S(2)}) collective-permute-start(bf16[4,1024,256]{2,1,0:T(8,128)(2,1)S(1)} %pad_maximum_fusion.2.rest_3_), channel_id=1, source_target_pairs={{0,3},{1,0},{2,1},{3,2},{4,7},{5,4},{6,5},{7,6},{8,11},{9,8},{10,9... | collective-permute-start | bytes 6291464 | tf_op jit(solution)/shard_map/ppermute | solution.py:33
  72.8 3.5 %collective-permute-start.14 = (bf16[4,1024,256]{2,1,0:T(8,128)(2,1)}, bf16[4,1024,256]{2,1,0:T(8,128)(2,1)}, u32[]{:S(2)}, u32[]{:S(2)}) collective-permute-start(bf16[4,1024,256]{2,1,0:T(8,128)(2,1)} %pad_maximum_fusion.1.rest_0_), channel_id=1, source_target_pairs={{0,12},{1,13},{2,14},{3,15},{4,0},{5,1},{6,2},{7,3},{8,4},{9,5},{1... | collective-permute-start | bytes 6291464 | tf_op jit(solution)/shard_map/ppermute | solution.py:33
  77.8 3.6 %all-to-all-start = ((f32[8,4,128]{2,1,0:T(4,128)}), f32[8,4,128]{2,1,0:T(4,128)S(1)}, u32[]{:S(2)}, u32[]{:S(2)}) async-start(f32[8,4,128]{2,1,0:T(4,128)} %plan.1), calls=%async_computation | async-start | bytes 32768 | tf_op jit(solution)/shard_map/all_to_all | solution.py:571
  82.2 3.9 %all-to-all-done.refs_4_.rest_13_ = f32[8,4,128]{2,1,0:T(4,128)S(1)} async-done(((f32[8,4,128]{2,1,0:T(4,128)}), f32[8,4,128]{2,1,0:T(4,128)S(1)}, u32[]{:S(2)}, u32[]{:S(2)}) %all-to-all-start) | async-done | bytes 16416 | tf_op jit(solution)/shard_map/all_to_all | solution.py:571
  86.7 12.1 %fill.1 = (bf16[2,8,96,4096]{3,2,1,0:T(8,128)(2,1)}, f32[2,8,96,128]{3,2,1,0:T(8,128)}) custom-call(s32[8]{0:T(128)} %stack.71.source_ref, bf16[3,128,4096]{2,1,0:T(8,128)(2,1)} %pad_maximum_fusion.refs_0_, bf16[1,128,4096]{2,1,0:T(8,128)(2,1)} %bitcast.44, bf16[3,128,4096]{2,1,0:T(8,128)(2,1)} %collective-permute-done.11.refs_2_, ...), custom_call_target="tpu_custom_call" | custom-call | flops 1610612736 | bytes 20971520 | tf_op jit(solution)/shard_map/fill/pallas_call | solution.py:139
  100.1 16.9 %whole.1 = (bf16[8,2,1,96,3072]{4,3,2,1,0:T(8,128)(2,1)}, f32[2,768,128]{2,1,0:T(8,128)}) custom-call(bf16[2,768,4096]{2,1,0:T(8,128)(2,1)} %bitcast.32, bf16[16,2,512,256]{3,2,1,0:T(8,128)(2,1)} %bitcast.38, bf16[8,2,1,96,3072]{4,3,2,1,0:T(8,128)(2,1)} %rest_9_.1, bf16[8,2,1,96,3072]{4,3,2,1,0:T(8,128)(2,1)} %rest_9_.1, f32[2,768,128]{2,1,0:T(8,128)} %bitcast.30), custom_call_target="tpu_custom_call" | custom-call | flops 6442450944 | bytes 27262976 | tf_op jit(solution)/shard_map/whole/pallas_call | solution.py:298
  117.1 12.6 %collective-permute-done.15.refs_2_.rest_4_ = bf16[4,1024,256]{2,1,0:T(8,128)(2,1)} collective-permute-done((bf16[4,1024,256]{2,1,0:T(8,128)(2,1)S(1)}, bf16[4,1024,256]{2,1,0:T(8,128)(2,1)}, u32[]{:S(2)}, u32[]{:S(2)}) %collective-permute-start.15) | collective-permute-done | bytes 2097184 | tf_op jit(solution)/shard_map/ppermute | solution.py:33
  132.0 3.4 %halves.1 = (bf16[2,1024,256]{2,1,0:T(8,128)(2,1)}, bf16[2,1024,256]{2,1,0:T(8,128)(2,1)}, bf16[2,1024,256]{2,1,0:T(8,128)(2,1)}, bf16[2,1024,256]{2,1,0:T(8,128)(2,1)}) custom-call(bf16[4,1024,256]{2,1,0:T(8,128)(2,1)} %collective-permute-done.13.refs_0_.rest_1_, bf16[4,1024,256]{2,1,0:T(8,128)(2,1)} %collective-permute-done.14.refs_1_.rest_2_, ...), custom_call_target="tpu_custom_call" | custom-call | tf_op jit(solution)/shard_map/halves/pallas_call | solution.py:528
  135.8 3.1 %collective-permute-start.18 = (bf16[2,1024,256]{2,1,0:T(8,128)(2,1)}, bf16[2,1024,256]{2,1,0:T(8,128)(2,1)}, u32[]{:S(2)}, u32[]{:S(2)}) collective-permute-start(bf16[2,1024,256]{2,1,0:T(8,128)(2,1)} %get-tuple-element.59), channel_id=1, source_target_pairs={{0,12},{1,13},{2,14},{3,15},{4,0},{5,1},{6,2},{7,3},{8,4},{9,5},{1... | collective-permute-start | bytes 3145736 | tf_op jit(solution)/shard_map/ppermute | solution.py:33
  138.9 2.7 %collective-permute-start.20 = (bf16[2,1024,256]{2,1,0:T(8,128)(2,1)}, bf16[2,1024,256]{2,1,0:T(8,128)(2,1)}, u32[]{:S(2)}, u32[]{:S(2)}) collective-permute-start(bf16[2,1024,256]{2,1,0:T(8,128)(2,1)} %get-tuple-element.61), channel_id=1, source_target_pairs={{0,3},{1,0},{2,1},{3,2},{4,7},{5,4},{6,5},{7,6},{8,11},{9,8},{10,9... | collective-permute-start | bytes 3145736 | tf_op jit(solution)/shard_map/ppermute | solution.py:33
  141.9 17.5 %most.1.rest_11_ = f32[2,768,1024]{2,1,0:T(8,128)S(1)} custom-call(s32[32]{0:T(128)S(1)} %pad_add_fusion.order_ref, bf16[2,768,4096]{2,1,0:T(8,128)(2,1)} %bitcast.33, bf16[4,1024,256]{2,1,0:T(8,128)(2,1)} %pad_maximum_fusion.1.rest_0_, bf16[4,1024,256]{2,1,0:T(8,128)(2,1)} %collective-permute-done.13.refs_0_.rest_1_, ...), custom_call_target="tpu_custom_call" | custom-call | flops 9663676416 | bytes 35651584 | tf_op jit(solution)/shard_map/most/pallas_call | solution.py:377
  159.4 2.6 %copy-done = f32[2,768,1024]{2,1,0:T(8,128)} copy-done((f32[2,768,1024]{2,1,0:T(8,128)}, f32[2,768,1024]{2,1,0:T(8,128)S(1)}, u32[]{:S(2)}) %copy-start) | copy-done | bytes 6291480
  162.1 2.1 %collective-permute-done.19.rest_6_ = bf16[2,1024,256]{2,1,0:T(8,128)(2,1)} collective-permute-done((bf16[2,1024,256]{2,1,0:T(8,128)(2,1)}, bf16[2,1024,256]{2,1,0:T(8,128)(2,1)}, u32[]{:S(2)}, u32[]{:S(2)}) %collective-permute-start.19) | collective-permute-done | bytes 1048608 | tf_op jit(solution)/shard_map/ppermute | solution.py:33
  164.3 13.8 %last.1 = (bf16[8,2,1,96,3072]{4,3,2,1,0:T(8,128)(2,1)}, f32[8,2,128]{2,1,0:T(2,128)S(1)}) custom-call(s32[32]{0:T(128)S(1)} %pad_add_fusion.order_ref, bf16[2,768,4096]{2,1,0:T(8,128)(2,1)} %bitcast.34, bf16[2,768,4096]{2,1,0:T(8,128)(2,1)} %bitcast.35, bf16[2,768,4096]{2,1,0:T(8,128)(2,1)} %bitcast.36, ...), custom_call_target="tpu_custom_call", output_to_operand_aliasing={{0}: (15, {})} | custom-call | flops 3221225472 | bytes 33554432 | tf_op jit(solution)/shard_map/last/pallas_call | solution.py:459
  178.0 10.5 %all_to_all.10.grads_ref = f32[8,2,128]{2,1,0:T(2,128)} all-to-all(f32[8,2,128]{2,1,0:T(2,128)S(1)} %get-tuple-element.69), channel_id=1, replica_groups=mesh['outer'=8,'inner'=16] {'outer'}, dimensions={0} | all-to-all | bytes 16384 | tf_op jit(solution)/shard_map/all_to_all | solution.py:601
  (68 shorter events, 30.1 us)
Async XLA Ops:
  7.2 93.0 %all-gather.3.cloned.1.call-start = ((), (), s32[]{:S(2)}) async-start(), calls=%async_computation.2 | async-start | bytes 8912896 | tf_op jit(solution)/shard_map/all_gather | solution.py:549
  9.2 27.1 %copy-start.8 = (bf16[128,4096]{1,0:T(8,128)(2,1)S(1)}, bf16[128,4096]{1,0:T(8,128)(2,1)}, u32[]{:S(2)}) copy-start(bf16[128,4096]{1,0:T(8,128)(2,1)} %param.6) | copy-start | bytes 3145732
  9.2 27.1 %collective-permute-start.4 = (bf16[128,4096]{1,0:T(8,128)(2,1)}, bf16[128,4096]{1,0:T(8,128)(2,1)S(1)}, u32[]{:S(2)}, u32[]{:S(2)}) collective-permute-start(bf16[128,4096]{1,0:T(8,128)(2,1)} %param.6), channel_id=1, source_target_pairs={{0,32},{16,112},{32,64},{48,16},{64,96},{80,48},{96,0},{112,80},{1... | collective-permute-start | bytes 3145736 | tf_op jit(solution)/shard_map/ppermute | solution.py:40
  12.8 15.3 %collective-permute-start = (bf16[1024,256]{1,0:T(8,128)(2,1)S(1)}, bf16[1024,256]{1,0:T(8,128)(2,1)S(1)}, u32[]{:S(2)}, u32[]{:S(2)}) collective-permute-start(bf16[1024,256]{1,0:T(8,128)(2,1)S(1)} %get-tuple-element.71), channel_id=1, source_target_pairs={{0,1},{1,2},{2,3},{3,0},{4,5},{5,6},{6,7},{7,4},{8,9},{9,10},{10,1... | collective-permute-start | bytes 1572872 | tf_op jit(solution)/shard_map/ppermute | solution.py:33
  14.1 15.6 %collective-permute-start.1 = (bf16[1024,256]{1,0:T(8,128)(2,1)S(1)}, bf16[1024,256]{1,0:T(8,128)(2,1)S(1)}, u32[]{:S(2)}, u32[]{:S(2)}) collective-permute-start(bf16[1024,256]{1,0:T(8,128)(2,1)S(1)} %get-tuple-element.71), channel_id=1, source_target_pairs={{0,3},{1,0},{2,1},{3,2},{4,7},{5,4},{6,5},{7,6},{8,11},{9,8},{10,9... | collective-permute-start | bytes 1572872 | tf_op jit(solution)/shard_map/ppermute | solution.py:33
  15.6 19.3 %collective-permute-start.2 = (bf16[1024,256]{1,0:T(8,128)(2,1)S(1)}, bf16[1024,256]{1,0:T(8,128)(2,1)S(1)}, u32[]{:S(2)}, u32[]{:S(2)}) collective-permute-start(bf16[1024,256]{1,0:T(8,128)(2,1)S(1)} %get-tuple-element.72), channel_id=1, source_target_pairs={{0,4},{1,5},{2,6},{3,7},{4,8},{5,9},{6,10},{7,11},{8,12},{9,13},{1... | collective-permute-start | bytes 1572872 | tf_op jit(solution)/shard_map/ppermute | solution.py:33
  17.3 19.0 %collective-permute-start.3 = (bf16[1024,256]{1,0:T(8,128)(2,1)S(1)}, bf16[1024,256]{1,0:T(8,128)(2,1)S(1)}, u32[]{:S(2)}, u32[]{:S(2)}) collective-permute-start(bf16[1024,256]{1,0:T(8,128)(2,1)S(1)} %get-tuple-element.72), channel_id=1, source_target_pairs={{0,12},{1,13},{2,14},{3,15},{4,0},{5,1},{6,2},{7,3},{8,4},{9,5},{1... | collective-permute-start | bytes 1572872 | tf_op jit(solution)/shard_map/ppermute | solution.py:33
  36.3 23.0 %collective-permute-start.9 = (bf16[128,4096]{1,0:T(8,128)(2,1)S(1)}, bf16[128,4096]{1,0:T(8,128)(2,1)S(1)}, u32[]{:S(2)}, u32[]{:S(2)}) collective-permute-start(bf16[128,4096]{1,0:T(8,128)(2,1)S(1)} %collective-permute-done.4), channel_id=1, source_target_pairs={{0,32},{16,112},{32,64},{48,16},{64,96},{80,48},{96,0},{112,80},{1... | collective-permute-start | bytes 3145736 | tf_op jit(solution)/shard_map/ppermute | solution.py:40
  36.4 24.5 %collective-permute-start.10 = (bf16[128,4096]{1,0:T(8,128)(2,1)S(1)}, bf16[128,4096]{1,0:T(8,128)(2,1)S(1)}, u32[]{:S(2)}, u32[]{:S(2)}) collective-permute-start(bf16[128,4096]{1,0:T(8,128)(2,1)S(1)} %copy-done.8), channel_id=1, source_target_pairs={{0,96},{16,48},{32,0},{48,80},{64,32},{80,112},{96,64},{112,16},{1... | collective-permute-start | bytes 3145736 | tf_op jit(solution)/shard_map/ppermute | solution.py:40
  37.8 6.8 %collective-permute-start.5 = (bf16[512,256]{1,0:T(8,128)(2,1)S(1)}, bf16[512,256]{1,0:T(8,128)(2,1)S(1)}, u32[]{:S(2)}, u32[]{:S(2)}) collective-permute-start(bf16[512,256]{1,0:T(8,128)(2,1)S(1)} %slice.23), channel_id=1, source_target_pairs={{0,1},{1,2},{2,3},{3,0},{4,5},{5,6},{6,7},{7,4},{8,9},{9,10},{10,1... | collective-permute-start | bytes 786440 | tf_op jit(solution)/shard_map/ppermute | solution.py:33
  37.9 10.2 %collective-permute-start.6 = (bf16[512,256]{1,0:T(8,128)(2,1)S(1)}, bf16[512,256]{1,0:T(8,128)(2,1)S(1)}, u32[]{:S(2)}, u32[]{:S(2)}) collective-permute-start(bf16[512,256]{1,0:T(8,128)(2,1)S(1)} %slice.24), channel_id=1, source_target_pairs={{0,3},{1,0},{2,1},{3,2},{4,7},{5,4},{6,5},{7,6},{8,11},{9,8},{10,9... | collective-permute-start | bytes 786440 | tf_op jit(solution)/shard_map/ppermute | solution.py:33
  40.7 7.6 %collective-permute-start.7 = (bf16[512,256]{1,0:T(8,128)(2,1)S(1)}, bf16[512,256]{1,0:T(8,128)(2,1)S(1)}, u32[]{:S(2)}, u32[]{:S(2)}) collective-permute-start(bf16[512,256]{1,0:T(8,128)(2,1)S(1)} %slice.25), channel_id=1, source_target_pairs={{0,4},{1,5},{2,6},{3,7},{4,8},{5,9},{6,10},{7,11},{8,12},{9,13},{1... | collective-permute-start | bytes 786440 | tf_op jit(solution)/shard_map/ppermute | solution.py:33
  44.6 13.2 %collective-permute-start.8 = (bf16[512,256]{1,0:T(8,128)(2,1)S(1)}, bf16[512,256]{1,0:T(8,128)(2,1)S(1)}, u32[]{:S(2)}, u32[]{:S(2)}) collective-permute-start(bf16[512,256]{1,0:T(8,128)(2,1)S(1)} %slice.26), channel_id=1, source_target_pairs={{0,12},{1,13},{2,14},{3,15},{4,0},{5,1},{6,2},{7,3},{8,4},{9,5},{1... | collective-permute-start | bytes 786440 | tf_op jit(solution)/shard_map/ppermute | solution.py:33
  62.8 23.3 %collective-permute-start.11 = (bf16[3,128,4096]{2,1,0:T(8,128)(2,1)}, bf16[3,128,4096]{2,1,0:T(8,128)(2,1)}, u32[]{:S(2)}, u32[]{:S(2)}) collective-permute-start(bf16[3,128,4096]{2,1,0:T(8,128)(2,1)} %pad_maximum_fusion.refs_0_), channel_id=1, source_target_pairs={{0,16},{16,0},{32,48},{48,32},{64,80},{80,64},{96,112},{112,96},{1... | collective-permute-start | bytes 9437192 | tf_op jit(solution)/shard_map/ppermute | solution.py:44
  65.2 6.6 %collective-permute-start.12 = (bf16[1,128,4096]{2,1,0:T(8,128)(2,1)S(1)}, bf16[1,128,4096]{2,1,0:T(8,128)(2,1)S(1)}, u32[]{:S(2)}, u32[]{:S(2)}) collective-permute-start(bf16[1,128,4096]{2,1,0:T(8,128)(2,1)S(1)} %bitcast.43), channel_id=1, source_target_pairs={{0,16},{16,0},{32,48},{48,32},{64,80},{80,64},{96,112},{112,96},{1... | collective-permute-start | bytes 3145736 | tf_op jit(solution)/shard_map/ppermute | solution.py:44
  65.5 64.2 %collective-permute-start.15 = (bf16[4,1024,256]{2,1,0:T(8,128)(2,1)S(1)}, bf16[4,1024,256]{2,1,0:T(8,128)(2,1)}, u32[]{:S(2)}, u32[]{:S(2)}) collective-permute-start(bf16[4,1024,256]{2,1,0:T(8,128)(2,1)S(1)} %pad_maximum_fusion.2.rest_3_), channel_id=1, source_target_pairs={{0,1},{1,2},{2,3},{3,0},{4,5},{5,6},{6,7},{7,4},{8,9},{9,10},{10,1... | collective-permute-start | bytes 6291464 | tf_op jit(solution)/shard_map/ppermute | solution.py:33
  65.6 64.1 %collective-permute-start.16 = (bf16[4,1024,256]{2,1,0:T(8,128)(2,1)S(1)}, bf16[4,1024,256]{2,1,0:T(8,128)(2,1)}, u32[]{:S(2)}, u32[]{:S(2)}) collective-permute-start(bf16[4,1024,256]{2,1,0:T(8,128)(2,1)S(1)} %pad_maximum_fusion.2.rest_3_), channel_id=1, source_target_pairs={{0,3},{1,0},{2,1},{3,2},{4,7},{5,4},{6,5},{7,6},{8,11},{9,8},{10,9... | collective-permute-start | bytes 6291464 | tf_op jit(solution)/shard_map/ppermute | solution.py:33
  70.0 60.8 %collective-permute-start.13 = (bf16[4,1024,256]{2,1,0:T(8,128)(2,1)}, bf16[4,1024,256]{2,1,0:T(8,128)(2,1)}, u32[]{:S(2)}, u32[]{:S(2)}) collective-permute-start(bf16[4,1024,256]{2,1,0:T(8,128)(2,1)} %pad_maximum_fusion.1.rest_0_), channel_id=1, source_target_pairs={{0,4},{1,5},{2,6},{3,7},{4,8},{5,9},{6,10},{7,11},{8,12},{9,13},{1... | collective-permute-start | bytes 6291464 | tf_op jit(solution)/shard_map/ppermute | solution.py:33
  72.8 59.2 %collective-permute-start.14 = (bf16[4,1024,256]{2,1,0:T(8,128)(2,1)}, bf16[4,1024,256]{2,1,0:T(8,128)(2,1)}, u32[]{:S(2)}, u32[]{:S(2)}) collective-permute-start(bf16[4,1024,256]{2,1,0:T(8,128)(2,1)} %pad_maximum_fusion.1.rest_0_), channel_id=1, source_target_pairs={{0,12},{1,13},{2,14},{3,15},{4,0},{5,1},{6,2},{7,3},{8,4},{9,5},{1... | collective-permute-start | bytes 6291464 | tf_op jit(solution)/shard_map/ppermute | solution.py:33
  77.8 8.3 %all-to-all-start = ((f32[8,4,128]{2,1,0:T(4,128)}), f32[8,4,128]{2,1,0:T(4,128)S(1)}, u32[]{:S(2)}, u32[]{:S(2)}) async-start(f32[8,4,128]{2,1,0:T(4,128)} %plan.1), calls=%async_computation | async-start | bytes 32768 | tf_op jit(solution)/shard_map/all_to_all | solution.py:571
  135.4 26.8 %collective-permute-start.17 = (bf16[2,1024,256]{2,1,0:T(8,128)(2,1)}, bf16[2,1024,256]{2,1,0:T(8,128)(2,1)S(1)}, u32[]{:S(2)}, u32[]{:S(2)}) collective-permute-start(bf16[2,1024,256]{2,1,0:T(8,128)(2,1)} %get-tuple-element.58), channel_id=1, source_target_pairs={{0,4},{1,5},{2,6},{3,7},{4,8},{5,9},{6,10},{7,11},{8,12},{9,13},{1... | collective-permute-start | bytes 3145736 | tf_op jit(solution)/shard_map/ppermute | solution.py:33
  135.8 26.3 %collective-permute-start.18 = (bf16[2,1024,256]{2,1,0:T(8,128)(2,1)}, bf16[2,1024,256]{2,1,0:T(8,128)(2,1)}, u32[]{:S(2)}, u32[]{:S(2)}) collective-permute-start(bf16[2,1024,256]{2,1,0:T(8,128)(2,1)} %get-tuple-element.59), channel_id=1, source_target_pairs={{0,12},{1,13},{2,14},{3,15},{4,0},{5,1},{6,2},{7,3},{8,4},{9,5},{1... | collective-permute-start | bytes 3145736 | tf_op jit(solution)/shard_map/ppermute | solution.py:33
  138.9 25.3 %collective-permute-start.19 = (bf16[2,1024,256]{2,1,0:T(8,128)(2,1)}, bf16[2,1024,256]{2,1,0:T(8,128)(2,1)}, u32[]{:S(2)}, u32[]{:S(2)}) collective-permute-start(bf16[2,1024,256]{2,1,0:T(8,128)(2,1)} %get-tuple-element.60), channel_id=1, source_target_pairs={{0,1},{1,2},{2,3},{3,0},{4,5},{5,6},{6,7},{7,4},{8,9},{9,10},{10,1... | collective-permute-start | bytes 3145736 | tf_op jit(solution)/shard_map/ppermute | solution.py:33
  138.9 25.3 %collective-permute-start.20 = (bf16[2,1024,256]{2,1,0:T(8,128)(2,1)}, bf16[2,1024,256]{2,1,0:T(8,128)(2,1)}, u32[]{:S(2)}, u32[]{:S(2)}) collective-permute-start(bf16[2,1024,256]{2,1,0:T(8,128)(2,1)} %get-tuple-element.61), channel_id=1, source_target_pairs={{0,3},{1,0},{2,1},{3,2},{4,7},{5,4},{6,5},{7,6},{8,11},{9,8},{10,9... | collective-permute-start | bytes 3145736 | tf_op jit(solution)/shard_map/ppermute | solution.py:33
  (9 other events, 94.1 us)
Sparse Core Ops, SparseCore 0:
  10.1 89.9 all-gather.2
